TPU v7x, 32 devices: a whole 2x2x4 slice. The times are simulated.
32 devices in a mesh: gx: 4 (over z), gy: 4 (over y, core), gz: 2 (over x).
Axes of the slice: x: 2, y: 2, z: 4, core: 2. Of those that a mesh axis runs over, the one named last changes fastest.
Arguments:
- incident: bfloat16 [4, 4, 2, 2, 1280, 128], P('gx', 'gy', 'gz'), may hold values from -6 to 6
- response: bfloat16 [4, 4, 2, 2, 1280, 1280], P('gx', 'gy', 'gz'), may hold values from -0.125 to 0.125
- radiation: bfloat16 [4, 4, 2, 2, 512, 1280], P('gx', 'gy', 'gz'), may hold values from -0.01953125 to 0.01953125
- face_index: int32 [4, 4, 2, 6, 192], P('gx', 'gy', 'gz'), may hold values from 0 to 1279, as said below
- linked: int32 [4, 4, 2, 6], P('gx', 'gy', 'gz'), may hold values 0 or 1
Outputs:
- far_field: float32 [2, 128, 512], P(None, ('gx', 'gy'), 'gz')
Inputs may be any that keep to these rules, and one draw needn't show every extreme that they name: `face_index`: the 1152 entries of one subdomain are distinct.
All inputs are finite; a program needn't handle non-finite values. No bound on the sum of `linked` on one device may be relied on, other than what follows from the above.
Results may differ from a plain program's by a relative error of at most 0.004.
Values may be sent and summed in bfloat16 or wider, within the bound.
No kernel may reach another device: no remote copies, remote signals or barrier semaphores. Data moves between devices by JAX's collectives and lax.ppermute only.
A program may use at most 64 MiB of HBM per device.

v0:
```python
import jax
import jax.numpy as jnp
from jax import lax
from jax.sharding import PartitionSpec as P

M = 1280
FACE = 192
ITERS = 2


def with_halo(cells, sides, width):
    for axis, dim in sides:
        count = lax.axis_size(axis)
        ends = count - 1
        head = lax.slice_in_dim(cells, 0, width, axis=dim)
        tail = lax.slice_in_dim(cells, cells.shape[dim] - width, cells.shape[dim], axis=dim)
        cells = jnp.concatenate(
            [
                lax.ppermute(tail, axis, [(i, (i + 1) % count) for i in range(ends)]),
                cells,
                lax.ppermute(head, axis, [((i + 1) % count, i) for i in range(ends)]),
            ],
            axis=dim,
        )
    return cells


def complex_dot(left_side, right_side):
    real_part = jnp.dot(left_side[0], right_side[0], preferred_element_type=jnp.float32) - jnp.dot(
        left_side[1], right_side[1], preferred_element_type=jnp.float32
    )
    imag_part = jnp.dot(left_side[0], right_side[1], preferred_element_type=jnp.float32) + jnp.dot(
        left_side[1], right_side[0], preferred_element_type=jnp.float32
    )
    return jnp.stack([real_part, imag_part])


def pick_rows(selector, values):
    picked = [
        jnp.dot(selector, values[part_pos], preferred_element_type=jnp.float32)
        for part_pos in range(2)
    ]
    return jnp.stack(picked).astype(jnp.bfloat16)


def put_rows(selector, values):
    placed = [
        lax.dot_general(
            selector, values[part_pos], (((0,), (0,)), ((), ())), preferred_element_type=jnp.float32
        )
        for part_pos in range(2)
    ]
    return jnp.stack(placed).astype(jnp.bfloat16)


def swap_faces(face_block, axis_pos):
    if axis_pos == 0:
        return with_halo(face_block, (("gx", 1),), 1)
    if axis_pos == 1:
        return with_halo(face_block, (("gy", 1),), 1)
    return with_halo(face_block, (("gz", 1),), 1)


def shards(incident, response, radiation, face_index, linked):
    source = incident[0, 0, 0]
    response_mat = response[0, 0, 0]
    radiation_mat = radiation[0, 0, 0]
    slots = face_index[0, 0, 0].reshape(-1)
    linked_faces = linked[0, 0, 0]
    columns = source.shape[-1]
    positions = lax.broadcasted_iota(jnp.int32, (slots.shape[0], M), 1)
    selector = (slots[:, None] == positions).astype(jnp.bfloat16)
    traces = jnp.zeros((2, M, columns), jnp.bfloat16)
    for sweep in range(ITERS):
        summed = (traces.astype(jnp.float32) + source.astype(jnp.float32)).astype(jnp.bfloat16)
        outgoing = complex_dot(response_mat, summed).astype(jnp.bfloat16)
        pieces = []
        all_faces = pick_rows(selector, outgoing).reshape(2, 6, FACE, columns)
        for axis_pos in range(3):
            arrived = swap_faces(all_faces[:, 2 * axis_pos : 2 * axis_pos + 2], axis_pos)
            pieces.append(arrived[:, 0])
            pieces.append(arrived[:, 3])
        incoming = jnp.stack(pieces, 1) * linked_faces[None, :, None, None].astype(jnp.bfloat16)
        traces = put_rows(selector, incoming.reshape(2, 6 * FACE, columns))
    currents = (traces.astype(jnp.float32) + source.astype(jnp.float32)).astype(jnp.bfloat16)
    contract = (((0,), (1,)), ((), ()))
    real_part = lax.dot_general(
        currents[0], radiation_mat[0], contract, preferred_element_type=jnp.float32
    ) - lax.dot_general(currents[1], radiation_mat[1], contract, preferred_element_type=jnp.float32)
    imag_part = lax.dot_general(
        currents[1], radiation_mat[0], contract, preferred_element_type=jnp.float32
    ) + lax.dot_general(currents[0], radiation_mat[1], contract, preferred_element_type=jnp.float32)
    radiated = jnp.stack([real_part, imag_part])
    partial_field = lax.psum_scatter(radiated, "gz", scatter_dimension=2, tiled=True)
    return lax.psum_scatter(partial_field, ("gx", "gy"), scatter_dimension=1, tiled=True)


def solution(mesh):
    return jax.shard_map(
        shards,
        mesh=mesh,
        in_specs=(
            P("gx", "gy", "gz", None, None, None),
            P("gx", "gy", "gz", None, None, None),
            P("gx", "gy", "gz", None, None, None),
            P("gx", "gy", "gz", None, None),
            P("gx", "gy", "gz", None),
        ),
        out_specs=P(None, ("gx", "gy"), "gz"),
        check_vma=False,
    )
```

profile of v0, /device:TPU:0, one launch (start us, length us, event | category | flops | bytes accessed | tf_op | source)
XLA Modules:
  0.0 167.7 jit_solution(11146396528298380669)
XLA Ops:
  6.5 3.1 %fusion.17 = f32[1280,128]{1,0:T(8,128)S(1)} fusion(bf16[1,1,1,2,1280,1280]{5,4,3,2,1,0:T(8,128)(2,1)} %param.6, bf16[1,1,1,2,1280,128]{5,4,3,2,1,0:T(8,128)(2,1)} %param.5), kind=kOutput, calls=%fused_computation.15 | convolution fusion | flops 419430400 | bytes 4259840 | tf_op jit(solution)/shard_map/dot_general | solution.py:32
  11.7 5.1 %fusion.117 = bf16[1,6,192,128]{3,2,1,0:T(8,128)(2,1)S(1)} fusion(s32[6,192]{1,0:T(8,128)S(1)} %bitcast.177, f32[1280,128]{1,0:T(8,128)S(1)} %fusion.17, bf16[1,1,1,2,1280,1280]{5,4,3,2,1,0:T(8,128)(2,1)} %param.6, bf16[1,1,1,2,1280,128]{5,4,3,2,1,0:T(8,128)(2,1)S(1)} %copy-done), kind=kOutput, calls=%fused_computation.81 | convolution fusion | flops 798867456 | bytes 4562944 | tf_op jit(solution)/shard_map/dot_general | solution.py:40
  16.8 5.1 %fusion.120 = bf16[1,6,192,128]{3,2,1,0:T(8,128)(2,1)S(1)} fusion(s32[6,192]{1,0:T(8,128)S(1)} %bitcast.178, f32[1280,128]{1,0:T(8,128)S(1)} %fusion.19, bf16[1,1,1,2,1280,1280]{5,4,3,2,1,0:T(8,128)(2,1)} %param.6, bf16[1,1,1,2,1280,128]{5,4,3,2,1,0:T(8,128)(2,1)S(1)} %copy-done), kind=kOutput, calls=%fused_computation.82 | convolution fusion | flops 798867456 | bytes 4562944 | tf_op jit(solution)/shard_map/dot_general | solution.py:40
  21.9 1.3 collective-permute-start.5
  23.2 4.9 %collective-permute-start = (bf16[2,1,192,128]{3,2,1,0:T(8,128)(2,1)S(1)}, bf16[2,1,192,128]{3,2,1,0:T(8,128)(2,1)S(1)}, u32[]{:S(2)}, u32[]{:S(2)}) collective-permute-start(bf16[2,1,192,128]{3,2,1,0:T(8,128)(2,1)S(1)} %get-tuple-element.16), channel_id=1, source_target_pairs={{0,8},{8,16},{16,24},{1,9},{9,17},{17,25},{2,10},{10,18},{18,26},{... | collective-permute-start | bytes 294920 | tf_op jit(solution)/shard_map/ppermute | solution.py:19
  28.2 1.3 collective-permute-start.1
  29.5 1.5 collective-permute-start.2
  31.0 1.3 collective-permute-start.3
  32.4 4.6 %collective-permute-start.4 = (bf16[2,1,192,128]{3,2,1,0:T(8,128)(2,1)S(1)}, bf16[2,1,192,128]{3,2,1,0:T(8,128)(2,1)S(1)}, u32[]{:S(2)}, u32[]{:S(2)}) collective-permute-start(bf16[2,1,192,128]{3,2,1,0:T(8,128)(2,1)S(1)} %get-tuple-element.20), channel_id=1, source_target_pairs={{0,1},{2,3},{4,5},{6,7},{8,9},{10,11},{12,13},{14,15},{16,17},{18,... | collective-permute-start | bytes 294920 | tf_op jit(solution)/shard_map/ppermute | solution.py:19
  37.1 1.9 %collective-permute-done.4 = bf16[2,1,192,128]{3,2,1,0:T(8,128)(2,1)S(1)} collective-permute-done((bf16[2,1,192,128]{3,2,1,0:T(8,128)(2,1)S(1)}, bf16[2,1,192,128]{3,2,1,0:T(8,128)(2,1)S(1)}, u32[]{:S(2)}, u32[]{:S(2)}) %collective-permute-start.4) | collective-permute-done | bytes 98336 | tf_op jit(solution)/shard_map/ppermute | solution.py:19
  39.2 1.9 %fusion.67 = bf16[1,1280,128]{2,1,0:T(8,128)(2,1)S(1)} fusion(bf16[1152,128]{1,0:T(8,128)(2,1)S(1)} %bitcast.175, s32[1152]{0:T(1024)S(1)} %eq.40), kind=kOutput, calls=%fused_computation.49 | convolution fusion | flops 379125760 | bytes 627200 | tf_op jit(solution)/shard_map/dot_general | solution.py:48
  41.1 1.9 %fusion.68 = bf16[1,1280,128]{2,1,0:T(8,128)(2,1)S(1)} fusion(bf16[1152,128]{1,0:T(8,128)(2,1)S(1)} %bitcast.174, s32[1152]{0:T(1024)S(1)} %eq.40), kind=kOutput, calls=%fused_computation.50 | convolution fusion | flops 379125760 | bytes 627200 | tf_op jit(solution)/shard_map/dot_general | solution.py:48
  45.7 4.0 %fusion.111 = bf16[1,6,192,128]{3,2,1,0:T(8,128)(2,1)S(1)} fusion(s32[6,192]{1,0:T(8,128)S(1)} %bitcast.179, f32[128,1280]{1,0:T(8,128)S(1)} %fusion.13, bf16[1,1,1,2,1280,1280]{5,4,3,2,1,0:T(8,128)(2,1)} %param.6, bf16[2,1280,128]{2,1,0:T(8,128)(2,1)S(1)} %fusion.89), kind=kOutput, calls=%fused_computation.79 | convolution fusion | flops 798867456 | bytes 4562944 | tf_op jit(solution)/shard_map/dot_general | solution.py:40
  49.7 4.0 %fusion.114 = bf16[1,6,192,128]{3,2,1,0:T(8,128)(2,1)S(1)} fusion(s32[6,192]{1,0:T(8,128)S(1)} %bitcast.180, f32[128,1280]{1,0:T(8,128)S(1)} %fusion.15, bf16[1,1,1,2,1280,1280]{5,4,3,2,1,0:T(8,128)(2,1)} %param.6, bf16[2,1280,128]{2,1,0:T(8,128)(2,1)S(1)} %fusion.89), kind=kOutput, calls=%fused_computation.80 | convolution fusion | flops 798867456 | bytes 4562944 | tf_op jit(solution)/shard_map/dot_general | solution.py:40
  53.8 4.6 %collective-permute-start.6 = (bf16[2,1,192,128]{3,2,1,0:T(8,128)(2,1)S(1)}, bf16[2,1,192,128]{3,2,1,0:T(8,128)(2,1)S(1)}, u32[]{:S(2)}, u32[]{:S(2)}) collective-permute-start(bf16[2,1,192,128]{3,2,1,0:T(8,128)(2,1)S(1)} %get-tuple-element.8), channel_id=1, source_target_pairs={{0,8},{8,16},{16,24},{1,9},{9,17},{17,25},{2,10},{10,18},{18,26},{... | collective-permute-start | bytes 294920 | tf_op jit(solution)/shard_map/ppermute | solution.py:19
  58.4 1.3 collective-permute-start.11
  59.7 1.3 collective-permute-start.7
  61.0 3.6 %collective-permute-start.8 = (bf16[2,1,192,128]{3,2,1,0:T(8,128)(2,1)S(1)}, bf16[2,1,192,128]{3,2,1,0:T(8,128)(2,1)S(1)}, u32[]{:S(2)}, u32[]{:S(2)}) collective-permute-start(bf16[2,1,192,128]{3,2,1,0:T(8,128)(2,1)S(1)} %get-tuple-element.10), channel_id=1, source_target_pairs={{0,2},{2,4},{4,6},{1,3},{3,5},{5,7},{8,10},{10,12},{12,14},{9,11},... | collective-permute-start | bytes 294920 | tf_op jit(solution)/shard_map/ppermute | solution.py:19
  65.9 4.5 %collective-permute-start.10 = (bf16[2,1,192,128]{3,2,1,0:T(8,128)(2,1)S(1)}, bf16[2,1,192,128]{3,2,1,0:T(8,128)(2,1)S(1)}, u32[]{:S(2)}, u32[]{:S(2)}) collective-permute-start(bf16[2,1,192,128]{3,2,1,0:T(8,128)(2,1)S(1)} %get-tuple-element.12), channel_id=1, source_target_pairs={{0,1},{2,3},{4,5},{6,7},{8,9},{10,11},{12,13},{14,15},{16,17},{18,... | collective-permute-start | bytes 294920 | tf_op jit(solution)/shard_map/ppermute | solution.py:19
  70.6 1.9 %collective-permute-done.10 = bf16[2,1,192,128]{3,2,1,0:T(8,128)(2,1)S(1)} collective-permute-done((bf16[2,1,192,128]{3,2,1,0:T(8,128)(2,1)S(1)}, bf16[2,1,192,128]{3,2,1,0:T(8,128)(2,1)S(1)}, u32[]{:S(2)}, u32[]{:S(2)}) %collective-permute-start.10) | collective-permute-done | bytes 98336 | tf_op jit(solution)/shard_map/ppermute | solution.py:19
  72.6 1.9 %fusion.65 = bf16[1,1280,128]{2,1,0:T(8,128)(2,1)S(1)} fusion(bf16[1152,128]{1,0:T(8,128)(2,1)S(1)} %bitcast.176, s32[1152]{0:T(1024)S(1)} %eq.40), kind=kOutput, calls=%fused_computation.47 | convolution fusion | flops 379125760 | bytes 627200 | tf_op jit(solution)/shard_map/dot_general | solution.py:48
  74.5 1.9 %fusion.66 = bf16[1,1280,128]{2,1,0:T(8,128)(2,1)S(1)} fusion(bf16[1152,128]{1,0:T(8,128)(2,1)S(1)} %bitcast.173, s32[1152]{0:T(1024)S(1)} %eq.40), kind=kOutput, calls=%fused_computation.48 | convolution fusion | flops 379125760 | bytes 627200 | tf_op jit(solution)/shard_map/dot_general | solution.py:48
  79.8 21.8 %reduce-scatter.3.cloned.1.call-done = f32[2,128,256]{2,1,0:T(8,128)} async-done(((f32[2,128,512]{2,1,0:T(8,128)}), f32[2,128,256]{2,1,0:T(8,128)}) %reduce-scatter.3.cloned.1.call-update) | async-done | bytes 262160 | tf_op jit(solution)/shard_map/reduce_scatter | solution.py:94
  101.6 59.3 %reduce-scatter.5.cloned.1.call-done = f32[2,8,256]{2,1,0:T(8,128)} async-done(((f32[2,128,256]{2,1,0:T(8,128)}), f32[2,8,256]{2,1,0:T(8,128)}) %reduce-scatter.5.cloned.1.call-update) | async-done | bytes 16400 | tf_op jit(solution)/shard_map/reduce_scatter | solution.py:95
  (62 shorter events, 10.1 us)
Async XLA Ops:
  6.5 3.1 %copy-start = (bf16[1,1,1,2,1280,128]{5,4,3,2,1,0:T(8,128)(2,1)S(1)}, bf16[1,1,1,2,1280,128]{5,4,3,2,1,0:T(8,128)(2,1)}, u32[]{:S(2)}) copy-start(bf16[1,1,1,2,1280,128]{5,4,3,2,1,0:T(8,128)(2,1)} %param.5) | copy-start | bytes 1966084
  6.5 95.1 %reduce-scatter.3.cloned.1.call-start = ((), (), s32[]{:S(2)}) async-start(), calls=%async_computation.2 | async-start | bytes 786432 | tf_op jit(solution)/shard_map/reduce_scatter | solution.py:94
  6.5 4.2 %copy-start.2 = (bf16[1,1,1,2,1280,1280]{5,4,3,2,1,0:T(8,128)(2,1)S(1)}, bf16[1,1,1,2,1280,1280]{5,4,3,2,1,0:T(8,128)(2,1)}, u32[]{:S(2)}) copy-start(bf16[1,1,1,2,1280,1280]{5,4,3,2,1,0:T(8,128)(2,1)} %param.6) | copy-start | bytes 19660804
  10.7 1.0 copy-start.1
  16.8 15.5 %copy-start.4 = (s32[1,1,1,6]{3,2,1,0:T(1,128)S(1)}, s32[1,1,1,6]{3,2,1,0:T(1,128)}, u32[]{:S(2)}) copy-start(s32[1,1,1,6]{3,2,1,0:T(1,128)} %param.9) | copy-start | bytes 76
  21.9 17.0 %collective-permute-start.5 = (bf16[2,1,192,128]{3,2,1,0:T(8,128)(2,1)S(1)}, bf16[2,1,192,128]{3,2,1,0:T(8,128)(2,1)S(1)}, u32[]{:S(2)}, u32[]{:S(2)}) collective-permute-start(bf16[2,1,192,128]{3,2,1,0:T(8,128)(2,1)S(1)} %get-tuple-element.15), channel_id=1, source_target_pairs={{1,0},{3,2},{5,4},{7,6},{9,8},{11,10},{13,12},{15,14},{17,16},{19,... | collective-permute-start | bytes 294920 | tf_op jit(solution)/shard_map/ppermute | solution.py:21
  23.2 9.1 %collective-permute-start = (bf16[2,1,192,128]{3,2,1,0:T(8,128)(2,1)S(1)}, bf16[2,1,192,128]{3,2,1,0:T(8,128)(2,1)S(1)}, u32[]{:S(2)}, u32[]{:S(2)}) collective-permute-start(bf16[2,1,192,128]{3,2,1,0:T(8,128)(2,1)S(1)} %get-tuple-element.16), channel_id=1, source_target_pairs={{0,8},{8,16},{16,24},{1,9},{9,17},{17,25},{2,10},{10,18},{18,26},{... | collective-permute-start | bytes 294920 | tf_op jit(solution)/shard_map/ppermute | solution.py:19
  28.2 8.8 %collective-permute-start.1 = (bf16[2,1,192,128]{3,2,1,0:T(8,128)(2,1)S(1)}, bf16[2,1,192,128]{3,2,1,0:T(8,128)(2,1)S(1)}, u32[]{:S(2)}, u32[]{:S(2)}) collective-permute-start(bf16[2,1,192,128]{3,2,1,0:T(8,128)(2,1)S(1)} %get-tuple-element.17), channel_id=1, source_target_pairs={{8,0},{16,8},{24,16},{9,1},{17,9},{25,17},{10,2},{18,10},{26,18},{... | collective-permute-start | bytes 294920 | tf_op jit(solution)/shard_map/ppermute | solution.py:21
  29.5 7.5 %collective-permute-start.2 = (bf16[2,1,192,128]{3,2,1,0:T(8,128)(2,1)S(1)}, bf16[2,1,192,128]{3,2,1,0:T(8,128)(2,1)S(1)}, u32[]{:S(2)}, u32[]{:S(2)}) collective-permute-start(bf16[2,1,192,128]{3,2,1,0:T(8,128)(2,1)S(1)} %get-tuple-element.18), channel_id=1, source_target_pairs={{0,2},{2,4},{4,6},{1,3},{3,5},{5,7},{8,10},{10,12},{12,14},{9,11},... | collective-permute-start | bytes 294920 | tf_op jit(solution)/shard_map/ppermute | solution.py:19
  31.0 6.1 %collective-permute-start.3 = (bf16[2,1,192,128]{3,2,1,0:T(8,128)(2,1)S(1)}, bf16[2,1,192,128]{3,2,1,0:T(8,128)(2,1)S(1)}, u32[]{:S(2)}, u32[]{:S(2)}) collective-permute-start(bf16[2,1,192,128]{3,2,1,0:T(8,128)(2,1)S(1)} %get-tuple-element.19), channel_id=1, source_target_pairs={{2,0},{4,2},{6,4},{3,1},{5,3},{7,5},{10,8},{12,10},{14,12},{11,9},... | collective-permute-start | bytes 294920 | tf_op jit(solution)/shard_map/ppermute | solution.py:21
  32.4 6.6 %collective-permute-start.4 = (bf16[2,1,192,128]{3,2,1,0:T(8,128)(2,1)S(1)}, bf16[2,1,192,128]{3,2,1,0:T(8,128)(2,1)S(1)}, u32[]{:S(2)}, u32[]{:S(2)}) collective-permute-start(bf16[2,1,192,128]{3,2,1,0:T(8,128)(2,1)S(1)} %get-tuple-element.20), channel_id=1, source_target_pairs={{0,1},{2,3},{4,5},{6,7},{8,9},{10,11},{12,13},{14,15},{16,17},{18,... | collective-permute-start | bytes 294920 | tf_op jit(solution)/shard_map/ppermute | solution.py:19
  39.0 4.2 %slice-start = ((s8[6553600]{0:T(1024)(128)(4,1)}), s8[4194304]{0:T(1024)(128)(4,1)S(1)}, s32[]{:S(2)}) async-start(s8[6553600]{0:T(1024)(128)(4,1)} %bitcast.181), calls=%async_computation.4 | async-start | bytes 8388608
  39.2 4.0 %slice-start.1 = ((s8[6553600]{0:T(1024)(128)(4,1)}), s8[2359296]{0:T(1024)(128)(4,1)S(1)}, s32[]{:S(2)}) async-start(s8[6553600]{0:T(1024)(128)(4,1)} %bitcast.181), calls=%async_computation.5 | async-start | bytes 4718592
  53.8 12.1 %collective-permute-start.6 = (bf16[2,1,192,128]{3,2,1,0:T(8,128)(2,1)S(1)}, bf16[2,1,192,128]{3,2,1,0:T(8,128)(2,1)S(1)}, u32[]{:S(2)}, u32[]{:S(2)}) collective-permute-start(bf16[2,1,192,128]{3,2,1,0:T(8,128)(2,1)S(1)} %get-tuple-element.8), channel_id=1, source_target_pairs={{0,8},{8,16},{16,24},{1,9},{9,17},{17,25},{2,10},{10,18},{18,26},{... | collective-permute-start | bytes 294920 | tf_op jit(solution)/shard_map/ppermute | solution.py:19
  58.4 14.1 %collective-permute-start.11 = (bf16[2,1,192,128]{3,2,1,0:T(8,128)(2,1)S(1)}, bf16[2,1,192,128]{3,2,1,0:T(8,128)(2,1)S(1)}, u32[]{:S(2)}, u32[]{:S(2)}) collective-permute-start(bf16[2,1,192,128]{3,2,1,0:T(8,128)(2,1)S(1)} %get-tuple-element.7), channel_id=1, source_target_pairs={{1,0},{3,2},{5,4},{7,6},{9,8},{11,10},{13,12},{15,14},{17,16},{19,... | collective-permute-start | bytes 294920 | tf_op jit(solution)/shard_map/ppermute | solution.py:21
  59.7 10.8 %collective-permute-start.7 = (bf16[2,1,192,128]{3,2,1,0:T(8,128)(2,1)S(1)}, bf16[2,1,192,128]{3,2,1,0:T(8,128)(2,1)S(1)}, u32[]{:S(2)}, u32[]{:S(2)}) collective-permute-start(bf16[2,1,192,128]{3,2,1,0:T(8,128)(2,1)S(1)} %get-tuple-element.9), channel_id=1, source_target_pairs={{8,0},{16,8},{24,16},{9,1},{17,9},{25,17},{10,2},{18,10},{26,18},{... | collective-permute-start | bytes 294920 | tf_op jit(solution)/shard_map/ppermute | solution.py:21
  61.0 9.5 %collective-permute-start.8 = (bf16[2,1,192,128]{3,2,1,0:T(8,128)(2,1)S(1)}, bf16[2,1,192,128]{3,2,1,0:T(8,128)(2,1)S(1)}, u32[]{:S(2)}, u32[]{:S(2)}) collective-permute-start(bf16[2,1,192,128]{3,2,1,0:T(8,128)(2,1)S(1)} %get-tuple-element.10), channel_id=1, source_target_pairs={{0,2},{2,4},{4,6},{1,3},{3,5},{5,7},{8,10},{10,12},{12,14},{9,11},... | collective-permute-start | bytes 294920 | tf_op jit(solution)/shard_map/ppermute | solution.py:19
  64.6 5.9 %collective-permute-start.9 = (bf16[2,1,192,128]{3,2,1,0:T(8,128)(2,1)S(1)}, bf16[2,1,192,128]{3,2,1,0:T(8,128)(2,1)S(1)}, u32[]{:S(2)}, u32[]{:S(2)}) collective-permute-start(bf16[2,1,192,128]{3,2,1,0:T(8,128)(2,1)S(1)} %get-tuple-element.11), channel_id=1, source_target_pairs={{2,0},{4,2},{6,4},{3,1},{5,3},{7,5},{10,8},{12,10},{14,12},{11,9},... | collective-permute-start | bytes 294920 | tf_op jit(solution)/shard_map/ppermute | solution.py:21
  65.9 6.5 %collective-permute-start.10 = (bf16[2,1,192,128]{3,2,1,0:T(8,128)(2,1)S(1)}, bf16[2,1,192,128]{3,2,1,0:T(8,128)(2,1)S(1)}, u32[]{:S(2)}, u32[]{:S(2)}) collective-permute-start(bf16[2,1,192,128]{3,2,1,0:T(8,128)(2,1)S(1)} %get-tuple-element.12), channel_id=1, source_target_pairs={{0,1},{2,3},{4,5},{6,7},{8,9},{10,11},{12,13},{14,15},{16,17},{18,... | collective-permute-start | bytes 294920 | tf_op jit(solution)/shard_map/ppermute | solution.py:19
  74.5 2.1 %copy-start.3 = (bf16[1,1,1,2,512,1280]{5,4,3,2,1,0:T(8,128)(2,1)S(1)}, bf16[1,1,1,2,512,1280]{5,4,3,2,1,0:T(8,128)(2,1)}, u32[]{:S(2)}) copy-start(bf16[1,1,1,2,512,1280]{5,4,3,2,1,0:T(8,128)(2,1)} %param.7) | copy-start | bytes 7864324
  79.8 81.1 %reduce-scatter.5.cloned.1.call-start = ((), (), s32[]{:S(2)}) async-start(), calls=%async_computation.3 | async-start | bytes 278528 | tf_op jit(solution)/shard_map/reduce_scatter | solution.py:95
Sparse Core Ops, SparseCore 0:
  79.9 21.6 reduce-scatter.2
  105.5 55.3 reduce-scatter.4
where the time goes:
time: 168 us
  waiting for transfers between devices  84.8 us (50%)
  matrix products  34.6 us (21%)
  starting transfers between devices  31.4 us (19%)
  between operations  13.9 us (8%)
    reduce_scatter x1, waiting for transfers between devices, shards(): lax.psum_scatter(partial_field, ('gx', 'gy'), scatter_dimension=1, tiled=...  59.3 us
    ppermute x6, starting transfers between devices, with_halo(): lax.ppermute(tail, axis, [(i, (i + 1) % count) for i in range(ends)])  23.6 us
    reduce_scatter x1, waiting for transfers between devices, shards(): lax.psum_scatter(radiated, 'gz', scatter_dimension=2, tiled=True)  21.8 us
    dot_general x4, matrix products, pick_rows(): jnp.dot(selector, values[part_pos], preferred_element_type=jnp.float32)  18.2 us
    ppermute x6, starting transfers between devices, with_halo(): lax.ppermute(head, axis, [((i + 1) % count, i) for i in range(ends)])  7.75 us
    dot_general x4, matrix products, put_rows(): lax.dot_general(selector, values[part_pos], (((0,), (0,)), ((), ())), pre...  7.54 us
    dot_general x2, matrix products, complex_dot(): jnp.dot(left_side[1], right_side[0], preferred_element_type=jnp.float32)  4.34 us
    ppermute x6, waiting for transfers between devices, with_halo(): lax.ppermute(tail, axis, [(i, (i + 1) % count) for i in range(ends)])  3.76 us
  transfers between devices with their start and end apart: 14, of which 4 were waited for; matrix products, arithmetic and copies ran while one was open for 0% of the time, Pallas kernels for 0%

commit v1 on v0

v1 whole, which is shorter than its diff:
```python
import functools

import jax
import jax.numpy as jnp
from jax import lax
from jax.experimental import pallas as pl
from jax.experimental.pallas import tpu as pltpu
from jax.sharding import PartitionSpec as P

ITERS = 2
AXES = ("gx", "gy", "gz")
F32 = jnp.float32
BF16 = jnp.bfloat16
CHUNKS = 5
VMEM_LIMIT = 40 * 1024 * 1024


def swap_rounds(sizes):
    rounds = []
    for pos, size in enumerate(sizes):
        if size > 1:
            rounds.append((pos, 0))
        if size > 2:
            rounds.append((pos, 1))
    return rounds


def swap_pairs(size, phase):
    pairs = []
    for low in range(phase, size - 1, 2):
        pairs += [(low, low + 1), (low + 1, low)]
    return pairs


def chosen_rows(slots_ref, ids_ref, count):
    return [slots_ref[pl.ds(ids_ref[pos], 1), :] for pos in range(count)]


def put_traces(rows, arrived, linked_ref, ids_ref, unknowns, width):
    total = None
    for pos, row in enumerate(rows):
        face = row.shape[-1]
        spots = lax.broadcasted_iota(jnp.int32, (unknowns, face), 0)
        chosen = jnp.where(spots == row, 1.0, 0.0).astype(BF16)
        gate = linked_ref[ids_ref[pos]].astype(F32)
        values = (arrived[pos][...].astype(F32) * gate).astype(BF16)
        part = jnp.dot(chosen, values, preferred_element_type=F32)
        total = part if total is None else total + part
    return total


def join(left, right):
    return jnp.concatenate([left, right], axis=1)


def sweep_kernel(count, first, ids_ref, linked_ref, slots_hbm, source_hbm, response_hbm, *refs):
    arrived = () if first else refs[:count]
    outs = refs[len(arrived) : len(arrived) + count]
    slots, source, response, straight, crossed, outgoing, sems = refs[len(arrived) + count :]
    unknowns = source.shape[1]
    columns = source.shape[2]
    step = unknowns // CHUNKS
    small = [
        pltpu.make_async_copy(slots_hbm, slots, sems.at[0]),
        pltpu.make_async_copy(source_hbm, source, sems.at[1]),
    ]
    large = [
        pltpu.make_async_copy(
            response_hbm.at[:, pl.ds(pos * step, step), :],
            response.at[:, pl.ds(pos * step, step), :],
            sems.at[2 + pos],
        )
        for pos in range(CHUNKS)
    ]
    for copy in small + large:
        copy.start()
    for copy in small:
        copy.wait()
    rows = chosen_rows(slots, ids_ref, count)
    if first:
        real, imag = source[0], source[1]
    else:
        traces = put_traces(rows, arrived, linked_ref, ids_ref, unknowns, 2 * columns)
        real = (traces[:, :columns] + source[0].astype(F32)).astype(BF16)
        imag = (traces[:, columns:] + source[1].astype(F32)).astype(BF16)
    straight[...] = join(real, imag)
    crossed[...] = join(-imag, real)
    for pos in range(CHUNKS):
        large[pos].wait()
        part = pl.ds(pos * step, step)
        outgoing[part, :] = (
            jnp.dot(response[0, part, :], straight[...], preferred_element_type=F32)
            + jnp.dot(response[1, part, :], crossed[...], preferred_element_type=F32)
        ).astype(BF16)
    face = slots.shape[1]
    padded = jnp.concatenate(rows + [rows[0]] * (8 - count), axis=0)
    upright = jnp.transpose(padded)
    spots = lax.broadcasted_iota(jnp.int32, (face, unknowns), 1)
    for pos in range(count):
        chosen = jnp.where(spots == upright[:, pos : pos + 1], 1.0, 0.0).astype(BF16)
        outs[pos][...] = jnp.dot(chosen, outgoing[...], preferred_element_type=F32).astype(BF16)


def radiate_kernel(count, ids_ref, linked_ref, slots_hbm, source_hbm, radiation_hbm, *refs):
    arrived = refs[:count]
    out = refs[count]
    slots, source, radiation, sems = refs[count + 1 :]
    unknowns = source.shape[1]
    columns = source.shape[2]
    copies = [
        pltpu.make_async_copy(slots_hbm, slots, sems.at[0]),
        pltpu.make_async_copy(source_hbm, source, sems.at[1]),
        pltpu.make_async_copy(radiation_hbm, radiation, sems.at[2]),
    ]
    for copy in copies:
        copy.start()
    for copy in copies[:2]:
        copy.wait()
    rows = chosen_rows(slots, ids_ref, count)
    traces = put_traces(rows, arrived, linked_ref, ids_ref, unknowns, 2 * columns)
    real = (traces[:, :columns] + source[0].astype(F32)).astype(BF16)
    imag = (traces[:, columns:] + source[1].astype(F32)).astype(BF16)
    straight = join(real, imag)
    crossed = join(-imag, real)
    copies[2].wait()
    field = jnp.dot(radiation[0], straight, preferred_element_type=F32) + jnp.dot(
        radiation[1], crossed, preferred_element_type=F32
    )
    out[0] = jnp.transpose(field[:, :columns])
    out[1] = jnp.transpose(field[:, columns:])


def any_spec():
    return pl.BlockSpec(memory_space=pl.ANY)


def smem_spec():
    return pl.BlockSpec(memory_space=pltpu.SMEM)


def vmem_spec():
    return pl.BlockSpec(memory_space=pltpu.VMEM)


def sweep(ids, linked, slots, source, response, arrived, count):
    unknowns, columns = source.shape[1:]
    face = slots.shape[1]
    first = arrived is None
    got = () if first else tuple(arrived)
    return pl.pallas_call(
        functools.partial(sweep_kernel, count, first),
        out_shape=[jax.ShapeDtypeStruct((face, 2 * columns), BF16)] * count,
        in_specs=[smem_spec(), smem_spec(), any_spec(), any_spec(), any_spec()] + [vmem_spec()] * len(got),
        out_specs=[vmem_spec()] * count,
        scratch_shapes=[
            pltpu.VMEM(slots.shape, slots.dtype),
            pltpu.VMEM(source.shape, BF16),
            pltpu.VMEM(response.shape, BF16),
            pltpu.VMEM((unknowns, 2 * columns), BF16),
            pltpu.VMEM((unknowns, 2 * columns), BF16),
            pltpu.VMEM((unknowns, 2 * columns), BF16),
            pltpu.SemaphoreType.DMA((2 + CHUNKS,)),
        ],
        compiler_params=pltpu.CompilerParams(vmem_limit_bytes=VMEM_LIMIT),
    )(ids, linked, slots, source, response, *got)


def radiate(ids, linked, slots, source, radiation, arrived, count):
    columns = source.shape[2]
    angles = radiation.shape[1]
    return pl.pallas_call(
        functools.partial(radiate_kernel, count),
        out_shape=jax.ShapeDtypeStruct((2, columns, angles), F32),
        in_specs=[smem_spec(), smem_spec(), any_spec(), any_spec(), any_spec()] + [vmem_spec()] * count,
        out_specs=vmem_spec(),
        scratch_shapes=[
            pltpu.VMEM(slots.shape, slots.dtype),
            pltpu.VMEM(source.shape, BF16),
            pltpu.VMEM(radiation.shape, BF16),
            pltpu.SemaphoreType.DMA((3,)),
        ],
        compiler_params=pltpu.CompilerParams(vmem_limit_bytes=VMEM_LIMIT),
    )(ids, linked, slots, source, radiation, *arrived)


def bit_count(size):
    return size.bit_length() - 1


def mask_pairs(sizes, flips):
    pairs = []
    for at_x in range(sizes[0]):
        for at_y in range(sizes[1]):
            for at_z in range(sizes[2]):
                here = (at_x * sizes[1] + at_y) * sizes[2] + at_z
                there = ((at_x ^ flips[0]) * sizes[1] + (at_y ^ flips[1])) * sizes[2] + (at_z ^ flips[2])
                pairs.append((here, there))
    return pairs


def scatter_sum(field, sizes, where):
    columns, angles = field.shape[1:]
    bits = [bit_count(size) for size in sizes]
    dims = {}
    shape = [2]
    for pos in (0, 1):
        for bit in reversed(range(bits[pos])):
            dims[(pos, bit)] = len(shape)
            shape.append(2)
    shape.append(columns // (sizes[0] * sizes[1]))
    for bit in reversed(range(bits[2])):
        dims[(2, bit)] = len(shape)
        shape.append(2)
    shape.append(angles // sizes[2])
    rounds = []
    rest = [(pos, bit) for bit in range(max(bits)) for pos in (1, 2, 0) if bit < bits[pos]]
    if (1, 0) in rest:
        rest.remove((1, 0))
        rounds.append([(1, 0)])
    planes = [item for item in rest if item[0] != 0] + [item for item in rest if item[0] == 0]
    rounds += [planes[pos : pos + 2] for pos in range(0, len(planes), 2)]
    total = field.reshape(shape)
    for group in rounds:
        def taken(code):
            piece = total
            for order, (pos, bit) in enumerate(group):
                mine = (where[pos] >> bit) & 1
                piece = lax.dynamic_slice_in_dim(piece, mine ^ ((code >> order) & 1), 1, axis=dims[(pos, bit)])
            return piece

        got = []
        for code in range(1, 2 ** len(group)):
            flips = [0, 0, 0]
            for order, (pos, bit) in enumerate(group):
                flips[pos] |= ((code >> order) & 1) << bit
            got.append(lax.ppermute(taken(code).astype(BF16), AXES, mask_pairs(sizes, flips)))
        total = taken(0)
        for piece in got:
            total = total + piece.astype(F32)
    return total.reshape(2, columns // (sizes[0] * sizes[1]), angles // sizes[2])


def shards(sizes, incident, response, radiation, face_index, linked):
    source = incident[0, 0, 0]
    response_mat = response[0, 0, 0]
    radiation_mat = radiation[0, 0, 0]
    slots = face_index[0, 0, 0]
    linked_faces = linked[0, 0, 0]
    where = [lax.axis_index(axis) for axis in AXES]
    rounds = swap_rounds(sizes)
    count = len(rounds)
    ids = jnp.stack([2 * pos + 1 - ((where[pos] + phase) & 1) for pos, phase in rounds]).astype(jnp.int32)
    arrived = None
    for turn in range(ITERS):
        faces = sweep(ids, linked_faces, slots, source, response_mat, arrived, count)
        arrived = [
            lax.ppermute(face, AXES[pos], swap_pairs(sizes[pos], phase))
            for face, (pos, phase) in zip(faces, rounds)
        ]
    field = radiate(ids, linked_faces, slots, source, radiation_mat, arrived, count)
    return scatter_sum(field, sizes, where)


def solution(mesh):
    sizes = tuple(mesh.shape[axis] for axis in AXES)
    return jax.shard_map(
        functools.partial(shards, sizes),
        mesh=mesh,
        in_specs=(
            P("gx", "gy", "gz", None, None, None),
            P("gx", "gy", "gz", None, None, None),
            P("gx", "gy", "gz", None, None, None),
            P("gx", "gy", "gz", None, None),
            P("gx", "gy", "gz", None),
        ),
        out_specs=P(None, ("gx", "gy"), "gz"),
        check_vma=False,
    )
```

time: 168 us -> 68.8 us (0.41)
  waiting for transfers between devices: 84.8 us -> 15.6 us
  matrix products: 34.6 us -> 0 us
  Pallas kernels: 0 us -> 19.7 us
  between operations: 13.9 us -> 0.15 us
  starting transfers between devices: 31.4 us -> 25.1 us
  local copies, waits for them, and re-layouts: 1.41 us -> 6.27 us
    reduce_scatter x2 -> x0, waiting for transfers between devices: 81 us -> none  [the longest x1 59.3 us: shards(): lax.psum_scatter(partial_field, ('gx', 'gy'), scatter_dimension=1, tiled=...]
    dot_general x16 -> x0, matrix products: 34.6 us -> none  [the longest x4 18.2 us: pick_rows(): jnp.dot(selector, values[part_pos], preferred_element_type=jnp.float32)]
    pallas_call x0 -> x3, Pallas kernels: none -> 19.7 us  [the longest x2 14.9 us: sweep(): pl.pallas_call(functools.partial(sweep_kernel, count, first), out_shape=[...]
    ppermute x12 -> x17, waiting for transfers between devices: 3.77 us -> 15.6 us  [the longest x7 9.06 us: scatter_sum(): lax.ppermute(taken(code).astype(BF16), AXES, mask_pairs(sizes, flips))]
    ppermute x12 -> x17, starting transfers between devices: 31.4 us -> 25.1 us  [the longest x10 15.5 us: shards(): lax.ppermute(face, AXES[pos], swap_pairs(sizes[pos], phase))]
    unnamed x25 -> x16, local copies, waits for them, and re-layouts: 1.22 us -> 6.12 us
  transfers between devices with their start and end apart: 14 -> 17, of which waited for: 4 -> 8; matrix products, arithmetic and copies ran while one was open for 0% -> 0% of each run, Pallas kernels for 0% -> 0%
where the time goes in v1:
time: 68.8 us; the launch traced here: 68.4 us
  starting transfers between devices  25.1 us (36%)
  Pallas kernels  19.7 us (29%)
  waiting for transfers between devices  15.6 us (23%)
  local copies, waits for them, and re-layouts  6.27 us (9%)
  other arithmetic  1.61 us (2%)
    ppermute x10, starting transfers between devices, shards(): lax.ppermute(face, AXES[pos], swap_pairs(sizes[pos], phase))  15.5 us
    pallas_call x2, Pallas kernels, sweep(): pl.pallas_call(functools.partial(sweep_kernel, count, first), out_shape=[...  14.9 us
    ppermute x7, starting transfers between devices, scatter_sum(): lax.ppermute(taken(code).astype(BF16), AXES, mask_pairs(sizes, flips))  9.66 us
    ppermute x7, waiting for transfers between devices, scatter_sum(): lax.ppermute(taken(code).astype(BF16), AXES, mask_pairs(sizes, flips))  9.06 us
    ppermute x10, waiting for transfers between devices, shards(): lax.ppermute(face, AXES[pos], swap_pairs(sizes[pos], phase))  6.54 us
    unnamed x16, local copies, waits for them, and re-layouts  6.12 us
    pallas_call x1, Pallas kernels, radiate(): pl.pallas_call(functools.partial(radiate_kernel, count), out_shape=jax.Sh...  4.7 us
  transfers between devices with their start and end apart: 17, of which 8 were waited for; matrix products, arithmetic and copies ran while one was open for 0% of the time, Pallas kernels for 0%

profile of v1, /device:TPU:0, one launch (start us, length us, event | category | flops | bytes accessed | tf_op | source)
XLA Modules:
  0.0 68.4 jit_solution(13038046764999394462)
XLA Ops:
  0.8 2.9 %copy-done = bf16[1,1,1,2,1280,1280]{5,4,3,2,1,0:T(8,128)(2,1)S(1)} copy-done((bf16[1,1,1,2,1280,1280]{5,4,3,2,1,0:T(8,128)(2,1)S(1)}, bf16[1,1,1,2,1280,1280]{5,4,3,2,1,0:T(8,128)(2,1)}, u32[]{:S(2)}) %copy-start) | copy-done | bytes 6553624
  3.6 1.1 %copy-done.1 = bf16[1,1,1,2,1280,128]{5,4,3,2,1,0:T(8,128)(2,1)S(1)} copy-done((bf16[1,1,1,2,1280,128]{5,4,3,2,1,0:T(8,128)(2,1)S(1)}, bf16[1,1,1,2,1280,128]{5,4,3,2,1,0:T(8,128)(2,1)}, u32[]{:S(2)}) %copy-start.1) | copy-done | bytes 655384
  5.4 6.4 %shard_map.55 = (bf16[192,256]{1,0:T(8,128)(2,1)S(1)}, bf16[192,256]{1,0:T(8,128)(2,1)S(1)}, bf16[192,256]{1,0:T(8,128)(2,1)S(1)}, bf16[192,256]{1,0:T(8,128)(2,1)S(1)}, bf16[192,256]{1,0:T(8,128)(2,1)S(1)}) custom-call(s32[5]{0:T(128)S(1)} %stack.23.ids_ref, s32[6]{0:T(128)S(1)} %bitcast.26, s32[6,192]{1,0:T(8,128)S(1)} %bitcast.23, ...), custom_call_target="tpu_custom_call" | custom-call | tf_op jit(solution)/shard_map/pallas_call | solution.py:150
  11.8 3.1 %collective-permute-start = (bf16[192,256]{1,0:T(8,128)(2,1)S(1)}, bf16[192,256]{1,0:T(8,128)(2,1)S(1)}, u32[]{:S(2)}, u32[]{:S(2)}) collective-permute-start(bf16[192,256]{1,0:T(8,128)(2,1)S(1)} %get-tuple-element.15), channel_id=1, source_target_pairs={{0,8},{8,0},{16,24},{24,16},{1,9},{9,1},{17,25},{25,17},{2,10},{10... | collective-permute-start | bytes 294920 | tf_op jit(solution)/shard_map/ppermute | solution.py:257
  16.3 1.6 %collective-permute-start.4 = (bf16[192,256]{1,0:T(8,128)(2,1)S(1)}, bf16[192,256]{1,0:T(8,128)(2,1)S(1)}, u32[]{:S(2)}, u32[]{:S(2)}) collective-permute-start(bf16[192,256]{1,0:T(8,128)(2,1)S(1)} %get-tuple-element.19), channel_id=1, source_target_pairs={{0,1},{1,0},{2,3},{3,2},{4,5},{5,4},{6,7},{7,6},{8,9},{9,8},{10,11... | collective-permute-start | bytes 294920 | tf_op jit(solution)/shard_map/ppermute | solution.py:257
  17.8 3.1 %collective-permute-done.4.refs_4_ = bf16[192,256]{1,0:T(8,128)(2,1)S(1)} collective-permute-done((bf16[192,256]{1,0:T(8,128)(2,1)S(1)}, bf16[192,256]{1,0:T(8,128)(2,1)S(1)}, u32[]{:S(2)}, u32[]{:S(2)}) %collective-permute-start.4) | collective-permute-done | bytes 98336 | tf_op jit(solution)/shard_map/ppermute | solution.py:257
  20.9 8.6 %shard_map.56 = (bf16[192,256]{1,0:T(8,128)(2,1)}, bf16[192,256]{1,0:T(8,128)(2,1)}, bf16[192,256]{1,0:T(8,128)(2,1)}, bf16[192,256]{1,0:T(8,128)(2,1)}, bf16[192,256]{1,0:T(8,128)(2,1)}) custom-call(s32[5]{0:T(128)S(1)} %stack.23.ids_ref, s32[6]{0:T(128)S(1)} %bitcast.27, s32[6,192]{1,0:T(8,128)S(1)} %bitcast.24, bf16[2,1280,128]{2,1,0:T(8,128)(2,1)S(1)} %bitcast.18, ...), custom_call_target="tpu_custom_call" | custom-call | tf_op jit(solution)/shard_map/pallas_call | solution.py:150
  29.5 4.5 %collective-permute-start.5 = (bf16[192,256]{1,0:T(8,128)(2,1)}, bf16[192,256]{1,0:T(8,128)(2,1)S(1)}, u32[]{:S(2)}, u32[]{:S(2)}) collective-permute-start(bf16[192,256]{1,0:T(8,128)(2,1)} %get-tuple-element.20), channel_id=1, source_target_pairs={{0,8},{8,0},{16,24},{24,16},{1,9},{9,1},{17,25},{25,17},{2,10},{10... | collective-permute-start | bytes 294920 | tf_op jit(solution)/shard_map/ppermute | solution.py:257
  34.7 1.5 %collective-permute-start.7 = (bf16[192,256]{1,0:T(8,128)(2,1)}, bf16[192,256]{1,0:T(8,128)(2,1)}, u32[]{:S(2)}, u32[]{:S(2)}) collective-permute-start(bf16[192,256]{1,0:T(8,128)(2,1)} %get-tuple-element.22), channel_id=1, source_target_pairs={{0,2},{2,0},{4,6},{6,4},{1,3},{3,1},{5,7},{7,5},{8,10},{10,8},{12,... | collective-permute-start | bytes 294920 | tf_op jit(solution)/shard_map/ppermute | solution.py:257
  36.2 1.3 %collective-permute-start.8 = (bf16[192,256]{1,0:T(8,128)(2,1)}, bf16[192,256]{1,0:T(8,128)(2,1)}, u32[]{:S(2)}, u32[]{:S(2)}) collective-permute-start(bf16[192,256]{1,0:T(8,128)(2,1)} %get-tuple-element.23), channel_id=1, source_target_pairs={{2,4},{4,2},{3,5},{5,3},{10,12},{12,10},{11,13},{13,11},{18,20},{2... | collective-permute-start | bytes 294920 | tf_op jit(solution)/shard_map/ppermute | solution.py:257
  37.5 1.5 %collective-permute-start.9 = (bf16[192,256]{1,0:T(8,128)(2,1)}, bf16[192,256]{1,0:T(8,128)(2,1)}, u32[]{:S(2)}, u32[]{:S(2)}) collective-permute-start(bf16[192,256]{1,0:T(8,128)(2,1)} %get-tuple-element.24), channel_id=1, source_target_pairs={{0,1},{1,0},{2,3},{3,2},{4,5},{5,4},{6,7},{7,6},{8,9},{9,8},{10,11... | collective-permute-start | bytes 294920 | tf_op jit(solution)/shard_map/ppermute | solution.py:257
  39.0 3.4 %collective-permute-done.9.refs_4_ = bf16[192,256]{1,0:T(8,128)(2,1)} collective-permute-done((bf16[192,256]{1,0:T(8,128)(2,1)}, bf16[192,256]{1,0:T(8,128)(2,1)}, u32[]{:S(2)}, u32[]{:S(2)}) %collective-permute-start.9) | collective-permute-done | bytes 98336 | tf_op jit(solution)/shard_map/ppermute | solution.py:257
  42.4 4.7 %shard_map.57 = f32[2,128,512]{2,1,0:T(8,128)S(1)} custom-call(s32[5]{0:T(128)S(1)} %stack.23.ids_ref, s32[6]{0:T(128)S(1)} %bitcast.28, s32[6,192]{1,0:T(8,128)S(1)} %bitcast.25, bf16[2,1280,128]{2,1,0:T(8,128)(2,1)S(1)} %bitcast.19, bf16[2,512,1280]{2,1,0:T(8,128)(2,1)S(1)} %bitcast.20, bf16[192,256]{1,0:T(8,128)(2,1)S(1)} %collective-permute-done.5.refs_0_, ...), custom_call_target="tpu_custom_call" | custom-call | tf_op jit(solution)/shard_map/pallas_call | solution.py:171
  48.0 1.6 %collective-permute-start.10 = (bf16[2,2,2,2,1,8,2,256]{7,5,0,6,4,3,2,1:T(8,128)(2,1)S(1)}, bf16[2,2,2,2,1,8,2,256]{7,5,0,6,4,3,2,1:T(8,128)(2,1)S(1)}, u32[]{:S(2)}, u32[]{:S(2)}) collective-permute-start(bf16[2,2,2,2,1,8,2,256]{7,5,0,6,4,3,2,1:T(8,128)(2,1)S(1)} %copy.14), channel_id=1, source_target_pairs={{0,2},{1,3},{2,0},{3,1},{4,6},{5,7},{6,4},{7,5},{8,10},{9,11},{10,... | collective-permute-start | bytes 393224 | tf_op jit(solution)/shard_map/ppermute | solution.py:236
  49.6 1.0 %collective-permute-done.10 = bf16[2,2,2,2,1,8,2,256]{7,5,0,6,4,3,2,1:T(8,128)(2,1)S(1)} collective-permute-done((bf16[2,2,2,2,1,8,2,256]{7,5,0,6,4,3,2,1:T(8,128)(2,1)S(1)}, bf16[2,2,2,2,1,8,2,256]{7,5,0,6,4,3,2,1:T(8,128)(2,1)S(1)}, u32[]{:S(2)}, u32[]{:S(2)}) %collective-permute-start.10) | collective-permute-done | bytes 131104 | tf_op jit(solution)/shard_map/ppermute | solution.py:236
  51.6 1.6 %collective-permute-start.11 = (bf16[2,2,2,1,1,8,1,256]{7,5,0,6,4,3,2,1:T(8,128)(2,1)S(1)}, bf16[2,2,2,1,1,8,1,256]{7,5,0,6,4,3,2,1:T(8,128)(2,1)S(1)}, u32[]{:S(2)}, u32[]{:S(2)}) collective-permute-start(bf16[2,2,2,1,1,8,1,256]{7,5,0,6,4,3,2,1:T(8,128)(2,1)S(1)} %get-tuple-element.25), channel_id=1, source_target_pairs={{0,1},{1,0},{2,3},{3,2},{4,5},{5,4},{6,7},{7,6},{8,9},{9,8},{10,11... | collective-permute-start | bytes 98312 | tf_op jit(solution)/shard_map/ppermute | solution.py:236
  53.2 1.4 %collective-permute-start.12 = (bf16[2,2,2,1,1,8,1,256]{7,5,0,6,4,3,2,1:T(8,128)(2,1)S(1)}, bf16[2,2,2,1,1,8,1,256]{7,5,0,6,4,3,2,1:T(8,128)(2,1)S(1)}, u32[]{:S(2)}, u32[]{:S(2)}) collective-permute-start(bf16[2,2,2,1,1,8,1,256]{7,5,0,6,4,3,2,1:T(8,128)(2,1)S(1)} %get-tuple-element.27), channel_id=1, source_target_pairs={{0,4},{1,5},{2,6},{3,7},{4,0},{5,1},{6,2},{7,3},{8,12},{9,13},{10,... | collective-permute-start | bytes 98312 | tf_op jit(solution)/shard_map/ppermute | solution.py:236
  55.6 1.5 %collective-permute-done.12 = bf16[2,2,2,1,1,8,1,256]{7,5,0,6,4,3,2,1:T(8,128)(2,1)S(1)} collective-permute-done((bf16[2,2,2,1,1,8,1,256]{7,5,0,6,4,3,2,1:T(8,128)(2,1)S(1)}, bf16[2,2,2,1,1,8,1,256]{7,5,0,6,4,3,2,1:T(8,128)(2,1)S(1)}, u32[]{:S(2)}, u32[]{:S(2)}) %collective-permute-start.12) | collective-permute-done | bytes 32800 | tf_op jit(solution)/shard_map/ppermute | solution.py:236
  57.1 2.3 %collective-permute-done.13 = bf16[2,2,2,1,1,8,1,256]{7,5,0,6,4,3,2,1:T(8,128)(2,1)S(1)} collective-permute-done((bf16[2,2,2,1,1,8,1,256]{7,5,0,6,4,3,2,1:T(8,128)(2,1)S(1)}, bf16[2,2,2,1,1,8,1,256]{7,5,0,6,4,3,2,1:T(8,128)(2,1)S(1)}, u32[]{:S(2)}, u32[]{:S(2)}) %collective-permute-start.13) | collective-permute-done | bytes 32800 | tf_op jit(solution)/shard_map/ppermute | solution.py:236
  59.5 1.3 %collective-permute-start.14 = (bf16[2,1,1,1,1,8,1,256]{7,5,0,6,4,3,2,1:T(8,128)(2,1)S(1)}, bf16[2,1,1,1,1,8,1,256]{7,5,0,6,4,3,2,1:T(8,128)(2,1)S(1)}, u32[]{:S(2)}, u32[]{:S(2)}) collective-permute-start(bf16[2,1,1,1,1,8,1,256]{7,5,0,6,4,3,2,1:T(8,128)(2,1)S(1)} %get-tuple-element.28), channel_id=1, source_target_pairs={{0,8},{1,9},{2,10},{3,11},{4,12},{5,13},{6,14},{7,15},{8,0},{9,1},... | collective-permute-start | bytes 24584 | tf_op jit(solution)/shard_map/ppermute | solution.py:236
  60.8 1.5 %collective-permute-start.15 = (bf16[2,1,1,1,1,8,1,256]{7,5,0,6,4,3,2,1:T(8,128)(2,1)S(1)}, bf16[2,1,1,1,1,8,1,256]{7,5,0,6,4,3,2,1:T(8,128)(2,1)S(1)}, u32[]{:S(2)}, u32[]{:S(2)}) collective-permute-start(bf16[2,1,1,1,1,8,1,256]{7,5,0,6,4,3,2,1:T(8,128)(2,1)S(1)} %get-tuple-element.30), channel_id=1, source_target_pairs={{0,16},{1,17},{2,18},{3,19},{4,20},{5,21},{6,22},{7,23},{8,24},{9,... | collective-permute-start | bytes 24584 | tf_op jit(solution)/shard_map/ppermute | solution.py:236
  62.3 1.6 %collective-permute-start.16 = (bf16[2,1,1,1,1,8,1,256]{7,5,0,6,4,3,2,1:T(8,128)(2,1)S(1)}, bf16[2,1,1,1,1,8,1,256]{7,5,0,6,4,3,2,1:T(8,128)(2,1)S(1)}, u32[]{:S(2)}, u32[]{:S(2)}) collective-permute-start(bf16[2,1,1,1,1,8,1,256]{7,5,0,6,4,3,2,1:T(8,128)(2,1)S(1)} %get-tuple-element.29), channel_id=1, source_target_pairs={{0,24},{1,25},{2,26},{3,27},{4,28},{5,29},{6,30},{7,31},{8,16},{9,... | collective-permute-start | bytes 24584 | tf_op jit(solution)/shard_map/ppermute | solution.py:236
  63.9 1.4 %collective-permute-done.15 = bf16[2,1,1,1,1,8,1,256]{7,5,0,6,4,3,2,1:T(8,128)(2,1)S(1)} collective-permute-done((bf16[2,1,1,1,1,8,1,256]{7,5,0,6,4,3,2,1:T(8,128)(2,1)S(1)}, bf16[2,1,1,1,1,8,1,256]{7,5,0,6,4,3,2,1:T(8,128)(2,1)S(1)}, u32[]{:S(2)}, u32[]{:S(2)}) %collective-permute-start.15) | collective-permute-done | bytes 8224 | tf_op jit(solution)/shard_map/ppermute | solution.py:236
  65.3 2.4 %collective-permute-done.16 = bf16[2,1,1,1,1,8,1,256]{7,5,0,6,4,3,2,1:T(8,128)(2,1)S(1)} collective-permute-done((bf16[2,1,1,1,1,8,1,256]{7,5,0,6,4,3,2,1:T(8,128)(2,1)S(1)}, bf16[2,1,1,1,1,8,1,256]{7,5,0,6,4,3,2,1:T(8,128)(2,1)S(1)}, u32[]{:S(2)}, u32[]{:S(2)}) %collective-permute-start.16) | collective-permute-done | bytes 8224 | tf_op jit(solution)/shard_map/ppermute | solution.py:236
  (36 shorter events, 7.0 us)
Async XLA Ops:
  0.8 2.9 %copy-start = (bf16[1,1,1,2,1280,1280]{5,4,3,2,1,0:T(8,128)(2,1)S(1)}, bf16[1,1,1,2,1280,1280]{5,4,3,2,1,0:T(8,128)(2,1)}, u32[]{:S(2)}) copy-start(bf16[1,1,1,2,1280,1280]{5,4,3,2,1,0:T(8,128)(2,1)} %param.6) | copy-start | bytes 19660804
  3.6 1.1 %copy-start.1 = (bf16[1,1,1,2,1280,128]{5,4,3,2,1,0:T(8,128)(2,1)S(1)}, bf16[1,1,1,2,1280,128]{5,4,3,2,1,0:T(8,128)(2,1)}, u32[]{:S(2)}) copy-start(bf16[1,1,1,2,1280,128]{5,4,3,2,1,0:T(8,128)(2,1)} %param.5) | copy-start | bytes 1966084
  4.7 0.7 copy-start.5
  5.4 37.0 %copy-start.2 = (bf16[1,1,1,2,1280,128]{5,4,3,2,1,0:T(8,128)(2,1)S(1)}, bf16[1,1,1,2,1280,128]{5,4,3,2,1,0:T(8,128)(2,1)}, u32[]{:S(2)}) copy-start(bf16[1,1,1,2,1280,128]{5,4,3,2,1,0:T(8,128)(2,1)} %param.5) | copy-start | bytes 1966084
  5.4 37.0 %copy-start.3 = (bf16[1,1,1,2,512,1280]{5,4,3,2,1,0:T(8,128)(2,1)S(1)}, bf16[1,1,1,2,512,1280]{5,4,3,2,1,0:T(8,128)(2,1)}, u32[]{:S(2)}) copy-start(bf16[1,1,1,2,512,1280]{5,4,3,2,1,0:T(8,128)(2,1)} %param.7) | copy-start | bytes 7864324
  5.4 37.0 %copy-start.6 = (s32[1,1,1,6]{3,2,1,0:T(1,128)S(1)}, s32[1,1,1,6]{3,2,1,0:T(1,128)}, u32[]{:S(2)}) copy-start(s32[1,1,1,6]{3,2,1,0:T(1,128)} %param.9) | copy-start | bytes 76
  11.8 6.1 %collective-permute-start = (bf16[192,256]{1,0:T(8,128)(2,1)S(1)}, bf16[192,256]{1,0:T(8,128)(2,1)S(1)}, u32[]{:S(2)}, u32[]{:S(2)}) collective-permute-start(bf16[192,256]{1,0:T(8,128)(2,1)S(1)} %get-tuple-element.15), channel_id=1, source_target_pairs={{0,8},{8,0},{16,24},{24,16},{1,9},{9,1},{17,25},{25,17},{2,10},{10... | collective-permute-start | bytes 294920 | tf_op jit(solution)/shard_map/ppermute | solution.py:257
  14.8 3.0 %collective-permute-start.1 = (bf16[192,256]{1,0:T(8,128)(2,1)S(1)}, bf16[192,256]{1,0:T(8,128)(2,1)S(1)}, u32[]{:S(2)}, u32[]{:S(2)}) collective-permute-start(bf16[192,256]{1,0:T(8,128)(2,1)S(1)} %get-tuple-element.16), channel_id=1, source_target_pairs={{8,16},{16,8},{9,17},{17,9},{10,18},{18,10},{11,19},{19,11},{12,20... | collective-permute-start | bytes 294920 | tf_op jit(solution)/shard_map/ppermute | solution.py:257
  15.5 2.3 %collective-permute-start.2 = (bf16[192,256]{1,0:T(8,128)(2,1)S(1)}, bf16[192,256]{1,0:T(8,128)(2,1)S(1)}, u32[]{:S(2)}, u32[]{:S(2)}) collective-permute-start(bf16[192,256]{1,0:T(8,128)(2,1)S(1)} %get-tuple-element.17), channel_id=1, source_target_pairs={{0,2},{2,0},{4,6},{6,4},{1,3},{3,1},{5,7},{7,5},{8,10},{10,8},{12,... | collective-permute-start | bytes 294920 | tf_op jit(solution)/shard_map/ppermute | solution.py:257
  15.6 2.2 %collective-permute-start.3 = (bf16[192,256]{1,0:T(8,128)(2,1)S(1)}, bf16[192,256]{1,0:T(8,128)(2,1)S(1)}, u32[]{:S(2)}, u32[]{:S(2)}) collective-permute-start(bf16[192,256]{1,0:T(8,128)(2,1)S(1)} %get-tuple-element.18), channel_id=1, source_target_pairs={{2,4},{4,2},{3,5},{5,3},{10,12},{12,10},{11,13},{13,11},{18,20},{2... | collective-permute-start | bytes 294920 | tf_op jit(solution)/shard_map/ppermute | solution.py:257
  16.3 4.7 %collective-permute-start.4 = (bf16[192,256]{1,0:T(8,128)(2,1)S(1)}, bf16[192,256]{1,0:T(8,128)(2,1)S(1)}, u32[]{:S(2)}, u32[]{:S(2)}) collective-permute-start(bf16[192,256]{1,0:T(8,128)(2,1)S(1)} %get-tuple-element.19), channel_id=1, source_target_pairs={{0,1},{1,0},{2,3},{3,2},{4,5},{5,4},{6,7},{7,6},{8,9},{9,8},{10,11... | collective-permute-start | bytes 294920 | tf_op jit(solution)/shard_map/ppermute | solution.py:257
  29.5 9.4 %collective-permute-start.5 = (bf16[192,256]{1,0:T(8,128)(2,1)}, bf16[192,256]{1,0:T(8,128)(2,1)S(1)}, u32[]{:S(2)}, u32[]{:S(2)}) collective-permute-start(bf16[192,256]{1,0:T(8,128)(2,1)} %get-tuple-element.20), channel_id=1, source_target_pairs={{0,8},{8,0},{16,24},{24,16},{1,9},{9,1},{17,25},{25,17},{2,10},{10... | collective-permute-start | bytes 294920 | tf_op jit(solution)/shard_map/ppermute | solution.py:257
  34.0 5.0 %collective-permute-start.6 = (bf16[192,256]{1,0:T(8,128)(2,1)}, bf16[192,256]{1,0:T(8,128)(2,1)S(1)}, u32[]{:S(2)}, u32[]{:S(2)}) collective-permute-start(bf16[192,256]{1,0:T(8,128)(2,1)} %get-tuple-element.21), channel_id=1, source_target_pairs={{8,16},{16,8},{9,17},{17,9},{10,18},{18,10},{11,19},{19,11},{12,20... | collective-permute-start | bytes 294920 | tf_op jit(solution)/shard_map/ppermute | solution.py:257
  34.7 4.3 %collective-permute-start.7 = (bf16[192,256]{1,0:T(8,128)(2,1)}, bf16[192,256]{1,0:T(8,128)(2,1)}, u32[]{:S(2)}, u32[]{:S(2)}) collective-permute-start(bf16[192,256]{1,0:T(8,128)(2,1)} %get-tuple-element.22), channel_id=1, source_target_pairs={{0,2},{2,0},{4,6},{6,4},{1,3},{3,1},{5,7},{7,5},{8,10},{10,8},{12,... | collective-permute-start | bytes 294920 | tf_op jit(solution)/shard_map/ppermute | solution.py:257
  36.2 2.8 %collective-permute-start.8 = (bf16[192,256]{1,0:T(8,128)(2,1)}, bf16[192,256]{1,0:T(8,128)(2,1)}, u32[]{:S(2)}, u32[]{:S(2)}) collective-permute-start(bf16[192,256]{1,0:T(8,128)(2,1)} %get-tuple-element.23), channel_id=1, source_target_pairs={{2,4},{4,2},{3,5},{5,3},{10,12},{12,10},{11,13},{13,11},{18,20},{2... | collective-permute-start | bytes 294920 | tf_op jit(solution)/shard_map/ppermute | solution.py:257
  37.5 4.9 %collective-permute-start.9 = (bf16[192,256]{1,0:T(8,128)(2,1)}, bf16[192,256]{1,0:T(8,128)(2,1)}, u32[]{:S(2)}, u32[]{:S(2)}) collective-permute-start(bf16[192,256]{1,0:T(8,128)(2,1)} %get-tuple-element.24), channel_id=1, source_target_pairs={{0,1},{1,0},{2,3},{3,2},{4,5},{5,4},{6,7},{7,6},{8,9},{9,8},{10,11... | collective-permute-start | bytes 294920 | tf_op jit(solution)/shard_map/ppermute | solution.py:257
  47.1 0.8 %copy-start.4 = (f32[2,128,512]{2,1,0:T(8,128)}, f32[2,128,512]{2,1,0:T(8,128)S(1)}, u32[]{:S(2)}) copy-start(f32[2,128,512]{2,1,0:T(8,128)S(1)} %shard_map.57) | copy-start | bytes 1572868
  48.0 2.6 %collective-permute-start.10 = (bf16[2,2,2,2,1,8,2,256]{7,5,0,6,4,3,2,1:T(8,128)(2,1)S(1)}, bf16[2,2,2,2,1,8,2,256]{7,5,0,6,4,3,2,1:T(8,128)(2,1)S(1)}, u32[]{:S(2)}, u32[]{:S(2)}) collective-permute-start(bf16[2,2,2,2,1,8,2,256]{7,5,0,6,4,3,2,1:T(8,128)(2,1)S(1)} %copy.14), channel_id=1, source_target_pairs={{0,2},{1,3},{2,0},{3,1},{4,6},{5,7},{6,4},{7,5},{8,10},{9,11},{10,... | collective-permute-start | bytes 393224 | tf_op jit(solution)/shard_map/ppermute | solution.py:236
  51.6 4.0 %collective-permute-start.11 = (bf16[2,2,2,1,1,8,1,256]{7,5,0,6,4,3,2,1:T(8,128)(2,1)S(1)}, bf16[2,2,2,1,1,8,1,256]{7,5,0,6,4,3,2,1:T(8,128)(2,1)S(1)}, u32[]{:S(2)}, u32[]{:S(2)}) collective-permute-start(bf16[2,2,2,1,1,8,1,256]{7,5,0,6,4,3,2,1:T(8,128)(2,1)S(1)} %get-tuple-element.25), channel_id=1, source_target_pairs={{0,1},{1,0},{2,3},{3,2},{4,5},{5,4},{6,7},{7,6},{8,9},{9,8},{10,11... | collective-permute-start | bytes 98312 | tf_op jit(solution)/shard_map/ppermute | solution.py:236
  53.2 3.9 %collective-permute-start.12 = (bf16[2,2,2,1,1,8,1,256]{7,5,0,6,4,3,2,1:T(8,128)(2,1)S(1)}, bf16[2,2,2,1,1,8,1,256]{7,5,0,6,4,3,2,1:T(8,128)(2,1)S(1)}, u32[]{:S(2)}, u32[]{:S(2)}) collective-permute-start(bf16[2,2,2,1,1,8,1,256]{7,5,0,6,4,3,2,1:T(8,128)(2,1)S(1)} %get-tuple-element.27), channel_id=1, source_target_pairs={{0,4},{1,5},{2,6},{3,7},{4,0},{5,1},{6,2},{7,3},{8,12},{9,13},{10,... | collective-permute-start | bytes 98312 | tf_op jit(solution)/shard_map/ppermute | solution.py:236
  54.6 4.8 %collective-permute-start.13 = (bf16[2,2,2,1,1,8,1,256]{7,5,0,6,4,3,2,1:T(8,128)(2,1)S(1)}, bf16[2,2,2,1,1,8,1,256]{7,5,0,6,4,3,2,1:T(8,128)(2,1)S(1)}, u32[]{:S(2)}, u32[]{:S(2)}) collective-permute-start(bf16[2,2,2,1,1,8,1,256]{7,5,0,6,4,3,2,1:T(8,128)(2,1)S(1)} %get-tuple-element.26), channel_id=1, source_target_pairs={{0,5},{1,4},{2,7},{3,6},{4,1},{5,0},{6,3},{7,2},{8,13},{9,12},{10,... | collective-permute-start | bytes 98312 | tf_op jit(solution)/shard_map/ppermute | solution.py:236
  59.5 4.5 %collective-permute-start.14 = (bf16[2,1,1,1,1,8,1,256]{7,5,0,6,4,3,2,1:T(8,128)(2,1)S(1)}, bf16[2,1,1,1,1,8,1,256]{7,5,0,6,4,3,2,1:T(8,128)(2,1)S(1)}, u32[]{:S(2)}, u32[]{:S(2)}) collective-permute-start(bf16[2,1,1,1,1,8,1,256]{7,5,0,6,4,3,2,1:T(8,128)(2,1)S(1)} %get-tuple-element.28), channel_id=1, source_target_pairs={{0,8},{1,9},{2,10},{3,11},{4,12},{5,13},{6,14},{7,15},{8,0},{9,1},... | collective-permute-start | bytes 24584 | tf_op jit(solution)/shard_map/ppermute | solution.py:236
  60.8 4.5 %collective-permute-start.15 = (bf16[2,1,1,1,1,8,1,256]{7,5,0,6,4,3,2,1:T(8,128)(2,1)S(1)}, bf16[2,1,1,1,1,8,1,256]{7,5,0,6,4,3,2,1:T(8,128)(2,1)S(1)}, u32[]{:S(2)}, u32[]{:S(2)}) collective-permute-start(bf16[2,1,1,1,1,8,1,256]{7,5,0,6,4,3,2,1:T(8,128)(2,1)S(1)} %get-tuple-element.30), channel_id=1, source_target_pairs={{0,16},{1,17},{2,18},{3,19},{4,20},{5,21},{6,22},{7,23},{8,24},{9,... | collective-permute-start | bytes 24584 | tf_op jit(solution)/shard_map/ppermute | solution.py:236
  62.3 5.4 %collective-permute-start.16 = (bf16[2,1,1,1,1,8,1,256]{7,5,0,6,4,3,2,1:T(8,128)(2,1)S(1)}, bf16[2,1,1,1,1,8,1,256]{7,5,0,6,4,3,2,1:T(8,128)(2,1)S(1)}, u32[]{:S(2)}, u32[]{:S(2)}) collective-permute-start(bf16[2,1,1,1,1,8,1,256]{7,5,0,6,4,3,2,1:T(8,128)(2,1)S(1)} %get-tuple-element.29), channel_id=1, source_target_pairs={{0,24},{1,25},{2,26},{3,27},{4,28},{5,29},{6,30},{7,31},{8,16},{9,... | collective-permute-start | bytes 24584 | tf_op jit(solution)/shard_map/ppermute | solution.py:236

commit v2 on v1

v2 whole, which is shorter than its diff:
```python
import functools

import jax
import jax.numpy as jnp
from jax import lax
from jax.experimental import pallas as pl
from jax.experimental.pallas import tpu as pltpu
from jax.sharding import PartitionSpec as P

ITERS = 2
AXES = ("gx", "gy", "gz")
F32 = jnp.float32
BF16 = jnp.bfloat16
CHUNKS = 5
VMEM_LIMIT = 40 * 1024 * 1024
OUT_VMEM = pltpu.VMEM


def swap_rounds(sizes):
    rounds = []
    for pos, size in enumerate(sizes):
        if size > 1:
            rounds.append((pos, 0))
        if size > 2:
            rounds.append((pos, 1))
    return rounds


def partner_of(sizes, pos, phase, here):
    there = list(here)
    near = here[pos] + (1 if (here[pos] + phase) % 2 == 0 else -1)
    if 0 <= near < sizes[pos]:
        there[pos] = near
    elif pos == 1 or sizes[1] % 2:
        there[pos] = sizes[pos] - 1 - here[pos]
    else:
        there[1] = here[1] ^ 1
    return there


def swap_pairs(sizes, pos, phase):
    pairs = []
    for at_x in range(sizes[0]):
        for at_y in range(sizes[1]):
            for at_z in range(sizes[2]):
                there = partner_of(sizes, pos, phase, (at_x, at_y, at_z))
                if there != [at_x, at_y, at_z]:
                    pairs.append(
                        ((at_x * sizes[1] + at_y) * sizes[2] + at_z, (there[0] * sizes[1] + there[1]) * sizes[2] + there[2])
                    )
    return pairs


def has_neighbour(sizes, where, pos, phase):
    near = where[pos] + 1 - 2 * ((where[pos] + phase) & 1)
    return jnp.logical_and(near >= 0, near < sizes[pos])


def face_id(where, pos, phase):
    return 2 * pos + 1 - ((where[pos] + phase) & 1)


def join(left, right):
    return jnp.concatenate([left, right], axis=1)


def blocks(total):
    return [pl.ds(pos * (total // CHUNKS), total // CHUNKS) for pos in range(CHUNKS)]


def respond(response, straight, crossed, outgoing, part):
    outgoing[part, :] = (
        jnp.dot(response[0, part, :], straight[...], preferred_element_type=F32)
        + jnp.dot(response[1, part, :], crossed[...], preferred_element_type=F32)
    ).astype(BF16)


def pick_faces(picks, outgoing, outs):
    face = outs[0].shape[0]
    chosen = jnp.dot(picks[...], outgoing[...], preferred_element_type=F32).astype(BF16)
    for pos, out in enumerate(outs):
        out[...] = chosen[pos * face : (pos + 1) * face]


def add_traces(puts, arrived, source, values, part):
    traces = jnp.dot(puts[part, :], values[...], preferred_element_type=F32)
    return (traces + source[part, :].astype(F32)).astype(BF16)


def gather_values(arrived, values):
    face = arrived[0].shape[0]
    for pos, faces in enumerate(arrived):
        values[pl.ds(pos * face, face), :] = faces[...]


def turned(both):
    columns = both.shape[1] // 2
    return join(-both[:, columns:], both[:, :columns])


def first_kernel(sizes, rounds, linked_hbm, slots_hbm, source_hbm, response_hbm, *refs):
    count = len(rounds)
    outs = refs[:count]
    response, source, puts, picks = refs[count : count + 4]
    linked, slots, parts, crossed, outgoing, sems = refs[count + 4 :]
    unknowns, face = response.shape[1], slots.shape[2]
    small = [
        pltpu.make_async_copy(linked_hbm, linked, sems.at[0]),
        pltpu.make_async_copy(slots_hbm, slots, sems.at[1]),
        pltpu.make_async_copy(source_hbm, parts, sems.at[2]),
    ]
    large = [
        pltpu.make_async_copy(response_hbm.at[:, part, :], response.at[:, part, :], sems.at[3 + pos])
        for pos, part in enumerate(blocks(unknowns))
    ]
    for copy in small + large:
        copy.start()
    for copy in small:
        copy.wait()
    where = [lax.axis_index(axis) for axis in AXES]
    ids = [face_id(where, pos, phase) for pos, phase in rounds]
    rows = [slots[face_pos] for face_pos in ids]
    source[...] = join(parts[0], parts[1])
    crossed[...] = turned(source)
    upright = jnp.transpose(jnp.concatenate(rows + [rows[0]] * (-count % 8), axis=0))
    gates = [
        jnp.logical_and(linked[face_pos] != 0, has_neighbour(sizes, where, pos, phase))
        for face_pos, (pos, phase) in zip(ids, rounds)
    ]
    accepted = jnp.concatenate([jnp.where(gate, row, -1) for gate, row in zip(gates, rows)], axis=1)
    across = lax.broadcasted_iota(jnp.int32, (face, unknowns), 1)
    parts_of = blocks(unknowns)
    for step in range(max(count, CHUNKS)):
        if step < count:
            chosen = jnp.where(across == upright[:, step : step + 1], 1.0, 0.0)
            picks[pl.ds(step * face, face), :] = chosen.astype(BF16)
        if step < CHUNKS:
            part = parts_of[step]
            down = part.start + lax.broadcasted_iota(jnp.int32, (part.size, count * face), 0)
            puts[part, :] = jnp.where(down == accepted, 1.0, 0.0).astype(BF16)
            large[step].wait()
            respond(response, source, crossed, outgoing, part)
    pick_faces(picks, outgoing, outs)


def sweep_kernel(count, response, source, puts, picks, *refs):
    arrived, outs = refs[:count], refs[count : 2 * count]
    values, straight, crossed, outgoing = refs[2 * count :]
    gather_values(arrived, values)
    for part in blocks(source.shape[0]):
        both = add_traces(puts, arrived, source, values, part)
        straight[part, :] = both
        crossed[part, :] = turned(both)
    for part in blocks(source.shape[0]):
        respond(response, straight, crossed, outgoing, part)
    pick_faces(picks, outgoing, outs)


def radiate_kernel(count, halves, eb, source, puts, radiation, *refs):
    arrived, outs = refs[:count], refs[count : count + 1 + halves]
    values, straight, crossed = refs[count + 1 + halves :]
    columns = source.shape[1] // 2
    gather_values(arrived, values)
    for part in blocks(source.shape[0]):
        both = add_traces(puts, arrived, source, values, part)
        straight[part, :] = both
        crossed[part, :] = turned(both)
    field = jnp.dot(radiation[0], straight[...], preferred_element_type=F32) + jnp.dot(
        radiation[1], crossed[...], preferred_element_type=F32
    )
    mine = lax.axis_index("gy") & 1
    for part in range(2):
        flat = jnp.transpose(field[:, part * columns : (part + 1) * columns])
        if not halves:
            outs[0][part] = flat
            continue
        split = [
            jnp.concatenate([flat[low : low + eb] for low in range(half * eb, columns, 2 * eb)], axis=0)
            for half in range(2)
        ]
        outs[0][part] = jnp.where(mine == 0, split[0], split[1])
        outs[1][part] = jnp.where(mine == 0, split[1], split[0])


def hbm_spec():
    return pl.BlockSpec(memory_space=pl.ANY)


def vmem_spec():
    return pl.BlockSpec(memory_space=pltpu.VMEM)


def in_hbm(value):
    return pltpu.with_memory_space_constraint(value, pltpu.HBM)


def in_vmem(value):
    return pltpu.with_memory_space_constraint(value, pltpu.VMEM)


def params():
    return pltpu.CompilerParams(vmem_limit_bytes=VMEM_LIMIT)


def first_sweep(sizes, rounds, linked, slots, source, response):
    unknowns, columns = source.shape[1:]
    face, count = slots.shape[2], len(rounds)
    kept = [
        (response.shape, BF16),
        ((unknowns, 2 * columns), BF16),
        ((unknowns, count * face), BF16),
        ((count * face, unknowns), BF16),
    ]
    outs = pl.pallas_call(
        functools.partial(first_kernel, sizes, rounds),
        out_shape=[jax.ShapeDtypeStruct((face, 2 * columns), BF16)] * count
        + [OUT_VMEM(shape, kind) for shape, kind in kept],
        in_specs=[hbm_spec()] * 4,
        out_specs=[vmem_spec()] * (count + len(kept)),
        scratch_shapes=[
            pltpu.SMEM(linked.shape, linked.dtype),
            pltpu.VMEM(slots.shape, slots.dtype),
            pltpu.VMEM(source.shape, BF16),
            pltpu.VMEM((unknowns, 2 * columns), BF16),
            pltpu.VMEM((unknowns, 2 * columns), BF16),
            pltpu.SemaphoreType.DMA((3 + CHUNKS,)),
        ],
        compiler_params=params(),
    )(in_hbm(linked), in_hbm(slots), in_hbm(source), in_hbm(response))
    return outs[:count], outs[count:]


def later_sweep(kept, arrived):
    response, source, puts, picks = kept
    count = len(arrived)
    return pl.pallas_call(
        functools.partial(sweep_kernel, count),
        out_shape=[jax.ShapeDtypeStruct(arrived[0].shape, BF16)] * count,
        in_specs=[vmem_spec()] * (4 + count),
        out_specs=[vmem_spec()] * count,
        scratch_shapes=[pltpu.VMEM((picks.shape[0], source.shape[1]), BF16)]
        + [pltpu.VMEM(source.shape, BF16)] * 3,
        compiler_params=params(),
    )(response, source, puts, picks, *arrived)


def radiate(kept, radiation, arrived, halves, eb):
    source, puts, picks = kept[1:]
    columns = source.shape[1] // 2
    angles = radiation.shape[1]
    count = len(arrived)
    shape = (2, columns // 2 if halves else columns, angles)
    outs = [jax.ShapeDtypeStruct(shape, F32)] * (1 + int(halves))
    return pl.pallas_call(
        functools.partial(radiate_kernel, count, int(halves), eb),
        out_shape=outs,
        in_specs=[vmem_spec()] * (3 + count),
        out_specs=[vmem_spec()] * len(outs),
        scratch_shapes=[pltpu.VMEM((picks.shape[0], source.shape[1]), BF16)]
        + [pltpu.VMEM(source.shape, BF16)] * 2,
        compiler_params=params(),
    )(source, puts, radiation, *arrived)


def bit_count(size):
    return size.bit_length() - 1


def mask_pairs(sizes, flips):
    pairs = []
    for at_x in range(sizes[0]):
        for at_y in range(sizes[1]):
            for at_z in range(sizes[2]):
                here = (at_x * sizes[1] + at_y) * sizes[2] + at_z
                there = ((at_x ^ flips[0]) * sizes[1] + (at_y ^ flips[1])) * sizes[2] + (at_z ^ flips[2])
                pairs.append((here, there))
    return pairs


def scatter_sum(parts, sizes, where, full):
    columns, angles = full
    bits = [bit_count(size) for size in sizes]
    halves = len(parts) > 1
    dims = {}
    shape = [2]
    for pos in (0, 1):
        for bit in reversed(range(bits[pos])):
            if halves and (pos, bit) == (1, 0):
                continue
            dims[(pos, bit)] = len(shape)
            shape.append(2)
    shape.append(columns // (sizes[0] * sizes[1]))
    for bit in reversed(range(bits[2])):
        dims[(2, bit)] = len(shape)
        shape.append(2)
    shape.append(angles // sizes[2])
    total = parts[0]
    if halves:
        total = total + lax.ppermute(parts[1], AXES, mask_pairs(sizes, (0, 1, 0)))
    total = total.reshape(shape)
    rest = [item for item in dims if item[0] != 0]
    rest = sorted(rest, key=lambda item: (item[1], item[0])) + sorted(item for item in dims if item[0] == 0)
    rounds = [rest[pos : pos + 2] for pos in range(0, len(rest), 2)]
    for order, group in enumerate(rounds):
        wide = order == len(rounds) - 1

        def taken(code):
            piece = total
            for place, (pos, bit) in enumerate(group):
                mine = (where[pos] >> bit) & 1
                piece = lax.dynamic_slice_in_dim(piece, mine ^ ((code >> place) & 1), 1, axis=dims[(pos, bit)])
            return piece

        got = []
        for code in range(1, 2 ** len(group)):
            flips = [0, 0, 0]
            for place, (pos, bit) in enumerate(group):
                flips[pos] |= ((code >> place) & 1) << bit
            piece = taken(code) if wide else taken(code).astype(BF16)
            got.append(lax.ppermute(piece, AXES, mask_pairs(sizes, flips)))
        total = taken(0)
        for piece in got:
            total = total + piece.astype(F32)
    return total.reshape(2, columns // (sizes[0] * sizes[1]), angles // sizes[2])


def shards(sizes, incident, response, radiation, face_index, linked):
    source = incident[0, 0, 0]
    response_mat = response[0, 0, 0]
    radiation_mat = radiation[0, 0, 0]
    slots = face_index[0, 0, 0][:, None, :]
    where = [lax.axis_index(axis) for axis in AXES]
    rounds = swap_rounds(sizes)
    columns, angles = source.shape[2], radiation_mat.shape[1]
    faces, kept = first_sweep(sizes, rounds, linked[0, 0, 0], slots, source, response_mat)
    for turn in range(ITERS):
        arrived = [
            lax.ppermute(face, AXES, swap_pairs(sizes, pos, phase))
            for face, (pos, phase) in zip(faces, rounds)
        ]
        if turn < ITERS - 1:
            faces = later_sweep(kept, arrived)
    halves = sizes[1] % 2 == 0
    parts = radiate(kept, radiation_mat, arrived, halves, columns // (sizes[0] * sizes[1]))
    return scatter_sum(parts, sizes, where, (columns, angles))


def solution(mesh):
    sizes = tuple(mesh.shape[axis] for axis in AXES)
    return jax.shard_map(
        functools.partial(shards, sizes),
        mesh=mesh,
        in_specs=(
            P("gx", "gy", "gz", None, None, None),
            P("gx", "gy", "gz", None, None, None),
            P("gx", "gy", "gz", None, None, None),
            P("gx", "gy", "gz", None, None),
            P("gx", "gy", "gz", None),
        ),
        out_specs=P(None, ("gx", "gy"), "gz"),
        check_vma=False,
    )
```

time: 68.8 us -> 47.7 us (0.69)
  Pallas kernels: 19.7 us -> 11.7 us
  local copies, waits for them, and re-layouts: 6.27 us -> 0.06 us
  starting transfers between devices: 25.1 us -> 19.1 us
  other arithmetic: 1.61 us -> 0.67 us
    pallas_call x3, Pallas kernels: 19.7 us -> 11.7 us  [the longest x1 6.46 us: first_sweep(): pl.pallas_call(functools.partial(first_kernel, sizes, rounds), out_shape=...]
    unnamed x16 -> x5, local copies, waits for them, and re-layouts: 6.12 us -> 0.01 us
    ppermute x17, starting transfers between devices: 25.1 us -> 19.1 us  [the longest x10 11 us: shards(): lax.ppermute(face, AXES, swap_pairs(sizes, pos, phase))]
    add x2 -> x1, other arithmetic: 0.99 us -> 0.02 us  [scatter_sum(): total = total + piece.astype(F32)]
  transfers between devices with their start and end apart: 17 -> 17, of which waited for: 8 -> 11; matrix products, arithmetic and copies ran while one was open for 0% -> 0% of each run, Pallas kernels for 0% -> 0%
where the time goes in v2:
time: 47.7 us; the launch traced here: 47.6 us
  starting transfers between devices  19.1 us (40%)
  waiting for transfers between devices  15.9 us (33%)
  Pallas kernels  11.7 us (25%)
  other arithmetic  0.67 us (1%)
    ppermute x10, starting transfers between devices, shards(): lax.ppermute(face, AXES, swap_pairs(sizes, pos, phase))  11 us
    ppermute x6, starting transfers between devices, scatter_sum(): got.append(lax.ppermute(piece, AXES, mask_pairs(sizes, flips)))  8.01 us
    ppermute x10, waiting for transfers between devices, shards(): lax.ppermute(face, AXES, swap_pairs(sizes, pos, phase))  7.43 us
    ppermute x6, waiting for transfers between devices, scatter_sum(): got.append(lax.ppermute(piece, AXES, mask_pairs(sizes, flips)))  6.95 us
    pallas_call x1, Pallas kernels, first_sweep(): pl.pallas_call(functools.partial(first_kernel, sizes, rounds), out_shape=...  6.46 us
    pallas_call x1, Pallas kernels, later_sweep(): pl.pallas_call(functools.partial(sweep_kernel, count), out_shape=[jax.Sha...  3.29 us
    pallas_call x1, Pallas kernels, radiate(): pl.pallas_call(functools.partial(radiate_kernel, count, int(halves), eb),...  1.99 us
    ppermute x1, waiting for transfers between devices, scatter_sum(): total = total + lax.ppermute(parts[1], AXES, mask_pairs(sizes, (0, 1, 0)))  1.49 us
  transfers between devices with their start and end apart: 17, of which 11 were waited for; matrix products, arithmetic and copies ran while one was open for 0% of the time, Pallas kernels for 0%

profile of v2, /device:TPU:0, one launch (start us, length us, event | category | flops | bytes accessed | tf_op | source)
XLA Modules:
  0.0 47.6 jit_solution(11125548695687525034)
XLA Ops:
  0.0 6.5 %shard_map.55 = (bf16[192,256]{1,0:T(8,128)(2,1)S(1)}, bf16[192,256]{1,0:T(8,128)(2,1)S(1)}, bf16[192,256]{1,0:T(8,128)(2,1)S(1)}, bf16[192,256]{1,0:T(8,128)(2,...) custom-call(s32[6]{0:T(128)} %bitcast.14, ...), custom_call_target="tpu_custom_call" | custom-call | tf_op jit(solution)/shard_map/pallas_call | solution.py:214
  6.5 3.1 %collective-permute-start = (bf16[192,256]{1,0:T(8,128)(2,1)S(1)}, bf16[192,256]{1,0:T(8,128)(2,1)S(1)}, u32[]{:S(2)}, u32[]{:S(2)}) collective-permute-start(bf16[192,256]{1,0:T(8,128)(2,1)S(1)} %get-tuple-element.25), channel_id=1, source_target_pairs={{0,8},{1,9},{2,10},{3,11},{4,12},{5,13},{6,14},{7,15},{8,0},{9,1},... | collective-permute-start | bytes 294920 | tf_op jit(solution)/shard_map/ppermute | solution.py:338
  9.6 0.5 %collective-permute-start.2 = (bf16[192,256]{1,0:T(8,128)(2,1)S(1)}, bf16[192,256]{1,0:T(8,128)(2,1)S(1)}, u32[]{:S(2)}, u32[]{:S(2)}) collective-permute-start(bf16[192,256]{1,0:T(8,128)(2,1)S(1)} %get-tuple-element.27), channel_id=1, source_target_pairs={{0,2},{1,3},{2,0},{3,1},{4,6},{5,7},{6,4},{7,5},{8,10},{9,11},{10,... | collective-permute-start | bytes 294920 | tf_op jit(solution)/shard_map/ppermute | solution.py:338
  10.1 1.1 %collective-permute-start.3 = (bf16[192,256]{1,0:T(8,128)(2,1)S(1)}, bf16[192,256]{1,0:T(8,128)(2,1)S(1)}, u32[]{:S(2)}, u32[]{:S(2)}) collective-permute-start(bf16[192,256]{1,0:T(8,128)(2,1)S(1)} %get-tuple-element.28), channel_id=1, source_target_pairs={{0,6},{1,7},{2,4},{3,5},{4,2},{5,3},{6,0},{7,1},{8,14},{9,15},{10,... | collective-permute-start | bytes 294920 | tf_op jit(solution)/shard_map/ppermute | solution.py:338
  11.2 1.5 %collective-permute-start.4 = (bf16[192,256]{1,0:T(8,128)(2,1)S(1)}, bf16[192,256]{1,0:T(8,128)(2,1)S(1)}, u32[]{:S(2)}, u32[]{:S(2)}) collective-permute-start(bf16[192,256]{1,0:T(8,128)(2,1)S(1)} %get-tuple-element.29), channel_id=1, source_target_pairs={{0,1},{1,0},{2,3},{3,2},{4,5},{5,4},{6,7},{7,6},{8,9},{9,8},{10,11... | collective-permute-start | bytes 294920 | tf_op jit(solution)/shard_map/ppermute | solution.py:338
  12.7 2.3 %collective-permute-done.3.refs_3_ = bf16[192,256]{1,0:T(8,128)(2,1)S(1)} collective-permute-done((bf16[192,256]{1,0:T(8,128)(2,1)S(1)}, bf16[192,256]{1,0:T(8,128)(2,1)S(1)}, u32[]{:S(2)}, u32[]{:S(2)}) %collective-permute-start.3) | collective-permute-done | bytes 98336 | tf_op jit(solution)/shard_map/ppermute | solution.py:338
  15.0 1.4 %collective-permute-done.4.refs_4_ = bf16[192,256]{1,0:T(8,128)(2,1)S(1)} collective-permute-done((bf16[192,256]{1,0:T(8,128)(2,1)S(1)}, bf16[192,256]{1,0:T(8,128)(2,1)S(1)}, u32[]{:S(2)}, u32[]{:S(2)}) %collective-permute-start.4) | collective-permute-done | bytes 98336 | tf_op jit(solution)/shard_map/ppermute | solution.py:338
  16.4 3.3 %shard_map.56 = (bf16[192,256]{1,0:T(8,128)(2,1)S(1)}, bf16[192,256]{1,0:T(8,128)(2,1)S(1)}, bf16[192,256]{1,0:T(8,128)(2,1)S(1)}, bf16[192,256]{1,0:T(8,128)(2,1)S(1)}, bf16[192,256]{1,0:T(8,128)(2,1)S(1)}) custom-call(bf16[2,1280,1280]{2,1,0:T(8,128)(2,1)S(1)} %get-tuple-element.23.response, bf16[1280,256]{1,0:T(8,128)(2,1)S(1)} %get-tuple-element.21.source, ...), custom_call_target="tpu_custom_call" | custom-call | tf_op jit(solution)/shard_map/pallas_call | solution.py:236
  19.7 2.7 %collective-permute-start.5 = (bf16[192,256]{1,0:T(8,128)(2,1)S(1)}, bf16[192,256]{1,0:T(8,128)(2,1)S(1)}, u32[]{:S(2)}, u32[]{:S(2)}) collective-permute-start(bf16[192,256]{1,0:T(8,128)(2,1)S(1)} %get-tuple-element.30), channel_id=1, source_target_pairs={{0,8},{1,9},{2,10},{3,11},{4,12},{5,13},{6,14},{7,15},{8,0},{9,1},... | collective-permute-start | bytes 294920 | tf_op jit(solution)/shard_map/ppermute | solution.py:338
  22.4 0.5 %collective-permute-start.7 = (bf16[192,256]{1,0:T(8,128)(2,1)S(1)}, bf16[192,256]{1,0:T(8,128)(2,1)S(1)}, u32[]{:S(2)}, u32[]{:S(2)}) collective-permute-start(bf16[192,256]{1,0:T(8,128)(2,1)S(1)} %get-tuple-element.32), channel_id=1, source_target_pairs={{0,2},{1,3},{2,0},{3,1},{4,6},{5,7},{6,4},{7,5},{8,10},{9,11},{10,... | collective-permute-start | bytes 294920 | tf_op jit(solution)/shard_map/ppermute | solution.py:338
  23.0 1.5 %collective-permute-start.9 = (bf16[192,256]{1,0:T(8,128)(2,1)S(1)}, bf16[192,256]{1,0:T(8,128)(2,1)S(1)}, u32[]{:S(2)}, u32[]{:S(2)}) collective-permute-start(bf16[192,256]{1,0:T(8,128)(2,1)S(1)} %get-tuple-element.34), channel_id=1, source_target_pairs={{0,1},{1,0},{2,3},{3,2},{4,5},{5,4},{6,7},{7,6},{8,9},{9,8},{10,11... | collective-permute-start | bytes 294920 | tf_op jit(solution)/shard_map/ppermute | solution.py:338
  25.0 2.8 %collective-permute-done.8.refs_3_ = bf16[192,256]{1,0:T(8,128)(2,1)S(1)} collective-permute-done((bf16[192,256]{1,0:T(8,128)(2,1)S(1)}, bf16[192,256]{1,0:T(8,128)(2,1)S(1)}, u32[]{:S(2)}, u32[]{:S(2)}) %collective-permute-start.8) | collective-permute-done | bytes 98336 | tf_op jit(solution)/shard_map/ppermute | solution.py:338
  28.3 2.0 %shard_map.57 = (f32[2,64,512]{2,1,0:T(8,128)S(1)}, f32[2,64,512]{2,1,0:T(8,128)S(1)}) custom-call(bf16[1280,256]{1,0:T(8,128)(2,1)S(1)} %get-tuple-element.21.source, bf16[1280,960]{1,0:T(8,128)(2,1)S(1)} %get-tuple-element.22.puts, bf16[2,512,1280]{2,1,0:T(8,128)(2,1)S(1)} %bitcast.8, bf16[192,256]{1,0:T(8,128)(2,1)S(1)} %collective-permute-done.5.refs_0_, ...), custom_call_target="tpu_custom_call" | custom-call | tf_op jit(solution)/shard_map/pallas_call | solution.py:254
  30.4 1.5 %collective-permute-done.10 = f32[2,64,512]{2,1,0:T(8,128)S(1)} collective-permute-done((f32[2,64,512]{2,1,0:T(8,128)S(1)}, f32[2,64,512]{2,1,0:T(8,128)S(1)}, u32[]{:S(2)}, u32[]{:S(2)}) %collective-permute-start.10) | collective-permute-done | bytes 262176 | tf_op jit(solution)/shard_map/ppermute | solution.py:299
  31.9 1.6 %collective-permute-start.11 = (bf16[2,2,2,1,8,1,256]{6,4,0,5,3,2,1:T(8,128)(2,1)S(1)}, bf16[2,2,2,1,8,1,256]{6,4,0,5,3,2,1:T(8,128)(2,1)S(1)}, u32[]{:S(2)}, u32[]{:S(2)}) collective-permute-start(bf16[2,2,2,1,8,1,256]{6,4,0,5,3,2,1:T(8,128)(2,1)S(1)} %copy.24), channel_id=1, source_target_pairs={{0,1},{1,0},{2,3},{3,2},{4,5},{5,4},{6,7},{7,6},{8,9},{9,8},{10,11... | collective-permute-start | bytes 98312 | tf_op jit(solution)/shard_map/ppermute | solution.py:320
  33.5 1.5 %collective-permute-start.12 = (bf16[2,2,2,1,8,1,256]{6,4,0,5,3,2,1:T(8,128)(2,1)S(1)}, bf16[2,2,2,1,8,1,256]{6,4,0,5,3,2,1:T(8,128)(2,1)S(1)}, u32[]{:S(2)}, u32[]{:S(2)}) collective-permute-start(bf16[2,2,2,1,8,1,256]{6,4,0,5,3,2,1:T(8,128)(2,1)S(1)} %copy.23), channel_id=1, source_target_pairs={{0,4},{1,5},{2,6},{3,7},{4,0},{5,1},{6,2},{7,3},{8,12},{9,13},{10,... | collective-permute-start | bytes 98312 | tf_op jit(solution)/shard_map/ppermute | solution.py:320
  35.9 1.5 %collective-permute-done.12 = bf16[2,2,2,1,8,1,256]{6,4,0,5,3,2,1:T(8,128)(2,1)S(1)} collective-permute-done((bf16[2,2,2,1,8,1,256]{6,4,0,5,3,2,1:T(8,128)(2,1)S(1)}, bf16[2,2,2,1,8,1,256]{6,4,0,5,3,2,1:T(8,128)(2,1)S(1)}, u32[]{:S(2)}, u32[]{:S(2)}) %collective-permute-start.12) | collective-permute-done | bytes 32800 | tf_op jit(solution)/shard_map/ppermute | solution.py:320
  37.4 2.4 %collective-permute-done.13 = bf16[2,2,2,1,8,1,256]{6,4,0,5,3,2,1:T(8,128)(2,1)S(1)} collective-permute-done((bf16[2,2,2,1,8,1,256]{6,4,0,5,3,2,1:T(8,128)(2,1)S(1)}, bf16[2,2,2,1,8,1,256]{6,4,0,5,3,2,1:T(8,128)(2,1)S(1)}, u32[]{:S(2)}, u32[]{:S(2)}) %collective-permute-start.13) | collective-permute-done | bytes 32800 | tf_op jit(solution)/shard_map/ppermute | solution.py:320
  39.9 0.5 %collective-permute-start.14 = (f32[2,1,1,1,8,1,256]{6,4,0,5,3,2,1:T(8,128)S(1)}, f32[2,1,1,1,8,1,256]{6,4,0,5,3,2,1:T(8,128)S(1)}, u32[]{:S(2)}, u32[]{:S(2)}) collective-permute-start(f32[2,1,1,1,8,1,256]{6,4,0,5,3,2,1:T(8,128)S(1)} %get-tuple-element.40), channel_id=1, source_target_pairs={{0,8},{1,9},{2,10},{3,11},{4,12},{5,13},{6,14},{7,15},{8,0},{9,1},... | collective-permute-start | bytes 49160 | tf_op jit(solution)/shard_map/ppermute | solution.py:320
  40.4 1.0 %collective-permute-start.15 = (f32[2,1,1,1,8,1,256]{6,4,0,5,3,2,1:T(8,128)S(1)}, f32[2,1,1,1,8,1,256]{6,4,0,5,3,2,1:T(8,128)S(1)}, u32[]{:S(2)}, u32[]{:S(2)}) collective-permute-start(f32[2,1,1,1,8,1,256]{6,4,0,5,3,2,1:T(8,128)S(1)} %get-tuple-element.42), channel_id=1, source_target_pairs={{0,16},{1,17},{2,18},{3,19},{4,20},{5,21},{6,22},{7,23},{8,24},{9,... | collective-permute-start | bytes 49160 | tf_op jit(solution)/shard_map/ppermute | solution.py:320
  41.4 2.9 %collective-permute-start.16 = (f32[2,1,1,1,8,1,256]{6,4,0,5,3,2,1:T(8,128)S(1)}, f32[2,1,1,1,8,1,256]{6,4,0,5,3,2,1:T(8,128)S(1)}, u32[]{:S(2)}, u32[]{:S(2)}) collective-permute-start(f32[2,1,1,1,8,1,256]{6,4,0,5,3,2,1:T(8,128)S(1)} %get-tuple-element.41), channel_id=1, source_target_pairs={{0,24},{1,25},{2,26},{3,27},{4,28},{5,29},{6,30},{7,31},{8,16},{9,... | collective-permute-start | bytes 49160 | tf_op jit(solution)/shard_map/ppermute | solution.py:320
  44.3 0.7 %collective-permute-done.15 = f32[2,1,1,1,8,1,256]{6,4,0,5,3,2,1:T(8,128)S(1)} collective-permute-done((f32[2,1,1,1,8,1,256]{6,4,0,5,3,2,1:T(8,128)S(1)}, f32[2,1,1,1,8,1,256]{6,4,0,5,3,2,1:T(8,128)S(1)}, u32[]{:S(2)}, u32[]{:S(2)}) %collective-permute-start.15) | collective-permute-done | bytes 16416 | tf_op jit(solution)/shard_map/ppermute | solution.py:320
  45.0 1.9 %collective-permute-done.16 = f32[2,1,1,1,8,1,256]{6,4,0,5,3,2,1:T(8,128)S(1)} collective-permute-done((f32[2,1,1,1,8,1,256]{6,4,0,5,3,2,1:T(8,128)S(1)}, f32[2,1,1,1,8,1,256]{6,4,0,5,3,2,1:T(8,128)S(1)}, u32[]{:S(2)}, u32[]{:S(2)}) %collective-permute-start.16) | collective-permute-done | bytes 16416 | tf_op jit(solution)/shard_map/ppermute | solution.py:320
  47.0 0.6 %add_bitcast_fusion = f32[2,8,256]{2,1,0:T(8,128)} fusion(f32[2,1,1,1,8,1,256]{6,4,0,5,3,2,1:T(8,128)S(1)} %collective-permute-done.16, f32[2,1,1,1,8,1,256]{6,4,0,5,3,2,1:T(8,128)S(1)} %collective-permute-done.15, f32[2,1,1,1,8,1,256]{6,4,0,5,3,2,1:T(8,128)S(1)} %collective-permute-done.14, f32[2,2,2,1,8,1,256]{6,4,0,5,3,2,1:T(8,128)S(1)} %fusion.1, ...), kind=kLoop, calls=%fused_computation.6 | loop fusion | flops 12288 | bytes 81928 | tf_op jit(solution)/shard_map/reshape | solution.py:324
  (23 shorter events, 2.1 us)
Async XLA Ops:
  6.5 6.2 %collective-permute-start = (bf16[192,256]{1,0:T(8,128)(2,1)S(1)}, bf16[192,256]{1,0:T(8,128)(2,1)S(1)}, u32[]{:S(2)}, u32[]{:S(2)}) collective-permute-start(bf16[192,256]{1,0:T(8,128)(2,1)S(1)} %get-tuple-element.25), channel_id=1, source_target_pairs={{0,8},{1,9},{2,10},{3,11},{4,12},{5,13},{6,14},{7,15},{8,0},{9,1},... | collective-permute-start | bytes 294920 | tf_op jit(solution)/shard_map/ppermute | solution.py:338
  9.6 3.1 %collective-permute-start.1 = (bf16[192,256]{1,0:T(8,128)(2,1)S(1)}, bf16[192,256]{1,0:T(8,128)(2,1)S(1)}, u32[]{:S(2)}, u32[]{:S(2)}) collective-permute-start(bf16[192,256]{1,0:T(8,128)(2,1)S(1)} %get-tuple-element.26), channel_id=1, source_target_pairs={{0,2},{1,3},{2,0},{3,1},{4,6},{5,7},{6,4},{7,5},{8,16},{9,17},{10,... | collective-permute-start | bytes 294920 | tf_op jit(solution)/shard_map/ppermute | solution.py:338
  9.6 3.1 %collective-permute-start.2 = (bf16[192,256]{1,0:T(8,128)(2,1)S(1)}, bf16[192,256]{1,0:T(8,128)(2,1)S(1)}, u32[]{:S(2)}, u32[]{:S(2)}) collective-permute-start(bf16[192,256]{1,0:T(8,128)(2,1)S(1)} %get-tuple-element.27), channel_id=1, source_target_pairs={{0,2},{1,3},{2,0},{3,1},{4,6},{5,7},{6,4},{7,5},{8,10},{9,11},{10,... | collective-permute-start | bytes 294920 | tf_op jit(solution)/shard_map/ppermute | solution.py:338
  10.1 4.9 %collective-permute-start.3 = (bf16[192,256]{1,0:T(8,128)(2,1)S(1)}, bf16[192,256]{1,0:T(8,128)(2,1)S(1)}, u32[]{:S(2)}, u32[]{:S(2)}) collective-permute-start(bf16[192,256]{1,0:T(8,128)(2,1)S(1)} %get-tuple-element.28), channel_id=1, source_target_pairs={{0,6},{1,7},{2,4},{3,5},{4,2},{5,3},{6,0},{7,1},{8,14},{9,15},{10,... | collective-permute-start | bytes 294920 | tf_op jit(solution)/shard_map/ppermute | solution.py:338
  11.2 5.2 %collective-permute-start.4 = (bf16[192,256]{1,0:T(8,128)(2,1)S(1)}, bf16[192,256]{1,0:T(8,128)(2,1)S(1)}, u32[]{:S(2)}, u32[]{:S(2)}) collective-permute-start(bf16[192,256]{1,0:T(8,128)(2,1)S(1)} %get-tuple-element.29), channel_id=1, source_target_pairs={{0,1},{1,0},{2,3},{3,2},{4,5},{5,4},{6,7},{7,6},{8,9},{9,8},{10,11... | collective-permute-start | bytes 294920 | tf_op jit(solution)/shard_map/ppermute | solution.py:338
  16.4 11.8 %copy-start = (bf16[1,1,1,2,512,1280]{5,4,3,2,1,0:T(8,128)(2,1)S(1)}, bf16[1,1,1,2,512,1280]{5,4,3,2,1,0:T(8,128)(2,1)}, u32[]{:S(2)}) copy-start(bf16[1,1,1,2,512,1280]{5,4,3,2,1,0:T(8,128)(2,1)} %param.7) | copy-start | bytes 7864324
  19.7 5.3 %collective-permute-start.5 = (bf16[192,256]{1,0:T(8,128)(2,1)S(1)}, bf16[192,256]{1,0:T(8,128)(2,1)S(1)}, u32[]{:S(2)}, u32[]{:S(2)}) collective-permute-start(bf16[192,256]{1,0:T(8,128)(2,1)S(1)} %get-tuple-element.30), channel_id=1, source_target_pairs={{0,8},{1,9},{2,10},{3,11},{4,12},{5,13},{6,14},{7,15},{8,0},{9,1},... | collective-permute-start | bytes 294920 | tf_op jit(solution)/shard_map/ppermute | solution.py:338
  22.4 2.6 %collective-permute-start.6 = (bf16[192,256]{1,0:T(8,128)(2,1)S(1)}, bf16[192,256]{1,0:T(8,128)(2,1)S(1)}, u32[]{:S(2)}, u32[]{:S(2)}) collective-permute-start(bf16[192,256]{1,0:T(8,128)(2,1)S(1)} %get-tuple-element.31), channel_id=1, source_target_pairs={{0,2},{1,3},{2,0},{3,1},{4,6},{5,7},{6,4},{7,5},{8,16},{9,17},{10,... | collective-permute-start | bytes 294920 | tf_op jit(solution)/shard_map/ppermute | solution.py:338
  22.4 2.6 %collective-permute-start.7 = (bf16[192,256]{1,0:T(8,128)(2,1)S(1)}, bf16[192,256]{1,0:T(8,128)(2,1)S(1)}, u32[]{:S(2)}, u32[]{:S(2)}) collective-permute-start(bf16[192,256]{1,0:T(8,128)(2,1)S(1)} %get-tuple-element.32), channel_id=1, source_target_pairs={{0,2},{1,3},{2,0},{3,1},{4,6},{5,7},{6,4},{7,5},{8,10},{9,11},{10,... | collective-permute-start | bytes 294920 | tf_op jit(solution)/shard_map/ppermute | solution.py:338
  22.9 4.9 %collective-permute-start.8 = (bf16[192,256]{1,0:T(8,128)(2,1)S(1)}, bf16[192,256]{1,0:T(8,128)(2,1)S(1)}, u32[]{:S(2)}, u32[]{:S(2)}) collective-permute-start(bf16[192,256]{1,0:T(8,128)(2,1)S(1)} %get-tuple-element.33), channel_id=1, source_target_pairs={{0,6},{1,7},{2,4},{3,5},{4,2},{5,3},{6,0},{7,1},{8,14},{9,15},{10,... | collective-permute-start | bytes 294920 | tf_op jit(solution)/shard_map/ppermute | solution.py:338
  23.0 5.2 %collective-permute-start.9 = (bf16[192,256]{1,0:T(8,128)(2,1)S(1)}, bf16[192,256]{1,0:T(8,128)(2,1)S(1)}, u32[]{:S(2)}, u32[]{:S(2)}) collective-permute-start(bf16[192,256]{1,0:T(8,128)(2,1)S(1)} %get-tuple-element.34), channel_id=1, source_target_pairs={{0,1},{1,0},{2,3},{3,2},{4,5},{5,4},{6,7},{7,6},{8,9},{9,8},{10,11... | collective-permute-start | bytes 294920 | tf_op jit(solution)/shard_map/ppermute | solution.py:338
  30.3 1.6 %collective-permute-start.10 = (f32[2,64,512]{2,1,0:T(8,128)S(1)}, f32[2,64,512]{2,1,0:T(8,128)S(1)}, u32[]{:S(2)}, u32[]{:S(2)}) collective-permute-start(f32[2,64,512]{2,1,0:T(8,128)S(1)} %get-tuple-element.36), channel_id=1, source_target_pairs={{0,2},{1,3},{2,0},{3,1},{4,6},{5,7},{6,4},{7,5},{8,10},{9,11},{10,... | collective-permute-start | bytes 786440 | tf_op jit(solution)/shard_map/ppermute | solution.py:299
  31.9 4.0 %collective-permute-start.11 = (bf16[2,2,2,1,8,1,256]{6,4,0,5,3,2,1:T(8,128)(2,1)S(1)}, bf16[2,2,2,1,8,1,256]{6,4,0,5,3,2,1:T(8,128)(2,1)S(1)}, u32[]{:S(2)}, u32[]{:S(2)}) collective-permute-start(bf16[2,2,2,1,8,1,256]{6,4,0,5,3,2,1:T(8,128)(2,1)S(1)} %copy.24), channel_id=1, source_target_pairs={{0,1},{1,0},{2,3},{3,2},{4,5},{5,4},{6,7},{7,6},{8,9},{9,8},{10,11... | collective-permute-start | bytes 98312 | tf_op jit(solution)/shard_map/ppermute | solution.py:320
  33.5 3.9 %collective-permute-start.12 = (bf16[2,2,2,1,8,1,256]{6,4,0,5,3,2,1:T(8,128)(2,1)S(1)}, bf16[2,2,2,1,8,1,256]{6,4,0,5,3,2,1:T(8,128)(2,1)S(1)}, u32[]{:S(2)}, u32[]{:S(2)}) collective-permute-start(bf16[2,2,2,1,8,1,256]{6,4,0,5,3,2,1:T(8,128)(2,1)S(1)} %copy.23), channel_id=1, source_target_pairs={{0,4},{1,5},{2,6},{3,7},{4,0},{5,1},{6,2},{7,3},{8,12},{9,13},{10,... | collective-permute-start | bytes 98312 | tf_op jit(solution)/shard_map/ppermute | solution.py:320
  35.0 4.8 %collective-permute-start.13 = (bf16[2,2,2,1,8,1,256]{6,4,0,5,3,2,1:T(8,128)(2,1)S(1)}, bf16[2,2,2,1,8,1,256]{6,4,0,5,3,2,1:T(8,128)(2,1)S(1)}, u32[]{:S(2)}, u32[]{:S(2)}) collective-permute-start(bf16[2,2,2,1,8,1,256]{6,4,0,5,3,2,1:T(8,128)(2,1)S(1)} %copy.22), channel_id=1, source_target_pairs={{0,5},{1,4},{2,7},{3,6},{4,1},{5,0},{6,3},{7,2},{8,13},{9,12},{10,... | collective-permute-start | bytes 98312 | tf_op jit(solution)/shard_map/ppermute | solution.py:320
  39.9 4.5 %collective-permute-start.14 = (f32[2,1,1,1,8,1,256]{6,4,0,5,3,2,1:T(8,128)S(1)}, f32[2,1,1,1,8,1,256]{6,4,0,5,3,2,1:T(8,128)S(1)}, u32[]{:S(2)}, u32[]{:S(2)}) collective-permute-start(f32[2,1,1,1,8,1,256]{6,4,0,5,3,2,1:T(8,128)S(1)} %get-tuple-element.40), channel_id=1, source_target_pairs={{0,8},{1,9},{2,10},{3,11},{4,12},{5,13},{6,14},{7,15},{8,0},{9,1},... | collective-permute-start | bytes 49160 | tf_op jit(solution)/shard_map/ppermute | solution.py:320
  40.4 4.6 %collective-permute-start.15 = (f32[2,1,1,1,8,1,256]{6,4,0,5,3,2,1:T(8,128)S(1)}, f32[2,1,1,1,8,1,256]{6,4,0,5,3,2,1:T(8,128)S(1)}, u32[]{:S(2)}, u32[]{:S(2)}) collective-permute-start(f32[2,1,1,1,8,1,256]{6,4,0,5,3,2,1:T(8,128)S(1)} %get-tuple-element.42), channel_id=1, source_target_pairs={{0,16},{1,17},{2,18},{3,19},{4,20},{5,21},{6,22},{7,23},{8,24},{9,... | collective-permute-start | bytes 49160 | tf_op jit(solution)/shard_map/ppermute | solution.py:320
  41.4 5.5 %collective-permute-start.16 = (f32[2,1,1,1,8,1,256]{6,4,0,5,3,2,1:T(8,128)S(1)}, f32[2,1,1,1,8,1,256]{6,4,0,5,3,2,1:T(8,128)S(1)}, u32[]{:S(2)}, u32[]{:S(2)}) collective-permute-start(f32[2,1,1,1,8,1,256]{6,4,0,5,3,2,1:T(8,128)S(1)} %get-tuple-element.41), channel_id=1, source_target_pairs={{0,24},{1,25},{2,26},{3,27},{4,28},{5,29},{6,30},{7,31},{8,16},{9,... | collective-permute-start | bytes 49160 | tf_op jit(solution)/shard_map/ppermute | solution.py:320

commit v3 on v2

--- a/solution.py
+++ b/solution.py
@@ -11,19 +11,15 @@
 AXES = ("gx", "gy", "gz")
 F32 = jnp.float32
 BF16 = jnp.bfloat16
-CHUNKS = 5
+CHUNKS = 8
+STAGES = (4, 6, 8)
 VMEM_LIMIT = 40 * 1024 * 1024
 OUT_VMEM = pltpu.VMEM
 
 
 def swap_rounds(sizes):
-    rounds = []
-    for pos, size in enumerate(sizes):
-        if size > 1:
-            rounds.append((pos, 0))
-        if size > 2:
-            rounds.append((pos, 1))
-    return rounds
+    rounds = [(pos, phase) for pos in (0, 2) for phase in (0, 1)] + [(1, 1), (1, 0)]
+    return [(pos, phase) for pos, phase in rounds if sizes[pos] > 1 + phase]
 
 
 def partner_of(sizes, pos, phase, here):
@@ -129,17 +125,19 @@
     ]
     accepted = jnp.concatenate([jnp.where(gate, row, -1) for gate, row in zip(gates, rows)], axis=1)
     across = lax.broadcasted_iota(jnp.int32, (face, unknowns), 1)
-    parts_of = blocks(unknowns)
-    for step in range(max(count, CHUNKS)):
-        if step < count:
-            chosen = jnp.where(across == upright[:, step : step + 1], 1.0, 0.0)
-            picks[pl.ds(step * face, face), :] = chosen.astype(BF16)
-        if step < CHUNKS:
-            part = parts_of[step]
-            down = part.start + lax.broadcasted_iota(jnp.int32, (part.size, count * face), 0)
-            puts[part, :] = jnp.where(down == accepted, 1.0, 0.0).astype(BF16)
-            large[step].wait()
+    for pos in range(count):
+        chosen = jnp.where(across == upright[:, pos : pos + 1], 1.0, 0.0)
+        picks[pl.ds(pos * face, face), :] = chosen.astype(BF16)
+    for part in blocks(unknowns):
+        down = part.start + lax.broadcasted_iota(jnp.int32, (part.size, count * face), 0)
+        puts[part, :] = jnp.where(down == accepted, 1.0, 0.0).astype(BF16)
+    ready = 0
+    for stage in STAGES:
+        for copy in large[ready:stage]:
+            copy.wait()
+        for part in blocks(unknowns)[ready:stage]:
             respond(response, source, crossed, outgoing, part)
+        ready = stage
     pick_faces(picks, outgoing, outs)
 
 
@@ -312,7 +310,7 @@
             return piece
 
         got = []
-        for code in range(1, 2 ** len(group)):
+        for code in reversed(range(1, 2 ** len(group))):
             flips = [0, 0, 0]
             for place, (pos, bit) in enumerate(group):
                 flips[pos] |= ((code >> place) & 1) << bit

time: 47.7 us -> 44 us (0.922)
  waiting for transfers between devices: 15.9 us -> 13.5 us
  Pallas kernels: 11.7 us -> 10.3 us
    ppermute x6, waiting for transfers between devices: 6.95 us -> 5.09 us  [scatter_sum(): got.append(lax.ppermute(piece, AXES, mask_pairs(sizes, flips)))]
    pallas_call x1, Pallas kernels: 6.46 us -> 5.46 us  [first_sweep(): pl.pallas_call(functools.partial(first_kernel, sizes, rounds), out_shape=...]
  transfers between devices with their start and end apart: 17 -> 17, of which waited for: 11 -> 12; matrix products, arithmetic and copies ran while one was open for 0% -> 0% of each run, Pallas kernels for 0% -> 0%
where the time goes in v3:
time: 44 us; the launch traced here: 43.9 us
  starting transfers between devices  19.3 us (44%)
  waiting for transfers between devices  13.5 us (31%)
  Pallas kernels  10.3 us (23%)
  other arithmetic  0.67 us (2%)
    ppermute x10, starting transfers between devices, shards(): lax.ppermute(face, AXES, swap_pairs(sizes, pos, phase))  11.1 us
    ppermute x6, starting transfers between devices, scatter_sum(): got.append(lax.ppermute(piece, AXES, mask_pairs(sizes, flips)))  8.01 us
    ppermute x10, waiting for transfers between devices, shards(): lax.ppermute(face, AXES, swap_pairs(sizes, pos, phase))  7.02 us
    pallas_call x1, Pallas kernels, first_sweep(): pl.pallas_call(functools.partial(first_kernel, sizes, rounds), out_shape=...  5.46 us
    ppermute x6, waiting for transfers between devices, scatter_sum(): got.append(lax.ppermute(piece, AXES, mask_pairs(sizes, flips)))  5.09 us
    pallas_call x1, Pallas kernels, later_sweep(): pl.pallas_call(functools.partial(sweep_kernel, count), out_shape=[jax.Sha...  3.18 us
    pallas_call x1, Pallas kernels, radiate(): pl.pallas_call(functools.partial(radiate_kernel, count, int(halves), eb),...  1.63 us
    ppermute x1, waiting for transfers between devices, scatter_sum(): total = total + lax.ppermute(parts[1], AXES, mask_pairs(sizes, (0, 1, 0)))  1.39 us
  transfers between devices with their start and end apart: 17, of which 12 were waited for; matrix products, arithmetic and copies ran while one was open for 0% of the time, Pallas kernels for 0%

profile of v3, /device:TPU:0, one launch (start us, length us, event | category | flops | bytes accessed | tf_op | source)
XLA Modules:
  0.0 43.9 jit_solution(7994326085079616182)
XLA Ops:
  0.0 5.5 %shard_map.55 = (bf16[192,256]{1,0:T(8,128)(2,1)S(1)}, bf16[192,256]{1,0:T(8,128)(2,1)S(1)}, bf16[192,256]{1,0:T(8,128)(2,1)S(1)}, bf16[192,256]{1,0:T(8,128)(2,...) custom-call(s32[6]{0:T(128)} %bitcast.14, ...), custom_call_target="tpu_custom_call" | custom-call | tf_op jit(solution)/shard_map/pallas_call | solution.py:212
  5.5 3.1 %collective-permute-start = (bf16[192,256]{1,0:T(8,128)(2,1)S(1)}, bf16[192,256]{1,0:T(8,128)(2,1)S(1)}, u32[]{:S(2)}, u32[]{:S(2)}) collective-permute-start(bf16[192,256]{1,0:T(8,128)(2,1)S(1)} %get-tuple-element.25), channel_id=1, source_target_pairs={{0,8},{1,9},{2,10},{3,11},{4,12},{5,13},{6,14},{7,15},{8,0},{9,1},... | collective-permute-start | bytes 294920 | tf_op jit(solution)/shard_map/ppermute | solution.py:336
  8.6 1.5 %collective-permute-start.2 = (bf16[192,256]{1,0:T(8,128)(2,1)S(1)}, bf16[192,256]{1,0:T(8,128)(2,1)S(1)}, u32[]{:S(2)}, u32[]{:S(2)}) collective-permute-start(bf16[192,256]{1,0:T(8,128)(2,1)S(1)} %get-tuple-element.27), channel_id=1, source_target_pairs={{0,1},{1,0},{2,3},{3,2},{4,5},{5,4},{6,7},{7,6},{8,9},{9,8},{10,11... | collective-permute-start | bytes 294920 | tf_op jit(solution)/shard_map/ppermute | solution.py:336
  10.1 1.4 %collective-permute-start.3 = (bf16[192,256]{1,0:T(8,128)(2,1)S(1)}, bf16[192,256]{1,0:T(8,128)(2,1)S(1)}, u32[]{:S(2)}, u32[]{:S(2)}) collective-permute-start(bf16[192,256]{1,0:T(8,128)(2,1)S(1)} %get-tuple-element.28), channel_id=1, source_target_pairs={{0,6},{1,7},{2,4},{3,5},{4,2},{5,3},{6,0},{7,1},{8,14},{9,15},{10,... | collective-permute-start | bytes 294920 | tf_op jit(solution)/shard_map/ppermute | solution.py:336
  11.7 2.1 %collective-permute-done.2.refs_2_ = bf16[192,256]{1,0:T(8,128)(2,1)S(1)} collective-permute-done((bf16[192,256]{1,0:T(8,128)(2,1)S(1)}, bf16[192,256]{1,0:T(8,128)(2,1)S(1)}, u32[]{:S(2)}, u32[]{:S(2)}) %collective-permute-start.2) | collective-permute-done | bytes 98336 | tf_op jit(solution)/shard_map/ppermute | solution.py:336
  13.8 1.1 %collective-permute-done.3.refs_3_ = bf16[192,256]{1,0:T(8,128)(2,1)S(1)} collective-permute-done((bf16[192,256]{1,0:T(8,128)(2,1)S(1)}, bf16[192,256]{1,0:T(8,128)(2,1)S(1)}, u32[]{:S(2)}, u32[]{:S(2)}) %collective-permute-start.3) | collective-permute-done | bytes 98336 | tf_op jit(solution)/shard_map/ppermute | solution.py:336
  14.8 3.2 %shard_map.56 = (bf16[192,256]{1,0:T(8,128)(2,1)S(1)}, bf16[192,256]{1,0:T(8,128)(2,1)S(1)}, bf16[192,256]{1,0:T(8,128)(2,1)S(1)}, bf16[192,256]{1,0:T(8,128)(2,1)S(1)}, bf16[192,256]{1,0:T(8,128)(2,1)S(1)}) custom-call(bf16[2,1280,1280]{2,1,0:T(8,128)(2,1)S(1)} %get-tuple-element.23.response, bf16[1280,256]{1,0:T(8,128)(2,1)S(1)} %get-tuple-element.21.source, ...), custom_call_target="tpu_custom_call" | custom-call | tf_op jit(solution)/shard_map/pallas_call | solution.py:234
  18.0 3.5 %collective-permute-start.5 = (bf16[192,256]{1,0:T(8,128)(2,1)S(1)}, bf16[192,256]{1,0:T(8,128)(2,1)S(1)}, u32[]{:S(2)}, u32[]{:S(2)}) collective-permute-start(bf16[192,256]{1,0:T(8,128)(2,1)S(1)} %get-tuple-element.30), channel_id=1, source_target_pairs={{0,8},{1,9},{2,10},{3,11},{4,12},{5,13},{6,14},{7,15},{8,0},{9,1},... | collective-permute-start | bytes 294920 | tf_op jit(solution)/shard_map/ppermute | solution.py:336
  22.0 0.6 %collective-permute-start.8 = (bf16[192,256]{1,0:T(8,128)(2,1)S(1)}, bf16[192,256]{1,0:T(8,128)(2,1)S(1)}, u32[]{:S(2)}, u32[]{:S(2)}) collective-permute-start(bf16[192,256]{1,0:T(8,128)(2,1)S(1)} %get-tuple-element.33), channel_id=1, source_target_pairs={{0,6},{1,7},{2,4},{3,5},{4,2},{5,3},{6,0},{7,1},{8,14},{9,15},{10,... | collective-permute-start | bytes 294920 | tf_op jit(solution)/shard_map/ppermute | solution.py:336
  22.9 1.7 %collective-permute-done.5.refs_0_ = bf16[192,256]{1,0:T(8,128)(2,1)S(1)} collective-permute-done((bf16[192,256]{1,0:T(8,128)(2,1)S(1)}, bf16[192,256]{1,0:T(8,128)(2,1)S(1)}, u32[]{:S(2)}, u32[]{:S(2)}) %collective-permute-start.5) | collective-permute-done | bytes 98336 | tf_op jit(solution)/shard_map/ppermute | solution.py:336
  24.6 2.1 %collective-permute-done.7.refs_2_ = bf16[192,256]{1,0:T(8,128)(2,1)S(1)} collective-permute-done((bf16[192,256]{1,0:T(8,128)(2,1)S(1)}, bf16[192,256]{1,0:T(8,128)(2,1)S(1)}, u32[]{:S(2)}, u32[]{:S(2)}) %collective-permute-start.7) | collective-permute-done | bytes 98336 | tf_op jit(solution)/shard_map/ppermute | solution.py:336
  26.8 1.6 %shard_map.57 = (f32[2,64,512]{2,1,0:T(8,128)S(1)}, f32[2,64,512]{2,1,0:T(8,128)S(1)}) custom-call(bf16[1280,256]{1,0:T(8,128)(2,1)S(1)} %get-tuple-element.21.source, bf16[1280,960]{1,0:T(8,128)(2,1)S(1)} %get-tuple-element.22.puts, bf16[2,512,1280]{2,1,0:T(8,128)(2,1)S(1)} %bitcast.8, bf16[192,256]{1,0:T(8,128)(2,1)S(1)} %collective-permute-done.5.refs_0_, ...), custom_call_target="tpu_custom_call" | custom-call | tf_op jit(solution)/shard_map/pallas_call | solution.py:252
  28.6 1.4 %collective-permute-done.10 = f32[2,64,512]{2,1,0:T(8,128)S(1)} collective-permute-done((f32[2,64,512]{2,1,0:T(8,128)S(1)}, f32[2,64,512]{2,1,0:T(8,128)S(1)}, u32[]{:S(2)}, u32[]{:S(2)}) %collective-permute-start.10) | collective-permute-done | bytes 262176 | tf_op jit(solution)/shard_map/ppermute | solution.py:297
  30.1 1.8 %collective-permute-start.11 = (bf16[2,2,2,1,8,1,256]{6,4,0,5,3,2,1:T(8,128)(2,1)S(1)}, bf16[2,2,2,1,8,1,256]{6,4,0,5,3,2,1:T(8,128)(2,1)S(1)}, u32[]{:S(2)}, u32[]{:S(2)}) collective-permute-start(bf16[2,2,2,1,8,1,256]{6,4,0,5,3,2,1:T(8,128)(2,1)S(1)} %copy.24), channel_id=1, source_target_pairs={{0,5},{1,4},{2,7},{3,6},{4,1},{5,0},{6,3},{7,2},{8,13},{9,12},{10,... | collective-permute-start | bytes 98312 | tf_op jit(solution)/shard_map/ppermute | solution.py:318
  31.9 1.3 %collective-permute-start.12 = (bf16[2,2,2,1,8,1,256]{6,4,0,5,3,2,1:T(8,128)(2,1)S(1)}, bf16[2,2,2,1,8,1,256]{6,4,0,5,3,2,1:T(8,128)(2,1)S(1)}, u32[]{:S(2)}, u32[]{:S(2)}) collective-permute-start(bf16[2,2,2,1,8,1,256]{6,4,0,5,3,2,1:T(8,128)(2,1)S(1)} %copy.23), channel_id=1, source_target_pairs={{0,4},{1,5},{2,6},{3,7},{4,0},{5,1},{6,2},{7,3},{8,12},{9,13},{10,... | collective-permute-start | bytes 98312 | tf_op jit(solution)/shard_map/ppermute | solution.py:318
  33.1 0.5 %collective-permute-start.13 = (bf16[2,2,2,1,8,1,256]{6,4,0,5,3,2,1:T(8,128)(2,1)S(1)}, bf16[2,2,2,1,8,1,256]{6,4,0,5,3,2,1:T(8,128)(2,1)S(1)}, u32[]{:S(2)}, u32[]{:S(2)}) collective-permute-start(bf16[2,2,2,1,8,1,256]{6,4,0,5,3,2,1:T(8,128)(2,1)S(1)} %copy.22), channel_id=1, source_target_pairs={{0,1},{1,0},{2,3},{3,2},{4,5},{5,4},{6,7},{7,6},{8,9},{9,8},{10,11... | collective-permute-start | bytes 98312 | tf_op jit(solution)/shard_map/ppermute | solution.py:318
  33.7 1.4 %collective-permute-done.11 = bf16[2,2,2,1,8,1,256]{6,4,0,5,3,2,1:T(8,128)(2,1)S(1)} collective-permute-done((bf16[2,2,2,1,8,1,256]{6,4,0,5,3,2,1:T(8,128)(2,1)S(1)}, bf16[2,2,2,1,8,1,256]{6,4,0,5,3,2,1:T(8,128)(2,1)S(1)}, u32[]{:S(2)}, u32[]{:S(2)}) %collective-permute-start.11) | collective-permute-done | bytes 32800 | tf_op jit(solution)/shard_map/ppermute | solution.py:318
  35.1 0.7 %collective-permute-done.12 = bf16[2,2,2,1,8,1,256]{6,4,0,5,3,2,1:T(8,128)(2,1)S(1)} collective-permute-done((bf16[2,2,2,1,8,1,256]{6,4,0,5,3,2,1:T(8,128)(2,1)S(1)}, bf16[2,2,2,1,8,1,256]{6,4,0,5,3,2,1:T(8,128)(2,1)S(1)}, u32[]{:S(2)}, u32[]{:S(2)}) %collective-permute-start.12) | collective-permute-done | bytes 32800 | tf_op jit(solution)/shard_map/ppermute | solution.py:318
  35.8 1.3 %collective-permute-done.13 = bf16[2,2,2,1,8,1,256]{6,4,0,5,3,2,1:T(8,128)(2,1)S(1)} collective-permute-done((bf16[2,2,2,1,8,1,256]{6,4,0,5,3,2,1:T(8,128)(2,1)S(1)}, bf16[2,2,2,1,8,1,256]{6,4,0,5,3,2,1:T(8,128)(2,1)S(1)}, u32[]{:S(2)}, u32[]{:S(2)}) %collective-permute-start.13) | collective-permute-done | bytes 32800 | tf_op jit(solution)/shard_map/ppermute | solution.py:318
  37.1 1.0 %collective-permute-start.14 = (f32[2,1,1,1,8,1,256]{6,4,0,5,3,2,1:T(8,128)S(1)}, f32[2,1,1,1,8,1,256]{6,4,0,5,3,2,1:T(8,128)S(1)}, u32[]{:S(2)}, u32[]{:S(2)}) collective-permute-start(f32[2,1,1,1,8,1,256]{6,4,0,5,3,2,1:T(8,128)S(1)} %get-tuple-element.40), channel_id=1, source_target_pairs={{0,24},{1,25},{2,26},{3,27},{4,28},{5,29},{6,30},{7,31},{8,16},{9,... | collective-permute-start | bytes 49160 | tf_op jit(solution)/shard_map/ppermute | solution.py:318
  38.1 1.0 %collective-permute-start.15 = (f32[2,1,1,1,8,1,256]{6,4,0,5,3,2,1:T(8,128)S(1)}, f32[2,1,1,1,8,1,256]{6,4,0,5,3,2,1:T(8,128)S(1)}, u32[]{:S(2)}, u32[]{:S(2)}) collective-permute-start(f32[2,1,1,1,8,1,256]{6,4,0,5,3,2,1:T(8,128)S(1)} %get-tuple-element.42), channel_id=1, source_target_pairs={{0,16},{1,17},{2,18},{3,19},{4,20},{5,21},{6,22},{7,23},{8,24},{9,... | collective-permute-start | bytes 49160 | tf_op jit(solution)/shard_map/ppermute | solution.py:318
  39.1 2.5 %collective-permute-start.16 = (f32[2,1,1,1,8,1,256]{6,4,0,5,3,2,1:T(8,128)S(1)}, f32[2,1,1,1,8,1,256]{6,4,0,5,3,2,1:T(8,128)S(1)}, u32[]{:S(2)}, u32[]{:S(2)}) collective-permute-start(f32[2,1,1,1,8,1,256]{6,4,0,5,3,2,1:T(8,128)S(1)} %get-tuple-element.41), channel_id=1, source_target_pairs={{0,8},{1,9},{2,10},{3,11},{4,12},{5,13},{6,14},{7,15},{8,0},{9,1},... | collective-permute-start | bytes 49160 | tf_op jit(solution)/shard_map/ppermute | solution.py:318
  41.6 1.2 %collective-permute-done.14 = f32[2,1,1,1,8,1,256]{6,4,0,5,3,2,1:T(8,128)S(1)} collective-permute-done((f32[2,1,1,1,8,1,256]{6,4,0,5,3,2,1:T(8,128)S(1)}, f32[2,1,1,1,8,1,256]{6,4,0,5,3,2,1:T(8,128)S(1)}, u32[]{:S(2)}, u32[]{:S(2)}) %collective-permute-start.14) | collective-permute-done | bytes 16416 | tf_op jit(solution)/shard_map/ppermute | solution.py:318
  43.3 0.6 %add_bitcast_fusion = f32[2,8,256]{2,1,0:T(8,128)} fusion(f32[2,1,1,1,8,1,256]{6,4,0,5,3,2,1:T(8,128)S(1)} %collective-permute-done.16, f32[2,1,1,1,8,1,256]{6,4,0,5,3,2,1:T(8,128)S(1)} %collective-permute-done.15, f32[2,1,1,1,8,1,256]{6,4,0,5,3,2,1:T(8,128)S(1)} %collective-permute-done.14, f32[2,2,2,1,8,1,256]{6,4,0,5,3,2,1:T(8,128)S(1)} %fusion.1, ...), kind=kLoop, calls=%fused_computation.6 | loop fusion | flops 12288 | bytes 81928 | tf_op jit(solution)/shard_map/reshape | solution.py:322
  (23 shorter events, 2.1 us)
Async XLA Ops:
  5.5 6.2 %collective-permute-start = (bf16[192,256]{1,0:T(8,128)(2,1)S(1)}, bf16[192,256]{1,0:T(8,128)(2,1)S(1)}, u32[]{:S(2)}, u32[]{:S(2)}) collective-permute-start(bf16[192,256]{1,0:T(8,128)(2,1)S(1)} %get-tuple-element.25), channel_id=1, source_target_pairs={{0,8},{1,9},{2,10},{3,11},{4,12},{5,13},{6,14},{7,15},{8,0},{9,1},... | collective-permute-start | bytes 294920 | tf_op jit(solution)/shard_map/ppermute | solution.py:336
  8.6 3.1 %collective-permute-start.1 = (bf16[192,256]{1,0:T(8,128)(2,1)S(1)}, bf16[192,256]{1,0:T(8,128)(2,1)S(1)}, u32[]{:S(2)}, u32[]{:S(2)}) collective-permute-start(bf16[192,256]{1,0:T(8,128)(2,1)S(1)} %get-tuple-element.26), channel_id=1, source_target_pairs={{0,2},{1,3},{2,0},{3,1},{4,6},{5,7},{6,4},{7,5},{8,16},{9,17},{10,... | collective-permute-start | bytes 294920 | tf_op jit(solution)/shard_map/ppermute | solution.py:336
  8.6 5.2 %collective-permute-start.2 = (bf16[192,256]{1,0:T(8,128)(2,1)S(1)}, bf16[192,256]{1,0:T(8,128)(2,1)S(1)}, u32[]{:S(2)}, u32[]{:S(2)}) collective-permute-start(bf16[192,256]{1,0:T(8,128)(2,1)S(1)} %get-tuple-element.27), channel_id=1, source_target_pairs={{0,1},{1,0},{2,3},{3,2},{4,5},{5,4},{6,7},{7,6},{8,9},{9,8},{10,11... | collective-permute-start | bytes 294920 | tf_op jit(solution)/shard_map/ppermute | solution.py:336
  10.1 4.8 %collective-permute-start.3 = (bf16[192,256]{1,0:T(8,128)(2,1)S(1)}, bf16[192,256]{1,0:T(8,128)(2,1)S(1)}, u32[]{:S(2)}, u32[]{:S(2)}) collective-permute-start(bf16[192,256]{1,0:T(8,128)(2,1)S(1)} %get-tuple-element.28), channel_id=1, source_target_pairs={{0,6},{1,7},{2,4},{3,5},{4,2},{5,3},{6,0},{7,1},{8,14},{9,15},{10,... | collective-permute-start | bytes 294920 | tf_op jit(solution)/shard_map/ppermute | solution.py:336
  11.4 3.4 %collective-permute-start.4 = (bf16[192,256]{1,0:T(8,128)(2,1)S(1)}, bf16[192,256]{1,0:T(8,128)(2,1)S(1)}, u32[]{:S(2)}, u32[]{:S(2)}) collective-permute-start(bf16[192,256]{1,0:T(8,128)(2,1)S(1)} %get-tuple-element.29), channel_id=1, source_target_pairs={{0,2},{1,3},{2,0},{3,1},{4,6},{5,7},{6,4},{7,5},{8,10},{9,11},{10,... | collective-permute-start | bytes 294920 | tf_op jit(solution)/shard_map/ppermute | solution.py:336
  14.8 12.0 %copy-start = (bf16[1,1,1,2,512,1280]{5,4,3,2,1,0:T(8,128)(2,1)S(1)}, bf16[1,1,1,2,512,1280]{5,4,3,2,1,0:T(8,128)(2,1)}, u32[]{:S(2)}) copy-start(bf16[1,1,1,2,512,1280]{5,4,3,2,1,0:T(8,128)(2,1)} %param.7) | copy-start | bytes 7864324
  18.0 6.5 %collective-permute-start.5 = (bf16[192,256]{1,0:T(8,128)(2,1)S(1)}, bf16[192,256]{1,0:T(8,128)(2,1)S(1)}, u32[]{:S(2)}, u32[]{:S(2)}) collective-permute-start(bf16[192,256]{1,0:T(8,128)(2,1)S(1)} %get-tuple-element.30), channel_id=1, source_target_pairs={{0,8},{1,9},{2,10},{3,11},{4,12},{5,13},{6,14},{7,15},{8,0},{9,1},... | collective-permute-start | bytes 294920 | tf_op jit(solution)/shard_map/ppermute | solution.py:336
  21.5 3.1 %collective-permute-start.6 = (bf16[192,256]{1,0:T(8,128)(2,1)S(1)}, bf16[192,256]{1,0:T(8,128)(2,1)S(1)}, u32[]{:S(2)}, u32[]{:S(2)}) collective-permute-start(bf16[192,256]{1,0:T(8,128)(2,1)S(1)} %get-tuple-element.31), channel_id=1, source_target_pairs={{0,2},{1,3},{2,0},{3,1},{4,6},{5,7},{6,4},{7,5},{8,16},{9,17},{10,... | collective-permute-start | bytes 294920 | tf_op jit(solution)/shard_map/ppermute | solution.py:336
  21.5 5.2 %collective-permute-start.7 = (bf16[192,256]{1,0:T(8,128)(2,1)S(1)}, bf16[192,256]{1,0:T(8,128)(2,1)S(1)}, u32[]{:S(2)}, u32[]{:S(2)}) collective-permute-start(bf16[192,256]{1,0:T(8,128)(2,1)S(1)} %get-tuple-element.32), channel_id=1, source_target_pairs={{0,1},{1,0},{2,3},{3,2},{4,5},{5,4},{6,7},{7,6},{8,9},{9,8},{10,11... | collective-permute-start | bytes 294920 | tf_op jit(solution)/shard_map/ppermute | solution.py:336
  22.0 4.8 %collective-permute-start.8 = (bf16[192,256]{1,0:T(8,128)(2,1)S(1)}, bf16[192,256]{1,0:T(8,128)(2,1)S(1)}, u32[]{:S(2)}, u32[]{:S(2)}) collective-permute-start(bf16[192,256]{1,0:T(8,128)(2,1)S(1)} %get-tuple-element.33), channel_id=1, source_target_pairs={{0,6},{1,7},{2,4},{3,5},{4,2},{5,3},{6,0},{7,1},{8,14},{9,15},{10,... | collective-permute-start | bytes 294920 | tf_op jit(solution)/shard_map/ppermute | solution.py:336
  22.6 4.2 %collective-permute-start.9 = (bf16[192,256]{1,0:T(8,128)(2,1)S(1)}, bf16[192,256]{1,0:T(8,128)(2,1)S(1)}, u32[]{:S(2)}, u32[]{:S(2)}) collective-permute-start(bf16[192,256]{1,0:T(8,128)(2,1)S(1)} %get-tuple-element.34), channel_id=1, source_target_pairs={{0,2},{1,3},{2,0},{3,1},{4,6},{5,7},{6,4},{7,5},{8,10},{9,11},{10,... | collective-permute-start | bytes 294920 | tf_op jit(solution)/shard_map/ppermute | solution.py:336
  28.4 1.6 %collective-permute-start.10 = (f32[2,64,512]{2,1,0:T(8,128)S(1)}, f32[2,64,512]{2,1,0:T(8,128)S(1)}, u32[]{:S(2)}, u32[]{:S(2)}) collective-permute-start(f32[2,64,512]{2,1,0:T(8,128)S(1)} %get-tuple-element.36), channel_id=1, source_target_pairs={{0,2},{1,3},{2,0},{3,1},{4,6},{5,7},{6,4},{7,5},{8,10},{9,11},{10,... | collective-permute-start | bytes 786440 | tf_op jit(solution)/shard_map/ppermute | solution.py:297
  30.1 4.9 %collective-permute-start.11 = (bf16[2,2,2,1,8,1,256]{6,4,0,5,3,2,1:T(8,128)(2,1)S(1)}, bf16[2,2,2,1,8,1,256]{6,4,0,5,3,2,1:T(8,128)(2,1)S(1)}, u32[]{:S(2)}, u32[]{:S(2)}) collective-permute-start(bf16[2,2,2,1,8,1,256]{6,4,0,5,3,2,1:T(8,128)(2,1)S(1)} %copy.24), channel_id=1, source_target_pairs={{0,5},{1,4},{2,7},{3,6},{4,1},{5,0},{6,3},{7,2},{8,13},{9,12},{10,... | collective-permute-start | bytes 98312 | tf_op jit(solution)/shard_map/ppermute | solution.py:318
  31.9 3.9 %collective-permute-start.12 = (bf16[2,2,2,1,8,1,256]{6,4,0,5,3,2,1:T(8,128)(2,1)S(1)}, bf16[2,2,2,1,8,1,256]{6,4,0,5,3,2,1:T(8,128)(2,1)S(1)}, u32[]{:S(2)}, u32[]{:S(2)}) collective-permute-start(bf16[2,2,2,1,8,1,256]{6,4,0,5,3,2,1:T(8,128)(2,1)S(1)} %copy.23), channel_id=1, source_target_pairs={{0,4},{1,5},{2,6},{3,7},{4,0},{5,1},{6,2},{7,3},{8,12},{9,13},{10,... | collective-permute-start | bytes 98312 | tf_op jit(solution)/shard_map/ppermute | solution.py:318
  33.1 3.9 %collective-permute-start.13 = (bf16[2,2,2,1,8,1,256]{6,4,0,5,3,2,1:T(8,128)(2,1)S(1)}, bf16[2,2,2,1,8,1,256]{6,4,0,5,3,2,1:T(8,128)(2,1)S(1)}, u32[]{:S(2)}, u32[]{:S(2)}) collective-permute-start(bf16[2,2,2,1,8,1,256]{6,4,0,5,3,2,1:T(8,128)(2,1)S(1)} %copy.22), channel_id=1, source_target_pairs={{0,1},{1,0},{2,3},{3,2},{4,5},{5,4},{6,7},{7,6},{8,9},{9,8},{10,11... | collective-permute-start | bytes 98312 | tf_op jit(solution)/shard_map/ppermute | solution.py:318
  37.1 5.6 %collective-permute-start.14 = (f32[2,1,1,1,8,1,256]{6,4,0,5,3,2,1:T(8,128)S(1)}, f32[2,1,1,1,8,1,256]{6,4,0,5,3,2,1:T(8,128)S(1)}, u32[]{:S(2)}, u32[]{:S(2)}) collective-permute-start(f32[2,1,1,1,8,1,256]{6,4,0,5,3,2,1:T(8,128)S(1)} %get-tuple-element.40), channel_id=1, source_target_pairs={{0,24},{1,25},{2,26},{3,27},{4,28},{5,29},{6,30},{7,31},{8,16},{9,... | collective-permute-start | bytes 49160 | tf_op jit(solution)/shard_map/ppermute | solution.py:318
  38.1 4.8 %collective-permute-start.15 = (f32[2,1,1,1,8,1,256]{6,4,0,5,3,2,1:T(8,128)S(1)}, f32[2,1,1,1,8,1,256]{6,4,0,5,3,2,1:T(8,128)S(1)}, u32[]{:S(2)}, u32[]{:S(2)}) collective-permute-start(f32[2,1,1,1,8,1,256]{6,4,0,5,3,2,1:T(8,128)S(1)} %get-tuple-element.42), channel_id=1, source_target_pairs={{0,16},{1,17},{2,18},{3,19},{4,20},{5,21},{6,22},{7,23},{8,24},{9,... | collective-permute-start | bytes 49160 | tf_op jit(solution)/shard_map/ppermute | solution.py:318
  39.1 4.2 %collective-permute-start.16 = (f32[2,1,1,1,8,1,256]{6,4,0,5,3,2,1:T(8,128)S(1)}, f32[2,1,1,1,8,1,256]{6,4,0,5,3,2,1:T(8,128)S(1)}, u32[]{:S(2)}, u32[]{:S(2)}) collective-permute-start(f32[2,1,1,1,8,1,256]{6,4,0,5,3,2,1:T(8,128)S(1)} %get-tuple-element.41), channel_id=1, source_target_pairs={{0,8},{1,9},{2,10},{3,11},{4,12},{5,13},{6,14},{7,15},{8,0},{9,1},... | collective-permute-start | bytes 49160 | tf_op jit(solution)/shard_map/ppermute | solution.py:318

commit v4 on v3

--- a/solution.py
+++ b/solution.py
@@ -154,7 +154,16 @@
     pick_faces(picks, outgoing, outs)
 
 
-def radiate_kernel(count, halves, eb, source, puts, radiation, *refs):
+def tint(at_x, at_y):
+    return (at_x ^ (at_y >> 1)) & 1
+
+
+def half_starts(sizes, half, eb, columns):
+    chips = sizes[1] // 2
+    return [(2 * pos + (half ^ tint(pos // chips, 2 * (pos % chips)))) * eb for pos in range(columns // (2 * eb))]
+
+
+def radiate_kernel(sizes, count, halves, eb, source, puts, radiation, *refs):
     arrived, outs = refs[:count], refs[count : count + 1 + halves]
     values, straight, crossed = refs[count + 1 + halves :]
     columns = source.shape[1] // 2
@@ -166,14 +175,15 @@
     field = jnp.dot(radiation[0], straight[...], preferred_element_type=F32) + jnp.dot(
         radiation[1], crossed[...], preferred_element_type=F32
     )
-    mine = lax.axis_index("gy") & 1
+    along, across = lax.axis_index("gy"), lax.axis_index("gx")
+    mine = (along & 1) ^ tint(across, along)
     for part in range(2):
         flat = jnp.transpose(field[:, part * columns : (part + 1) * columns])
         if not halves:
             outs[0][part] = flat
             continue
         split = [
-            jnp.concatenate([flat[low : low + eb] for low in range(half * eb, columns, 2 * eb)], axis=0)
+            jnp.concatenate([flat[start : start + eb] for start in half_starts(sizes, half, eb, columns)], axis=0)
             for half in range(2)
         ]
         outs[0][part] = jnp.where(mine == 0, split[0], split[1])
@@ -242,7 +252,7 @@
     )(response, source, puts, picks, *arrived)
 
 
-def radiate(kept, radiation, arrived, halves, eb):
+def radiate(sizes, kept, radiation, arrived, halves, eb):
     source, puts, picks = kept[1:]
     columns = source.shape[1] // 2
     angles = radiation.shape[1]
@@ -250,7 +260,7 @@
     shape = (2, columns // 2 if halves else columns, angles)
     outs = [jax.ShapeDtypeStruct(shape, F32)] * (1 + int(halves))
     return pl.pallas_call(
-        functools.partial(radiate_kernel, count, int(halves), eb),
+        functools.partial(radiate_kernel, sizes, count, int(halves), eb),
         out_shape=outs,
         in_specs=[vmem_spec()] * (3 + count),
         out_specs=[vmem_spec()] * len(outs),
@@ -314,6 +324,8 @@
             flips = [0, 0, 0]
             for place, (pos, bit) in enumerate(group):
                 flips[pos] |= ((code >> place) & 1) << bit
+            if halves:
+                flips[1] ^= tint(flips[0], flips[1])
             piece = taken(code) if wide else taken(code).astype(BF16)
             got.append(lax.ppermute(piece, AXES, mask_pairs(sizes, flips)))
         total = taken(0)
@@ -339,7 +351,7 @@
         if turn < ITERS - 1:
             faces = later_sweep(kept, arrived)
     halves = sizes[1] % 2 == 0
-    parts = radiate(kept, radiation_mat, arrived, halves, columns // (sizes[0] * sizes[1]))
+    parts = radiate(sizes, kept, radiation_mat, arrived, halves, columns // (sizes[0] * sizes[1]))
     return scatter_sum(parts, sizes, where, (columns, angles))
 
 

time: 44 us -> 43.2 us (0.982)
  starting transfers between devices: 19.3 us -> 18.5 us
    ppermute x6, starting transfers between devices: 8.01 us -> 7.16 us  [scatter_sum(): got.append(lax.ppermute(piece, AXES, mask_pairs(sizes, flips)))]
where the time goes in v4:
time: 43.2 us; the launch traced here: 43 us
  starting transfers between devices  18.5 us (43%)
  waiting for transfers between devices  13.5 us (31%)
  Pallas kernels  10.3 us (24%)
  other arithmetic  0.67 us (2%)
    ppermute x10, starting transfers between devices, shards(): lax.ppermute(face, AXES, swap_pairs(sizes, pos, phase))  11.1 us
    ppermute x6, starting transfers between devices, scatter_sum(): got.append(lax.ppermute(piece, AXES, mask_pairs(sizes, flips)))  7.16 us
    ppermute x10, waiting for transfers between devices, shards(): lax.ppermute(face, AXES, swap_pairs(sizes, pos, phase))  7.02 us
    pallas_call x1, Pallas kernels, first_sweep(): pl.pallas_call(functools.partial(first_kernel, sizes, rounds), out_shape=...  5.46 us
    ppermute x6, waiting for transfers between devices, scatter_sum(): got.append(lax.ppermute(piece, AXES, mask_pairs(sizes, flips)))  5.06 us
    pallas_call x1, Pallas kernels, later_sweep(): pl.pallas_call(functools.partial(sweep_kernel, count), out_shape=[jax.Sha...  3.18 us
    pallas_call x1, Pallas kernels, radiate(): pl.pallas_call(functools.partial(radiate_kernel, sizes, count, int(halves...  1.63 us
    ppermute x1, waiting for transfers between devices, scatter_sum(): total = total + lax.ppermute(parts[1], AXES, mask_pairs(sizes, (0, 1, 0)))  1.39 us
  transfers between devices with their start and end apart: 17, of which 12 were waited for; matrix products, arithmetic and copies ran while one was open for 0% of the time, Pallas kernels for 0%

profile of v4, /device:TPU:0, one launch (start us, length us, event | category | flops | bytes accessed | tf_op | source)
XLA Modules:
  0.0 43.0 jit_solution(15692220598151432652)
XLA Ops:
  0.0 5.5 %shard_map.55 = (bf16[192,256]{1,0:T(8,128)(2,1)S(1)}, bf16[192,256]{1,0:T(8,128)(2,1)S(1)}, bf16[192,256]{1,0:T(8,128)(2,1)S(1)}, bf16[192,256]{1,0:T(8,128)(2,...) custom-call(s32[6]{0:T(128)} %bitcast.14, ...), custom_call_target="tpu_custom_call" | custom-call | tf_op jit(solution)/shard_map/pallas_call | solution.py:222
  5.5 3.1 %collective-permute-start = (bf16[192,256]{1,0:T(8,128)(2,1)S(1)}, bf16[192,256]{1,0:T(8,128)(2,1)S(1)}, u32[]{:S(2)}, u32[]{:S(2)}) collective-permute-start(bf16[192,256]{1,0:T(8,128)(2,1)S(1)} %get-tuple-element.25), channel_id=1, source_target_pairs={{0,8},{1,9},{2,10},{3,11},{4,12},{5,13},{6,14},{7,15},{8,0},{9,1},... | collective-permute-start | bytes 294920 | tf_op jit(solution)/shard_map/ppermute | solution.py:348
  8.6 1.5 %collective-permute-start.2 = (bf16[192,256]{1,0:T(8,128)(2,1)S(1)}, bf16[192,256]{1,0:T(8,128)(2,1)S(1)}, u32[]{:S(2)}, u32[]{:S(2)}) collective-permute-start(bf16[192,256]{1,0:T(8,128)(2,1)S(1)} %get-tuple-element.27), channel_id=1, source_target_pairs={{0,1},{1,0},{2,3},{3,2},{4,5},{5,4},{6,7},{7,6},{8,9},{9,8},{10,11... | collective-permute-start | bytes 294920 | tf_op jit(solution)/shard_map/ppermute | solution.py:348
  10.1 1.4 %collective-permute-start.3 = (bf16[192,256]{1,0:T(8,128)(2,1)S(1)}, bf16[192,256]{1,0:T(8,128)(2,1)S(1)}, u32[]{:S(2)}, u32[]{:S(2)}) collective-permute-start(bf16[192,256]{1,0:T(8,128)(2,1)S(1)} %get-tuple-element.28), channel_id=1, source_target_pairs={{0,6},{1,7},{2,4},{3,5},{4,2},{5,3},{6,0},{7,1},{8,14},{9,15},{10,... | collective-permute-start | bytes 294920 | tf_op jit(solution)/shard_map/ppermute | solution.py:348
  11.7 2.1 %collective-permute-done.2.refs_2_ = bf16[192,256]{1,0:T(8,128)(2,1)S(1)} collective-permute-done((bf16[192,256]{1,0:T(8,128)(2,1)S(1)}, bf16[192,256]{1,0:T(8,128)(2,1)S(1)}, u32[]{:S(2)}, u32[]{:S(2)}) %collective-permute-start.2) | collective-permute-done | bytes 98336 | tf_op jit(solution)/shard_map/ppermute | solution.py:348
  13.8 1.1 %collective-permute-done.3.refs_3_ = bf16[192,256]{1,0:T(8,128)(2,1)S(1)} collective-permute-done((bf16[192,256]{1,0:T(8,128)(2,1)S(1)}, bf16[192,256]{1,0:T(8,128)(2,1)S(1)}, u32[]{:S(2)}, u32[]{:S(2)}) %collective-permute-start.3) | collective-permute-done | bytes 98336 | tf_op jit(solution)/shard_map/ppermute | solution.py:348
  14.8 3.2 %shard_map.56 = (bf16[192,256]{1,0:T(8,128)(2,1)S(1)}, bf16[192,256]{1,0:T(8,128)(2,1)S(1)}, bf16[192,256]{1,0:T(8,128)(2,1)S(1)}, bf16[192,256]{1,0:T(8,128)(2,1)S(1)}, bf16[192,256]{1,0:T(8,128)(2,1)S(1)}) custom-call(bf16[2,1280,1280]{2,1,0:T(8,128)(2,1)S(1)} %get-tuple-element.23.response, bf16[1280,256]{1,0:T(8,128)(2,1)S(1)} %get-tuple-element.21.source, ...), custom_call_target="tpu_custom_call" | custom-call | tf_op jit(solution)/shard_map/pallas_call | solution.py:244
  18.0 3.5 %collective-permute-start.5 = (bf16[192,256]{1,0:T(8,128)(2,1)S(1)}, bf16[192,256]{1,0:T(8,128)(2,1)S(1)}, u32[]{:S(2)}, u32[]{:S(2)}) collective-permute-start(bf16[192,256]{1,0:T(8,128)(2,1)S(1)} %get-tuple-element.30), channel_id=1, source_target_pairs={{0,8},{1,9},{2,10},{3,11},{4,12},{5,13},{6,14},{7,15},{8,0},{9,1},... | collective-permute-start | bytes 294920 | tf_op jit(solution)/shard_map/ppermute | solution.py:348
  21.5 0.5 %collective-permute-start.7 = (bf16[192,256]{1,0:T(8,128)(2,1)S(1)}, bf16[192,256]{1,0:T(8,128)(2,1)S(1)}, u32[]{:S(2)}, u32[]{:S(2)}) collective-permute-start(bf16[192,256]{1,0:T(8,128)(2,1)S(1)} %get-tuple-element.32), channel_id=1, source_target_pairs={{0,1},{1,0},{2,3},{3,2},{4,5},{5,4},{6,7},{7,6},{8,9},{9,8},{10,11... | collective-permute-start | bytes 294920 | tf_op jit(solution)/shard_map/ppermute | solution.py:348
  22.0 0.6 %collective-permute-start.8 = (bf16[192,256]{1,0:T(8,128)(2,1)S(1)}, bf16[192,256]{1,0:T(8,128)(2,1)S(1)}, u32[]{:S(2)}, u32[]{:S(2)}) collective-permute-start(bf16[192,256]{1,0:T(8,128)(2,1)S(1)} %get-tuple-element.33), channel_id=1, source_target_pairs={{0,6},{1,7},{2,4},{3,5},{4,2},{5,3},{6,0},{7,1},{8,14},{9,15},{10,... | collective-permute-start | bytes 294920 | tf_op jit(solution)/shard_map/ppermute | solution.py:348
  22.9 1.7 %collective-permute-done.5.refs_0_ = bf16[192,256]{1,0:T(8,128)(2,1)S(1)} collective-permute-done((bf16[192,256]{1,0:T(8,128)(2,1)S(1)}, bf16[192,256]{1,0:T(8,128)(2,1)S(1)}, u32[]{:S(2)}, u32[]{:S(2)}) %collective-permute-start.5) | collective-permute-done | bytes 98336 | tf_op jit(solution)/shard_map/ppermute | solution.py:348
  24.6 2.1 %collective-permute-done.7.refs_2_ = bf16[192,256]{1,0:T(8,128)(2,1)S(1)} collective-permute-done((bf16[192,256]{1,0:T(8,128)(2,1)S(1)}, bf16[192,256]{1,0:T(8,128)(2,1)S(1)}, u32[]{:S(2)}, u32[]{:S(2)}) %collective-permute-start.7) | collective-permute-done | bytes 98336 | tf_op jit(solution)/shard_map/ppermute | solution.py:348
  26.8 1.6 %shard_map.57 = (f32[2,64,512]{2,1,0:T(8,128)S(1)}, f32[2,64,512]{2,1,0:T(8,128)S(1)}) custom-call(bf16[1280,256]{1,0:T(8,128)(2,1)S(1)} %get-tuple-element.21.source, bf16[1280,960]{1,0:T(8,128)(2,1)S(1)} %get-tuple-element.22.puts, bf16[2,512,1280]{2,1,0:T(8,128)(2,1)S(1)} %bitcast.8, bf16[192,256]{1,0:T(8,128)(2,1)S(1)} %collective-permute-done.5.refs_0_, ...), custom_call_target="tpu_custom_call" | custom-call | tf_op jit(solution)/shard_map/pallas_call | solution.py:262
  28.6 1.4 %collective-permute-done.10 = f32[2,64,512]{2,1,0:T(8,128)S(1)} collective-permute-done((f32[2,64,512]{2,1,0:T(8,128)S(1)}, f32[2,64,512]{2,1,0:T(8,128)S(1)}, u32[]{:S(2)}, u32[]{:S(2)}) %collective-permute-start.10) | collective-permute-done | bytes 262176 | tf_op jit(solution)/shard_map/ppermute | solution.py:307
  30.1 1.5 %collective-permute-start.11 = (bf16[2,2,2,1,8,1,256]{6,4,0,5,3,2,1:T(8,128)(2,1)S(1)}, bf16[2,2,2,1,8,1,256]{6,4,0,5,3,2,1:T(8,128)(2,1)S(1)}, u32[]{:S(2)}, u32[]{:S(2)}) collective-permute-start(bf16[2,2,2,1,8,1,256]{6,4,0,5,3,2,1:T(8,128)(2,1)S(1)} %copy.24), channel_id=1, source_target_pairs={{0,7},{1,6},{2,5},{3,4},{4,3},{5,2},{6,1},{7,0},{8,15},{9,14},{10,... | collective-permute-start | bytes 98312 | tf_op jit(solution)/shard_map/ppermute | solution.py:330
  31.6 1.2 %collective-permute-start.12 = (bf16[2,2,2,1,8,1,256]{6,4,0,5,3,2,1:T(8,128)(2,1)S(1)}, bf16[2,2,2,1,8,1,256]{6,4,0,5,3,2,1:T(8,128)(2,1)S(1)}, u32[]{:S(2)}, u32[]{:S(2)}) collective-permute-start(bf16[2,2,2,1,8,1,256]{6,4,0,5,3,2,1:T(8,128)(2,1)S(1)} %copy.23), channel_id=1, source_target_pairs={{0,6},{1,7},{2,4},{3,5},{4,2},{5,3},{6,0},{7,1},{8,14},{9,15},{10,... | collective-permute-start | bytes 98312 | tf_op jit(solution)/shard_map/ppermute | solution.py:330
  32.9 0.5 %collective-permute-start.13 = (bf16[2,2,2,1,8,1,256]{6,4,0,5,3,2,1:T(8,128)(2,1)S(1)}, bf16[2,2,2,1,8,1,256]{6,4,0,5,3,2,1:T(8,128)(2,1)S(1)}, u32[]{:S(2)}, u32[]{:S(2)}) collective-permute-start(bf16[2,2,2,1,8,1,256]{6,4,0,5,3,2,1:T(8,128)(2,1)S(1)} %copy.22), channel_id=1, source_target_pairs={{0,1},{1,0},{2,3},{3,2},{4,5},{5,4},{6,7},{7,6},{8,9},{9,8},{10,11... | collective-permute-start | bytes 98312 | tf_op jit(solution)/shard_map/ppermute | solution.py:330
  33.4 1.0 %collective-permute-done.11 = bf16[2,2,2,1,8,1,256]{6,4,0,5,3,2,1:T(8,128)(2,1)S(1)} collective-permute-done((bf16[2,2,2,1,8,1,256]{6,4,0,5,3,2,1:T(8,128)(2,1)S(1)}, bf16[2,2,2,1,8,1,256]{6,4,0,5,3,2,1:T(8,128)(2,1)S(1)}, u32[]{:S(2)}, u32[]{:S(2)}) %collective-permute-start.11) | collective-permute-done | bytes 32800 | tf_op jit(solution)/shard_map/ppermute | solution.py:330
  34.4 0.7 %collective-permute-done.12 = bf16[2,2,2,1,8,1,256]{6,4,0,5,3,2,1:T(8,128)(2,1)S(1)} collective-permute-done((bf16[2,2,2,1,8,1,256]{6,4,0,5,3,2,1:T(8,128)(2,1)S(1)}, bf16[2,2,2,1,8,1,256]{6,4,0,5,3,2,1:T(8,128)(2,1)S(1)}, u32[]{:S(2)}, u32[]{:S(2)}) %collective-permute-start.12) | collective-permute-done | bytes 32800 | tf_op jit(solution)/shard_map/ppermute | solution.py:330
  35.1 1.7 %collective-permute-done.13 = bf16[2,2,2,1,8,1,256]{6,4,0,5,3,2,1:T(8,128)(2,1)S(1)} collective-permute-done((bf16[2,2,2,1,8,1,256]{6,4,0,5,3,2,1:T(8,128)(2,1)S(1)}, bf16[2,2,2,1,8,1,256]{6,4,0,5,3,2,1:T(8,128)(2,1)S(1)}, u32[]{:S(2)}, u32[]{:S(2)}) %collective-permute-start.13) | collective-permute-done | bytes 32800 | tf_op jit(solution)/shard_map/ppermute | solution.py:330
  36.9 1.7 %collective-permute-start.15 = (f32[2,1,1,1,8,1,256]{6,4,0,5,3,2,1:T(8,128)S(1)}, f32[2,1,1,1,8,1,256]{6,4,0,5,3,2,1:T(8,128)S(1)}, u32[]{:S(2)}, u32[]{:S(2)}) collective-permute-start(f32[2,1,1,1,8,1,256]{6,4,0,5,3,2,1:T(8,128)S(1)} %get-tuple-element.42), channel_id=1, source_target_pairs={{0,16},{1,17},{2,18},{3,19},{4,20},{5,21},{6,22},{7,23},{8,24},{9,... | collective-permute-start | bytes 49160 | tf_op jit(solution)/shard_map/ppermute | solution.py:330
  38.6 2.2 %collective-permute-start.16 = (f32[2,1,1,1,8,1,256]{6,4,0,5,3,2,1:T(8,128)S(1)}, f32[2,1,1,1,8,1,256]{6,4,0,5,3,2,1:T(8,128)S(1)}, u32[]{:S(2)}, u32[]{:S(2)}) collective-permute-start(f32[2,1,1,1,8,1,256]{6,4,0,5,3,2,1:T(8,128)S(1)} %get-tuple-element.41), channel_id=1, source_target_pairs={{0,10},{1,11},{2,8},{3,9},{4,14},{5,15},{6,12},{7,13},{8,2},{9,3},... | collective-permute-start | bytes 49160 | tf_op jit(solution)/shard_map/ppermute | solution.py:330
  40.7 1.4 %collective-permute-done.14 = f32[2,1,1,1,8,1,256]{6,4,0,5,3,2,1:T(8,128)S(1)} collective-permute-done((f32[2,1,1,1,8,1,256]{6,4,0,5,3,2,1:T(8,128)S(1)}, f32[2,1,1,1,8,1,256]{6,4,0,5,3,2,1:T(8,128)S(1)}, u32[]{:S(2)}, u32[]{:S(2)}) %collective-permute-start.14) | collective-permute-done | bytes 16416 | tf_op jit(solution)/shard_map/ppermute | solution.py:330
  42.4 0.6 %add_bitcast_fusion = f32[2,8,256]{2,1,0:T(8,128)} fusion(f32[2,1,1,1,8,1,256]{6,4,0,5,3,2,1:T(8,128)S(1)} %collective-permute-done.16, f32[2,1,1,1,8,1,256]{6,4,0,5,3,2,1:T(8,128)S(1)} %collective-permute-done.15, f32[2,1,1,1,8,1,256]{6,4,0,5,3,2,1:T(8,128)S(1)} %collective-permute-done.14, f32[2,2,2,1,8,1,256]{6,4,0,5,3,2,1:T(8,128)S(1)} %fusion.1, ...), kind=kLoop, calls=%fused_computation.6 | loop fusion | flops 12288 | bytes 81928 | tf_op jit(solution)/shard_map/reshape | solution.py:334
  (23 shorter events, 1.4 us)
Async XLA Ops:
  5.5 6.2 %collective-permute-start = (bf16[192,256]{1,0:T(8,128)(2,1)S(1)}, bf16[192,256]{1,0:T(8,128)(2,1)S(1)}, u32[]{:S(2)}, u32[]{:S(2)}) collective-permute-start(bf16[192,256]{1,0:T(8,128)(2,1)S(1)} %get-tuple-element.25), channel_id=1, source_target_pairs={{0,8},{1,9},{2,10},{3,11},{4,12},{5,13},{6,14},{7,15},{8,0},{9,1},... | collective-permute-start | bytes 294920 | tf_op jit(solution)/shard_map/ppermute | solution.py:348
  8.6 3.1 %collective-permute-start.1 = (bf16[192,256]{1,0:T(8,128)(2,1)S(1)}, bf16[192,256]{1,0:T(8,128)(2,1)S(1)}, u32[]{:S(2)}, u32[]{:S(2)}) collective-permute-start(bf16[192,256]{1,0:T(8,128)(2,1)S(1)} %get-tuple-element.26), channel_id=1, source_target_pairs={{0,2},{1,3},{2,0},{3,1},{4,6},{5,7},{6,4},{7,5},{8,16},{9,17},{10,... | collective-permute-start | bytes 294920 | tf_op jit(solution)/shard_map/ppermute | solution.py:348
  8.6 5.2 %collective-permute-start.2 = (bf16[192,256]{1,0:T(8,128)(2,1)S(1)}, bf16[192,256]{1,0:T(8,128)(2,1)S(1)}, u32[]{:S(2)}, u32[]{:S(2)}) collective-permute-start(bf16[192,256]{1,0:T(8,128)(2,1)S(1)} %get-tuple-element.27), channel_id=1, source_target_pairs={{0,1},{1,0},{2,3},{3,2},{4,5},{5,4},{6,7},{7,6},{8,9},{9,8},{10,11... | collective-permute-start | bytes 294920 | tf_op jit(solution)/shard_map/ppermute | solution.py:348
  10.1 4.8 %collective-permute-start.3 = (bf16[192,256]{1,0:T(8,128)(2,1)S(1)}, bf16[192,256]{1,0:T(8,128)(2,1)S(1)}, u32[]{:S(2)}, u32[]{:S(2)}) collective-permute-start(bf16[192,256]{1,0:T(8,128)(2,1)S(1)} %get-tuple-element.28), channel_id=1, source_target_pairs={{0,6},{1,7},{2,4},{3,5},{4,2},{5,3},{6,0},{7,1},{8,14},{9,15},{10,... | collective-permute-start | bytes 294920 | tf_op jit(solution)/shard_map/ppermute | solution.py:348
  11.4 3.4 %collective-permute-start.4 = (bf16[192,256]{1,0:T(8,128)(2,1)S(1)}, bf16[192,256]{1,0:T(8,128)(2,1)S(1)}, u32[]{:S(2)}, u32[]{:S(2)}) collective-permute-start(bf16[192,256]{1,0:T(8,128)(2,1)S(1)} %get-tuple-element.29), channel_id=1, source_target_pairs={{0,2},{1,3},{2,0},{3,1},{4,6},{5,7},{6,4},{7,5},{8,10},{9,11},{10,... | collective-permute-start | bytes 294920 | tf_op jit(solution)/shard_map/ppermute | solution.py:348
  14.8 12.0 %copy-start = (bf16[1,1,1,2,512,1280]{5,4,3,2,1,0:T(8,128)(2,1)S(1)}, bf16[1,1,1,2,512,1280]{5,4,3,2,1,0:T(8,128)(2,1)}, u32[]{:S(2)}) copy-start(bf16[1,1,1,2,512,1280]{5,4,3,2,1,0:T(8,128)(2,1)} %param.7) | copy-start | bytes 7864324
  18.0 6.5 %collective-permute-start.5 = (bf16[192,256]{1,0:T(8,128)(2,1)S(1)}, bf16[192,256]{1,0:T(8,128)(2,1)S(1)}, u32[]{:S(2)}, u32[]{:S(2)}) collective-permute-start(bf16[192,256]{1,0:T(8,128)(2,1)S(1)} %get-tuple-element.30), channel_id=1, source_target_pairs={{0,8},{1,9},{2,10},{3,11},{4,12},{5,13},{6,14},{7,15},{8,0},{9,1},... | collective-permute-start | bytes 294920 | tf_op jit(solution)/shard_map/ppermute | solution.py:348
  21.5 3.1 %collective-permute-start.6 = (bf16[192,256]{1,0:T(8,128)(2,1)S(1)}, bf16[192,256]{1,0:T(8,128)(2,1)S(1)}, u32[]{:S(2)}, u32[]{:S(2)}) collective-permute-start(bf16[192,256]{1,0:T(8,128)(2,1)S(1)} %get-tuple-element.31), channel_id=1, source_target_pairs={{0,2},{1,3},{2,0},{3,1},{4,6},{5,7},{6,4},{7,5},{8,16},{9,17},{10,... | collective-permute-start | bytes 294920 | tf_op jit(solution)/shard_map/ppermute | solution.py:348
  21.5 5.2 %collective-permute-start.7 = (bf16[192,256]{1,0:T(8,128)(2,1)S(1)}, bf16[192,256]{1,0:T(8,128)(2,1)S(1)}, u32[]{:S(2)}, u32[]{:S(2)}) collective-permute-start(bf16[192,256]{1,0:T(8,128)(2,1)S(1)} %get-tuple-element.32), channel_id=1, source_target_pairs={{0,1},{1,0},{2,3},{3,2},{4,5},{5,4},{6,7},{7,6},{8,9},{9,8},{10,11... | collective-permute-start | bytes 294920 | tf_op jit(solution)/shard_map/ppermute | solution.py:348
  22.0 4.8 %collective-permute-start.8 = (bf16[192,256]{1,0:T(8,128)(2,1)S(1)}, bf16[192,256]{1,0:T(8,128)(2,1)S(1)}, u32[]{:S(2)}, u32[]{:S(2)}) collective-permute-start(bf16[192,256]{1,0:T(8,128)(2,1)S(1)} %get-tuple-element.33), channel_id=1, source_target_pairs={{0,6},{1,7},{2,4},{3,5},{4,2},{5,3},{6,0},{7,1},{8,14},{9,15},{10,... | collective-permute-start | bytes 294920 | tf_op jit(solution)/shard_map/ppermute | solution.py:348
  22.6 4.2 %collective-permute-start.9 = (bf16[192,256]{1,0:T(8,128)(2,1)S(1)}, bf16[192,256]{1,0:T(8,128)(2,1)S(1)}, u32[]{:S(2)}, u32[]{:S(2)}) collective-permute-start(bf16[192,256]{1,0:T(8,128)(2,1)S(1)} %get-tuple-element.34), channel_id=1, source_target_pairs={{0,2},{1,3},{2,0},{3,1},{4,6},{5,7},{6,4},{7,5},{8,10},{9,11},{10,... | collective-permute-start | bytes 294920 | tf_op jit(solution)/shard_map/ppermute | solution.py:348
  28.4 1.6 %collective-permute-start.10 = (f32[2,64,512]{2,1,0:T(8,128)S(1)}, f32[2,64,512]{2,1,0:T(8,128)S(1)}, u32[]{:S(2)}, u32[]{:S(2)}) collective-permute-start(f32[2,64,512]{2,1,0:T(8,128)S(1)} %get-tuple-element.36), channel_id=1, source_target_pairs={{0,2},{1,3},{2,0},{3,1},{4,6},{5,7},{6,4},{7,5},{8,10},{9,11},{10,... | collective-permute-start | bytes 786440 | tf_op jit(solution)/shard_map/ppermute | solution.py:307
  30.1 4.3 %collective-permute-start.11 = (bf16[2,2,2,1,8,1,256]{6,4,0,5,3,2,1:T(8,128)(2,1)S(1)}, bf16[2,2,2,1,8,1,256]{6,4,0,5,3,2,1:T(8,128)(2,1)S(1)}, u32[]{:S(2)}, u32[]{:S(2)}) collective-permute-start(bf16[2,2,2,1,8,1,256]{6,4,0,5,3,2,1:T(8,128)(2,1)S(1)} %copy.24), channel_id=1, source_target_pairs={{0,7},{1,6},{2,5},{3,4},{4,3},{5,2},{6,1},{7,0},{8,15},{9,14},{10,... | collective-permute-start | bytes 98312 | tf_op jit(solution)/shard_map/ppermute | solution.py:330
  31.6 3.5 %collective-permute-start.12 = (bf16[2,2,2,1,8,1,256]{6,4,0,5,3,2,1:T(8,128)(2,1)S(1)}, bf16[2,2,2,1,8,1,256]{6,4,0,5,3,2,1:T(8,128)(2,1)S(1)}, u32[]{:S(2)}, u32[]{:S(2)}) collective-permute-start(bf16[2,2,2,1,8,1,256]{6,4,0,5,3,2,1:T(8,128)(2,1)S(1)} %copy.23), channel_id=1, source_target_pairs={{0,6},{1,7},{2,4},{3,5},{4,2},{5,3},{6,0},{7,1},{8,14},{9,15},{10,... | collective-permute-start | bytes 98312 | tf_op jit(solution)/shard_map/ppermute | solution.py:330
  32.9 3.9 %collective-permute-start.13 = (bf16[2,2,2,1,8,1,256]{6,4,0,5,3,2,1:T(8,128)(2,1)S(1)}, bf16[2,2,2,1,8,1,256]{6,4,0,5,3,2,1:T(8,128)(2,1)S(1)}, u32[]{:S(2)}, u32[]{:S(2)}) collective-permute-start(bf16[2,2,2,1,8,1,256]{6,4,0,5,3,2,1:T(8,128)(2,1)S(1)} %copy.22), channel_id=1, source_target_pairs={{0,1},{1,0},{2,3},{3,2},{4,5},{5,4},{6,7},{7,6},{8,9},{9,8},{10,11... | collective-permute-start | bytes 98312 | tf_op jit(solution)/shard_map/ppermute | solution.py:330
  36.8 5.3 %collective-permute-start.14 = (f32[2,1,1,1,8,1,256]{6,4,0,5,3,2,1:T(8,128)S(1)}, f32[2,1,1,1,8,1,256]{6,4,0,5,3,2,1:T(8,128)S(1)}, u32[]{:S(2)}, u32[]{:S(2)}) collective-permute-start(f32[2,1,1,1,8,1,256]{6,4,0,5,3,2,1:T(8,128)S(1)} %get-tuple-element.40), channel_id=1, source_target_pairs={{0,26},{1,27},{2,24},{3,25},{4,30},{5,31},{6,28},{7,29},{8,18},{9,... | collective-permute-start | bytes 49160 | tf_op jit(solution)/shard_map/ppermute | solution.py:330
  36.9 5.4 %collective-permute-start.15 = (f32[2,1,1,1,8,1,256]{6,4,0,5,3,2,1:T(8,128)S(1)}, f32[2,1,1,1,8,1,256]{6,4,0,5,3,2,1:T(8,128)S(1)}, u32[]{:S(2)}, u32[]{:S(2)}) collective-permute-start(f32[2,1,1,1,8,1,256]{6,4,0,5,3,2,1:T(8,128)S(1)} %get-tuple-element.42), channel_id=1, source_target_pairs={{0,16},{1,17},{2,18},{3,19},{4,20},{5,21},{6,22},{7,23},{8,24},{9,... | collective-permute-start | bytes 49160 | tf_op jit(solution)/shard_map/ppermute | solution.py:330
  38.6 3.8 %collective-permute-start.16 = (f32[2,1,1,1,8,1,256]{6,4,0,5,3,2,1:T(8,128)S(1)}, f32[2,1,1,1,8,1,256]{6,4,0,5,3,2,1:T(8,128)S(1)}, u32[]{:S(2)}, u32[]{:S(2)}) collective-permute-start(f32[2,1,1,1,8,1,256]{6,4,0,5,3,2,1:T(8,128)S(1)} %get-tuple-element.41), channel_id=1, source_target_pairs={{0,10},{1,11},{2,8},{3,9},{4,14},{5,15},{6,12},{7,13},{8,2},{9,3},... | collective-permute-start | bytes 49160 | tf_op jit(solution)/shard_map/ppermute | solution.py:330

commit v5 on v4

--- a/solution.py
+++ b/solution.py
@@ -18,7 +18,7 @@
 
 
 def swap_rounds(sizes):
-    rounds = [(pos, phase) for pos in (0, 2) for phase in (0, 1)] + [(1, 1), (1, 0)]
+    rounds = [(2,0),(2,1),(0,0),(0,1),(1,1),(1,0)]
     return [(pos, phase) for pos, phase in rounds if sizes[pos] > 1 + phase]
 
 
@@ -27,7 +27,9 @@
     near = here[pos] + (1 if (here[pos] + phase) % 2 == 0 else -1)
     if 0 <= near < sizes[pos]:
         there[pos] = near
-    elif pos == 1 or sizes[1] % 2:
+    elif pos == 1:
+        there[0] = here[0] ^ 1
+    elif sizes[1] % 2:
         there[pos] = sizes[pos] - 1 - here[pos]
     else:
         there[1] = here[1] ^ 1
@@ -163,17 +165,26 @@
     return [(2 * pos + (half ^ tint(pos // chips, 2 * (pos % chips)))) * eb for pos in range(columns // (2 * eb))]
 
 
-def radiate_kernel(sizes, count, halves, eb, source, puts, radiation, *refs):
+def columns_kernel(part, radiation, puts, out):
+    out[...] = jnp.dot(radiation[part], puts[...], preferred_element_type=F32).astype(BF16)
+
+
+def incident_kernel(radiation, source, puts, base, out):
+    columns_kernel(1, radiation, puts, out)
+    base[...] = jnp.dot(radiation[0], source[...], preferred_element_type=F32) + jnp.dot(
+        radiation[1], turned(source[...]), preferred_element_type=F32
+    )
+
+
+def radiate_kernel(sizes, count, halves, eb, base, placed, placed_imag, *refs):
     arrived, outs = refs[:count], refs[count : count + 1 + halves]
-    values, straight, crossed = refs[count + 1 + halves :]
-    columns = source.shape[1] // 2
+    (values,) = refs[count + 1 + halves :]
+    columns = base.shape[1] // 2
     gather_values(arrived, values)
-    for part in blocks(source.shape[0]):
-        both = add_traces(puts, arrived, source, values, part)
-        straight[part, :] = both
-        crossed[part, :] = turned(both)
-    field = jnp.dot(radiation[0], straight[...], preferred_element_type=F32) + jnp.dot(
-        radiation[1], crossed[...], preferred_element_type=F32
+    field = (
+        base[...]
+        + jnp.dot(placed[...], values[...], preferred_element_type=F32)
+        + jnp.dot(placed_imag[...], turned(values[...]), preferred_element_type=F32)
     )
     along, across = lax.axis_index("gy"), lax.axis_index("gx")
     mine = (along & 1) ^ tint(across, along)
@@ -252,10 +263,38 @@
     )(response, source, puts, picks, *arrived)
 
 
-def radiate(sizes, kept, radiation, arrived, halves, eb):
-    source, puts, picks = kept[1:]
-    columns = source.shape[1] // 2
+def cost(rows, depth, columns):
+    moved = 2 * (rows * depth + depth * columns + rows * columns)
+    return pl.CostEstimate(flops=2 * rows * depth * columns, bytes_accessed=moved, transcendentals=0)
+
+
+def placed_real(radiation, puts):
+    shape = (radiation.shape[1], puts.shape[1])
+    return pl.pallas_call(
+        functools.partial(columns_kernel, 0),
+        out_shape=OUT_VMEM(shape, BF16),
+        in_specs=[vmem_spec()] * 2,
+        out_specs=vmem_spec(),
+        cost_estimate=cost(shape[0], *puts.shape),
+        compiler_params=params(),
+    )(radiation, puts)
+
+
+def placed_imag_and_incident(radiation, source, puts):
     angles = radiation.shape[1]
+    return pl.pallas_call(
+        incident_kernel,
+        out_shape=[OUT_VMEM((angles, source.shape[1]), F32), OUT_VMEM((angles, puts.shape[1]), BF16)],
+        in_specs=[vmem_spec()] * 3,
+        out_specs=[vmem_spec()] * 2,
+        cost_estimate=cost(2 * angles, *puts.shape),
+        compiler_params=params(),
+    )(radiation, source, puts)
+
+
+def radiate(sizes, base, placed, placed_imag, arrived, halves, eb):
+    columns = base.shape[1] // 2
+    angles = base.shape[0]
     count = len(arrived)
     shape = (2, columns // 2 if halves else columns, angles)
     outs = [jax.ShapeDtypeStruct(shape, F32)] * (1 + int(halves))
@@ -264,10 +303,9 @@
         out_shape=outs,
         in_specs=[vmem_spec()] * (3 + count),
         out_specs=[vmem_spec()] * len(outs),
-        scratch_shapes=[pltpu.VMEM((picks.shape[0], source.shape[1]), BF16)]
-        + [pltpu.VMEM(source.shape, BF16)] * 2,
+        scratch_shapes=[pltpu.VMEM((placed.shape[1], 2 * columns), BF16)],
         compiler_params=params(),
-    )(source, puts, radiation, *arrived)
+    )(base, placed, placed_imag, *arrived)
 
 
 def bit_count(size):
@@ -343,15 +381,21 @@
     rounds = swap_rounds(sizes)
     columns, angles = source.shape[2], radiation_mat.shape[1]
     faces, kept = first_sweep(sizes, rounds, linked[0, 0, 0], slots, source, response_mat)
+    placed = placed_real(radiation_mat, kept[2])
     for turn in range(ITERS):
+        if turn == ITERS - 1:
+            source_now, puts_now, faces = lax.optimization_barrier((kept[1], kept[2], list(faces)))
+            base, placed_imag = placed_imag_and_incident(radiation_mat, source_now, puts_now)
         arrived = [
             lax.ppermute(face, AXES, swap_pairs(sizes, pos, phase))
             for face, (pos, phase) in zip(faces, rounds)
         ]
+        if turn == 0:
+            placed, arrived = lax.optimization_barrier((placed, arrived))
         if turn < ITERS - 1:
             faces = later_sweep(kept, arrived)
     halves = sizes[1] % 2 == 0
-    parts = radiate(sizes, kept, radiation_mat, arrived, halves, columns // (sizes[0] * sizes[1]))
+    parts = radiate(sizes, base, placed, placed_imag, arrived, halves, columns // (sizes[0] * sizes[1]))
     return scatter_sum(parts, sizes, where, (columns, angles))
 
 

time: 43.2 us -> 41.7 us (0.965)
  waiting for transfers between devices: 13.5 us -> 8.62 us
  Pallas kernels: 10.3 us -> 13.4 us
    ppermute x10, waiting for transfers between devices: 7.02 us -> 2.38 us  [shards(): lax.ppermute(face, AXES, swap_pairs(sizes, pos, phase))]
    pallas_call x0 -> x2, Pallas kernels: none -> 3.71 us  [the longest x1 2.19 us: placed_imag_and_incident(): pl.pallas_call(incident_kernel, out_shape=[OUT_VMEM((angles, source.shape...]
    pallas_call x1, Pallas kernels: 1.63 us -> 0.86 us  [radiate(): pl.pallas_call(functools.partial(radiate_kernel, sizes, count, int(halves...]
  transfers between devices with their start and end apart: 17 -> 17, of which waited for: 12 -> 8; matrix products, arithmetic and copies ran while one was open for 0% -> 0% of each run, Pallas kernels for 0% -> 9%
where the time goes in v5:
time: 41.7 us; the launch traced here: 41.6 us
  starting transfers between devices  18.8 us (45%)
  Pallas kernels  13.4 us (32%)
  waiting for transfers between devices  8.62 us (21%)
  other arithmetic  0.66 us (2%)
    ppermute x10, starting transfers between devices, shards(): lax.ppermute(face, AXES, swap_pairs(sizes, pos, phase))  11.4 us
    ppermute x6, starting transfers between devices, scatter_sum(): got.append(lax.ppermute(piece, AXES, mask_pairs(sizes, flips)))  7.16 us
    pallas_call x1, Pallas kernels, first_sweep(): pl.pallas_call(functools.partial(first_kernel, sizes, rounds), out_shape=...  5.61 us
    ppermute x6, waiting for transfers between devices, scatter_sum(): got.append(lax.ppermute(piece, AXES, mask_pairs(sizes, flips)))  4.82 us
    pallas_call x1, Pallas kernels, later_sweep(): pl.pallas_call(functools.partial(sweep_kernel, count), out_shape=[jax.Sha...  3.18 us
    ppermute x10, waiting for transfers between devices, shards(): lax.ppermute(face, AXES, swap_pairs(sizes, pos, phase))  2.38 us
    pallas_call x1, Pallas kernels, placed_imag_and_incident(): pl.pallas_call(incident_kernel, out_shape=[OUT_VMEM((angles, source.shape...  2.19 us
    pallas_call x1, Pallas kernels, placed_real(): pl.pallas_call(functools.partial(columns_kernel, 0), out_shape=OUT_VMEM(s...  1.52 us
  transfers between devices with their start and end apart: 17, of which 8 were waited for; matrix products, arithmetic and copies ran while one was open for 0% of the time, Pallas kernels for 9%

profile of v5, /device:TPU:0, one launch (start us, length us, event | category | flops | bytes accessed | tf_op | source)
XLA Modules:
  0.0 41.6 jit_solution(2772989245258451714)
XLA Ops:
  0.0 5.6 %shard_map.55 = (bf16[192,256]{1,0:T(8,128)(2,1)S(1)}, bf16[192,256]{1,0:T(8,128)(2,1)S(1)}, bf16[192,256]{1,0:T(8,128)(2,1)S(1)}, bf16[192,256]{1,0:T(8,128)(2,...) custom-call(s32[6]{0:T(128)} %bitcast.15, ...), custom_call_target="tpu_custom_call" | custom-call | tf_op jit(solution)/shard_map/pallas_call | solution.py:233
  5.6 3.0 %collective-permute-start = (bf16[192,256]{1,0:T(8,128)(2,1)S(1)}, bf16[192,256]{1,0:T(8,128)(2,1)S(1)}, u32[]{:S(2)}, u32[]{:S(2)}) collective-permute-start(bf16[192,256]{1,0:T(8,128)(2,1)S(1)} %get-tuple-element.40), channel_id=1, source_target_pairs={{0,1},{1,0},{2,3},{3,2},{4,5},{5,4},{6,7},{7,6},{8,9},{9,8},{10,11... | collective-permute-start | bytes 294920 | tf_op jit(solution)/shard_map/ppermute | solution.py:390
  8.6 1.6 %collective-permute-start.1 = (bf16[192,256]{1,0:T(8,128)(2,1)S(1)}, bf16[192,256]{1,0:T(8,128)(2,1)S(1)}, u32[]{:S(2)}, u32[]{:S(2)}) collective-permute-start(bf16[192,256]{1,0:T(8,128)(2,1)S(1)} %get-tuple-element.41), channel_id=1, source_target_pairs={{0,8},{1,9},{2,10},{3,11},{4,12},{5,13},{6,14},{7,15},{8,0},{9,1},... | collective-permute-start | bytes 294920 | tf_op jit(solution)/shard_map/ppermute | solution.py:390
  10.2 3.1 %collective-permute-start.3 = (bf16[192,256]{1,0:T(8,128)(2,1)S(1)}, bf16[192,256]{1,0:T(8,128)(2,1)S(1)}, u32[]{:S(2)}, u32[]{:S(2)}) collective-permute-start(bf16[192,256]{1,0:T(8,128)(2,1)S(1)} %get-tuple-element.43), channel_id=1, source_target_pairs={{0,8},{1,9},{2,4},{3,5},{4,2},{5,3},{6,14},{7,15},{8,0},{9,1},{10,... | collective-permute-start | bytes 294920 | tf_op jit(solution)/shard_map/ppermute | solution.py:390
  13.4 1.5 %shard_map.56.placed = bf16[512,960]{1,0:T(8,128)(2,1)S(1)} custom-call(bf16[2,512,1280]{2,1,0:T(8,128)(2,1)S(1)} %bitcast.8, bf16[1280,960]{1,0:T(8,128)(2,1)S(1)} %get-tuple-element.56.puts), custom_call_target="tpu_custom_call" | custom-call | flops 1258291200 | bytes 4751360 | tf_op jit(solution)/shard_map/pallas_call | solution.py:273
  14.9 1.0 %collective-permute-done.3.refs_3_ = bf16[192,256]{1,0:T(8,128)(2,1)S(1)} collective-permute-done((bf16[192,256]{1,0:T(8,128)(2,1)S(1)}, bf16[192,256]{1,0:T(8,128)(2,1)S(1)}, u32[]{:S(2)}, u32[]{:S(2)}) %collective-permute-start.3) | collective-permute-done | bytes 98336 | tf_op jit(solution)/shard_map/ppermute | solution.py:390
  15.9 3.2 %shard_map.57 = (bf16[192,256]{1,0:T(8,128)(2,1)S(1)}, bf16[192,256]{1,0:T(8,128)(2,1)S(1)}, bf16[192,256]{1,0:T(8,128)(2,1)S(1)}, bf16[192,256]{1,0:T(8,128)(2,1)S(1)}, bf16[192,256]{1,0:T(8,128)(2,1)S(1)}) custom-call(bf16[2,1280,1280]{2,1,0:T(8,128)(2,1)S(1)} %get-tuple-element.38.response, bf16[1280,256]{1,0:T(8,128)(2,1)S(1)} %get-tuple-element.55.source, ...), custom_call_target="tpu_custom_call" | custom-call | tf_op jit(solution)/shard_map/pallas_call | solution.py:255
  19.1 0.6 %collective-permute-start.5 = (bf16[192,256]{1,0:T(8,128)(2,1)S(1)}, bf16[192,256]{1,0:T(8,128)(2,1)S(1)}, u32[]{:S(2)}, u32[]{:S(2)}) collective-permute-start(bf16[192,256]{1,0:T(8,128)(2,1)S(1)} %get-tuple-element.60), channel_id=1, source_target_pairs={{0,1},{1,0},{2,3},{3,2},{4,5},{5,4},{6,7},{7,6},{8,9},{9,8},{10,11... | collective-permute-start | bytes 294920 | tf_op jit(solution)/shard_map/ppermute | solution.py:390
  19.7 2.0 %collective-permute-start.6 = (bf16[192,256]{1,0:T(8,128)(2,1)S(1)}, bf16[192,256]{1,0:T(8,128)(2,1)S(1)}, u32[]{:S(2)}, u32[]{:S(2)}) collective-permute-start(bf16[192,256]{1,0:T(8,128)(2,1)S(1)} %get-tuple-element.61), channel_id=1, source_target_pairs={{0,8},{1,9},{2,10},{3,11},{4,12},{5,13},{6,14},{7,15},{8,0},{9,1},... | collective-permute-start | bytes 294920 | tf_op jit(solution)/shard_map/ppermute | solution.py:390
  21.8 1.1 %collective-permute-start.8 = (bf16[192,256]{1,0:T(8,128)(2,1)S(1)}, bf16[192,256]{1,0:T(8,128)(2,1)S(1)}, u32[]{:S(2)}, u32[]{:S(2)}) collective-permute-start(bf16[192,256]{1,0:T(8,128)(2,1)S(1)} %get-tuple-element.63), channel_id=1, source_target_pairs={{0,8},{1,9},{2,4},{3,5},{4,2},{5,3},{6,14},{7,15},{8,0},{9,1},{10,... | collective-permute-start | bytes 294920 | tf_op jit(solution)/shard_map/ppermute | solution.py:390
  22.8 2.2 %shard_map.58 = (f32[512,256]{1,0:T(8,128)S(1)}, bf16[512,960]{1,0:T(8,128)(2,1)S(1)}) custom-call(bf16[2,512,1280]{2,1,0:T(8,128)(2,1)S(1)} %bitcast.9, bf16[1280,256]{1,0:T(8,128)(2,1)S(1)} %get-tuple-element.55.source, bf16[1280,960]{1,0:T(8,128)(2,1)S(1)} %get-tuple-element.56.puts), custom_call_target="tpu_custom_call" | custom-call | flops 2516582400 | bytes 7045120 | tf_op jit(solution)/shard_map/pallas_call | solution.py:285
  25.1 1.3 %collective-permute-done.8.refs_3_ = bf16[192,256]{1,0:T(8,128)(2,1)S(1)} collective-permute-done((bf16[192,256]{1,0:T(8,128)(2,1)S(1)}, bf16[192,256]{1,0:T(8,128)(2,1)S(1)}, u32[]{:S(2)}, u32[]{:S(2)}) %collective-permute-start.8) | collective-permute-done | bytes 98336 | tf_op jit(solution)/shard_map/ppermute | solution.py:390
  26.4 0.9 %shard_map.59 = (f32[2,64,512]{2,1,0:T(8,128)S(1)}, f32[2,64,512]{2,1,0:T(8,128)S(1)}) custom-call(f32[512,256]{1,0:T(8,128)S(1)} %get-tuple-element.57.base, bf16[512,960]{1,0:T(8,128)(2,1)S(1)} %shard_map.56.placed, bf16[512,960]{1,0:T(8,128)(2,1)S(1)} %get-tuple-element.59.placed_imag, bf16[192,256]{1,0:T(8,128)(2,1)S(1)} %collective-permute-done.5.refs_0_, ...), custom_call_target="tpu_custom_call" | custom-call | tf_op jit(solution)/shard_map/pallas_call | solution.py:301
  27.4 1.4 %collective-permute-done.10 = f32[2,64,512]{2,1,0:T(8,128)S(1)} collective-permute-done((f32[2,64,512]{2,1,0:T(8,128)S(1)}, f32[2,64,512]{2,1,0:T(8,128)S(1)}, u32[]{:S(2)}, u32[]{:S(2)}) %collective-permute-start.10) | collective-permute-done | bytes 262176 | tf_op jit(solution)/shard_map/ppermute | solution.py:345
  28.9 1.1 %collective-permute-start.11 = (bf16[2,2,2,1,8,1,256]{6,4,0,5,3,2,1:T(8,128)(2,1)S(1)}, bf16[2,2,2,1,8,1,256]{6,4,0,5,3,2,1:T(8,128)(2,1)S(1)}, u32[]{:S(2)}, u32[]{:S(2)}) collective-permute-start(bf16[2,2,2,1,8,1,256]{6,4,0,5,3,2,1:T(8,128)(2,1)S(1)} %copy.24), channel_id=1, source_target_pairs={{0,7},{1,6},{2,5},{3,4},{4,3},{5,2},{6,1},{7,0},{8,15},{9,14},{10,... | collective-permute-start | bytes 98312 | tf_op jit(solution)/shard_map/ppermute | solution.py:368
  30.1 1.6 %collective-permute-start.12 = (bf16[2,2,2,1,8,1,256]{6,4,0,5,3,2,1:T(8,128)(2,1)S(1)}, bf16[2,2,2,1,8,1,256]{6,4,0,5,3,2,1:T(8,128)(2,1)S(1)}, u32[]{:S(2)}, u32[]{:S(2)}) collective-permute-start(bf16[2,2,2,1,8,1,256]{6,4,0,5,3,2,1:T(8,128)(2,1)S(1)} %copy.23), channel_id=1, source_target_pairs={{0,6},{1,7},{2,4},{3,5},{4,2},{5,3},{6,0},{7,1},{8,14},{9,15},{10,... | collective-permute-start | bytes 98312 | tf_op jit(solution)/shard_map/ppermute | solution.py:368
  31.7 0.5 %collective-permute-start.13 = (bf16[2,2,2,1,8,1,256]{6,4,0,5,3,2,1:T(8,128)(2,1)S(1)}, bf16[2,2,2,1,8,1,256]{6,4,0,5,3,2,1:T(8,128)(2,1)S(1)}, u32[]{:S(2)}, u32[]{:S(2)}) collective-permute-start(bf16[2,2,2,1,8,1,256]{6,4,0,5,3,2,1:T(8,128)(2,1)S(1)} %copy.22), channel_id=1, source_target_pairs={{0,1},{1,0},{2,3},{3,2},{4,5},{5,4},{6,7},{7,6},{8,9},{9,8},{10,11... | collective-permute-start | bytes 98312 | tf_op jit(solution)/shard_map/ppermute | solution.py:368
  32.2 1.1 %collective-permute-done.11 = bf16[2,2,2,1,8,1,256]{6,4,0,5,3,2,1:T(8,128)(2,1)S(1)} collective-permute-done((bf16[2,2,2,1,8,1,256]{6,4,0,5,3,2,1:T(8,128)(2,1)S(1)}, bf16[2,2,2,1,8,1,256]{6,4,0,5,3,2,1:T(8,128)(2,1)S(1)}, u32[]{:S(2)}, u32[]{:S(2)}) %collective-permute-start.11) | collective-permute-done | bytes 32800 | tf_op jit(solution)/shard_map/ppermute | solution.py:368
  33.3 0.9 %collective-permute-done.12 = bf16[2,2,2,1,8,1,256]{6,4,0,5,3,2,1:T(8,128)(2,1)S(1)} collective-permute-done((bf16[2,2,2,1,8,1,256]{6,4,0,5,3,2,1:T(8,128)(2,1)S(1)}, bf16[2,2,2,1,8,1,256]{6,4,0,5,3,2,1:T(8,128)(2,1)S(1)}, u32[]{:S(2)}, u32[]{:S(2)}) %collective-permute-start.12) | collective-permute-done | bytes 32800 | tf_op jit(solution)/shard_map/ppermute | solution.py:368
  34.3 1.4 %collective-permute-done.13 = bf16[2,2,2,1,8,1,256]{6,4,0,5,3,2,1:T(8,128)(2,1)S(1)} collective-permute-done((bf16[2,2,2,1,8,1,256]{6,4,0,5,3,2,1:T(8,128)(2,1)S(1)}, bf16[2,2,2,1,8,1,256]{6,4,0,5,3,2,1:T(8,128)(2,1)S(1)}, u32[]{:S(2)}, u32[]{:S(2)}) %collective-permute-start.13) | collective-permute-done | bytes 32800 | tf_op jit(solution)/shard_map/ppermute | solution.py:368
  35.7 1.5 %collective-permute-start.15 = (f32[2,1,1,1,8,1,256]{6,4,0,5,3,2,1:T(8,128)S(1)}, f32[2,1,1,1,8,1,256]{6,4,0,5,3,2,1:T(8,128)S(1)}, u32[]{:S(2)}, u32[]{:S(2)}) collective-permute-start(f32[2,1,1,1,8,1,256]{6,4,0,5,3,2,1:T(8,128)S(1)} %get-tuple-element.72), channel_id=1, source_target_pairs={{0,16},{1,17},{2,18},{3,19},{4,20},{5,21},{6,22},{7,23},{8,24},{9,... | collective-permute-start | bytes 49160 | tf_op jit(solution)/shard_map/ppermute | solution.py:368
  37.3 2.3 %collective-permute-start.16 = (f32[2,1,1,1,8,1,256]{6,4,0,5,3,2,1:T(8,128)S(1)}, f32[2,1,1,1,8,1,256]{6,4,0,5,3,2,1:T(8,128)S(1)}, u32[]{:S(2)}, u32[]{:S(2)}) collective-permute-start(f32[2,1,1,1,8,1,256]{6,4,0,5,3,2,1:T(8,128)S(1)} %get-tuple-element.71), channel_id=1, source_target_pairs={{0,10},{1,11},{2,8},{3,9},{4,14},{5,15},{6,12},{7,13},{8,2},{9,3},... | collective-permute-start | bytes 49160 | tf_op jit(solution)/shard_map/ppermute | solution.py:368
  39.5 1.2 %collective-permute-done.14 = f32[2,1,1,1,8,1,256]{6,4,0,5,3,2,1:T(8,128)S(1)} collective-permute-done((f32[2,1,1,1,8,1,256]{6,4,0,5,3,2,1:T(8,128)S(1)}, f32[2,1,1,1,8,1,256]{6,4,0,5,3,2,1:T(8,128)S(1)}, u32[]{:S(2)}, u32[]{:S(2)}) %collective-permute-start.14) | collective-permute-done | bytes 16416 | tf_op jit(solution)/shard_map/ppermute | solution.py:368
  41.0 0.6 %add_bitcast_fusion = f32[2,8,256]{2,1,0:T(8,128)} fusion(f32[2,1,1,1,8,1,256]{6,4,0,5,3,2,1:T(8,128)S(1)} %collective-permute-done.16, f32[2,1,1,1,8,1,256]{6,4,0,5,3,2,1:T(8,128)S(1)} %collective-permute-done.15, f32[2,1,1,1,8,1,256]{6,4,0,5,3,2,1:T(8,128)S(1)} %collective-permute-done.14, f32[2,2,2,1,8,1,256]{6,4,0,5,3,2,1:T(8,128)S(1)} %fusion.1, ...), kind=kLoop, calls=%fused_computation.6 | loop fusion | flops 12288 | bytes 81928 | tf_op jit(solution)/shard_map/reshape | solution.py:372
  (25 shorter events, 0.6 us)
Async XLA Ops:
  0.0 13.4 %copy-start = (bf16[1,1,1,2,512,1280]{5,4,3,2,1,0:T(8,128)(2,1)S(1)}, bf16[1,1,1,2,512,1280]{5,4,3,2,1,0:T(8,128)(2,1)}, u32[]{:S(2)}) copy-start(bf16[1,1,1,2,512,1280]{5,4,3,2,1,0:T(8,128)(2,1)} %param.7) | copy-start | bytes 7864324
  5.6 9.3 %collective-permute-start = (bf16[192,256]{1,0:T(8,128)(2,1)S(1)}, bf16[192,256]{1,0:T(8,128)(2,1)S(1)}, u32[]{:S(2)}, u32[]{:S(2)}) collective-permute-start(bf16[192,256]{1,0:T(8,128)(2,1)S(1)} %get-tuple-element.40), channel_id=1, source_target_pairs={{0,1},{1,0},{2,3},{3,2},{4,5},{5,4},{6,7},{7,6},{8,9},{9,8},{10,11... | collective-permute-start | bytes 294920 | tf_op jit(solution)/shard_map/ppermute | solution.py:390
  8.6 6.3 %collective-permute-start.1 = (bf16[192,256]{1,0:T(8,128)(2,1)S(1)}, bf16[192,256]{1,0:T(8,128)(2,1)S(1)}, u32[]{:S(2)}, u32[]{:S(2)}) collective-permute-start(bf16[192,256]{1,0:T(8,128)(2,1)S(1)} %get-tuple-element.41), channel_id=1, source_target_pairs={{0,8},{1,9},{2,10},{3,11},{4,12},{5,13},{6,14},{7,15},{8,0},{9,1},... | collective-permute-start | bytes 294920 | tf_op jit(solution)/shard_map/ppermute | solution.py:390
  10.2 4.7 %collective-permute-start.2 = (bf16[192,256]{1,0:T(8,128)(2,1)S(1)}, bf16[192,256]{1,0:T(8,128)(2,1)S(1)}, u32[]{:S(2)}, u32[]{:S(2)}) collective-permute-start(bf16[192,256]{1,0:T(8,128)(2,1)S(1)} %get-tuple-element.42), channel_id=1, source_target_pairs={{0,2},{1,3},{2,0},{3,1},{4,6},{5,7},{6,4},{7,5},{8,16},{9,17},{10,... | collective-permute-start | bytes 294920 | tf_op jit(solution)/shard_map/ppermute | solution.py:390
  10.2 5.7 %collective-permute-start.3 = (bf16[192,256]{1,0:T(8,128)(2,1)S(1)}, bf16[192,256]{1,0:T(8,128)(2,1)S(1)}, u32[]{:S(2)}, u32[]{:S(2)}) collective-permute-start(bf16[192,256]{1,0:T(8,128)(2,1)S(1)} %get-tuple-element.43), channel_id=1, source_target_pairs={{0,8},{1,9},{2,4},{3,5},{4,2},{5,3},{6,14},{7,15},{8,0},{9,1},{10,... | collective-permute-start | bytes 294920 | tf_op jit(solution)/shard_map/ppermute | solution.py:390
  13.4 2.6 %collective-permute-start.4 = (bf16[192,256]{1,0:T(8,128)(2,1)S(1)}, bf16[192,256]{1,0:T(8,128)(2,1)S(1)}, u32[]{:S(2)}, u32[]{:S(2)}) collective-permute-start(bf16[192,256]{1,0:T(8,128)(2,1)S(1)} %get-tuple-element.44), channel_id=1, source_target_pairs={{0,2},{1,3},{2,0},{3,1},{4,6},{5,7},{6,4},{7,5},{8,10},{9,11},{10,... | collective-permute-start | bytes 294920 | tf_op jit(solution)/shard_map/ppermute | solution.py:390
  19.1 5.9 %collective-permute-start.5 = (bf16[192,256]{1,0:T(8,128)(2,1)S(1)}, bf16[192,256]{1,0:T(8,128)(2,1)S(1)}, u32[]{:S(2)}, u32[]{:S(2)}) collective-permute-start(bf16[192,256]{1,0:T(8,128)(2,1)S(1)} %get-tuple-element.60), channel_id=1, source_target_pairs={{0,1},{1,0},{2,3},{3,2},{4,5},{5,4},{6,7},{7,6},{8,9},{9,8},{10,11... | collective-permute-start | bytes 294920 | tf_op jit(solution)/shard_map/ppermute | solution.py:390
  19.7 5.3 %collective-permute-start.6 = (bf16[192,256]{1,0:T(8,128)(2,1)S(1)}, bf16[192,256]{1,0:T(8,128)(2,1)S(1)}, u32[]{:S(2)}, u32[]{:S(2)}) collective-permute-start(bf16[192,256]{1,0:T(8,128)(2,1)S(1)} %get-tuple-element.61), channel_id=1, source_target_pairs={{0,8},{1,9},{2,10},{3,11},{4,12},{5,13},{6,14},{7,15},{8,0},{9,1},... | collective-permute-start | bytes 294920 | tf_op jit(solution)/shard_map/ppermute | solution.py:390
  21.8 3.3 %collective-permute-start.7 = (bf16[192,256]{1,0:T(8,128)(2,1)S(1)}, bf16[192,256]{1,0:T(8,128)(2,1)S(1)}, u32[]{:S(2)}, u32[]{:S(2)}) collective-permute-start(bf16[192,256]{1,0:T(8,128)(2,1)S(1)} %get-tuple-element.62), channel_id=1, source_target_pairs={{0,2},{1,3},{2,0},{3,1},{4,6},{5,7},{6,4},{7,5},{8,16},{9,17},{10,... | collective-permute-start | bytes 294920 | tf_op jit(solution)/shard_map/ppermute | solution.py:390
  21.8 4.6 %collective-permute-start.8 = (bf16[192,256]{1,0:T(8,128)(2,1)S(1)}, bf16[192,256]{1,0:T(8,128)(2,1)S(1)}, u32[]{:S(2)}, u32[]{:S(2)}) collective-permute-start(bf16[192,256]{1,0:T(8,128)(2,1)S(1)} %get-tuple-element.63), channel_id=1, source_target_pairs={{0,8},{1,9},{2,4},{3,5},{4,2},{5,3},{6,14},{7,15},{8,0},{9,1},{10,... | collective-permute-start | bytes 294920 | tf_op jit(solution)/shard_map/ppermute | solution.py:390
  22.8 3.6 %collective-permute-start.9 = (bf16[192,256]{1,0:T(8,128)(2,1)S(1)}, bf16[192,256]{1,0:T(8,128)(2,1)S(1)}, u32[]{:S(2)}, u32[]{:S(2)}) collective-permute-start(bf16[192,256]{1,0:T(8,128)(2,1)S(1)} %get-tuple-element.64), channel_id=1, source_target_pairs={{0,2},{1,3},{2,0},{3,1},{4,6},{5,7},{6,4},{7,5},{8,10},{9,11},{10,... | collective-permute-start | bytes 294920 | tf_op jit(solution)/shard_map/ppermute | solution.py:390
  27.3 1.6 %collective-permute-start.10 = (f32[2,64,512]{2,1,0:T(8,128)S(1)}, f32[2,64,512]{2,1,0:T(8,128)S(1)}, u32[]{:S(2)}, u32[]{:S(2)}) collective-permute-start(f32[2,64,512]{2,1,0:T(8,128)S(1)} %get-tuple-element.66), channel_id=1, source_target_pairs={{0,2},{1,3},{2,0},{3,1},{4,6},{5,7},{6,4},{7,5},{8,10},{9,11},{10,... | collective-permute-start | bytes 786440 | tf_op jit(solution)/shard_map/ppermute | solution.py:345
  28.9 4.4 %collective-permute-start.11 = (bf16[2,2,2,1,8,1,256]{6,4,0,5,3,2,1:T(8,128)(2,1)S(1)}, bf16[2,2,2,1,8,1,256]{6,4,0,5,3,2,1:T(8,128)(2,1)S(1)}, u32[]{:S(2)}, u32[]{:S(2)}) collective-permute-start(bf16[2,2,2,1,8,1,256]{6,4,0,5,3,2,1:T(8,128)(2,1)S(1)} %copy.24), channel_id=1, source_target_pairs={{0,7},{1,6},{2,5},{3,4},{4,3},{5,2},{6,1},{7,0},{8,15},{9,14},{10,... | collective-permute-start | bytes 98312 | tf_op jit(solution)/shard_map/ppermute | solution.py:368
  30.1 4.2 %collective-permute-start.12 = (bf16[2,2,2,1,8,1,256]{6,4,0,5,3,2,1:T(8,128)(2,1)S(1)}, bf16[2,2,2,1,8,1,256]{6,4,0,5,3,2,1:T(8,128)(2,1)S(1)}, u32[]{:S(2)}, u32[]{:S(2)}) collective-permute-start(bf16[2,2,2,1,8,1,256]{6,4,0,5,3,2,1:T(8,128)(2,1)S(1)} %copy.23), channel_id=1, source_target_pairs={{0,6},{1,7},{2,4},{3,5},{4,2},{5,3},{6,0},{7,1},{8,14},{9,15},{10,... | collective-permute-start | bytes 98312 | tf_op jit(solution)/shard_map/ppermute | solution.py:368
  31.7 3.9 %collective-permute-start.13 = (bf16[2,2,2,1,8,1,256]{6,4,0,5,3,2,1:T(8,128)(2,1)S(1)}, bf16[2,2,2,1,8,1,256]{6,4,0,5,3,2,1:T(8,128)(2,1)S(1)}, u32[]{:S(2)}, u32[]{:S(2)}) collective-permute-start(bf16[2,2,2,1,8,1,256]{6,4,0,5,3,2,1:T(8,128)(2,1)S(1)} %copy.22), channel_id=1, source_target_pairs={{0,1},{1,0},{2,3},{3,2},{4,5},{5,4},{6,7},{7,6},{8,9},{9,8},{10,11... | collective-permute-start | bytes 98312 | tf_op jit(solution)/shard_map/ppermute | solution.py:368
  35.6 5.1 %collective-permute-start.14 = (f32[2,1,1,1,8,1,256]{6,4,0,5,3,2,1:T(8,128)S(1)}, f32[2,1,1,1,8,1,256]{6,4,0,5,3,2,1:T(8,128)S(1)}, u32[]{:S(2)}, u32[]{:S(2)}) collective-permute-start(f32[2,1,1,1,8,1,256]{6,4,0,5,3,2,1:T(8,128)S(1)} %get-tuple-element.70), channel_id=1, source_target_pairs={{0,26},{1,27},{2,24},{3,25},{4,30},{5,31},{6,28},{7,29},{8,18},{9,... | collective-permute-start | bytes 49160 | tf_op jit(solution)/shard_map/ppermute | solution.py:368
  35.7 5.1 %collective-permute-start.15 = (f32[2,1,1,1,8,1,256]{6,4,0,5,3,2,1:T(8,128)S(1)}, f32[2,1,1,1,8,1,256]{6,4,0,5,3,2,1:T(8,128)S(1)}, u32[]{:S(2)}, u32[]{:S(2)}) collective-permute-start(f32[2,1,1,1,8,1,256]{6,4,0,5,3,2,1:T(8,128)S(1)} %get-tuple-element.72), channel_id=1, source_target_pairs={{0,16},{1,17},{2,18},{3,19},{4,20},{5,21},{6,22},{7,23},{8,24},{9,... | collective-permute-start | bytes 49160 | tf_op jit(solution)/shard_map/ppermute | solution.py:368
  37.3 3.7 %collective-permute-start.16 = (f32[2,1,1,1,8,1,256]{6,4,0,5,3,2,1:T(8,128)S(1)}, f32[2,1,1,1,8,1,256]{6,4,0,5,3,2,1:T(8,128)S(1)}, u32[]{:S(2)}, u32[]{:S(2)}) collective-permute-start(f32[2,1,1,1,8,1,256]{6,4,0,5,3,2,1:T(8,128)S(1)} %get-tuple-element.71), channel_id=1, source_target_pairs={{0,10},{1,11},{2,8},{3,9},{4,14},{5,15},{6,12},{7,13},{8,2},{9,3},... | collective-permute-start | bytes 49160 | tf_op jit(solution)/shard_map/ppermute | solution.py:368

commit v6 on v5

--- a/solution.py
+++ b/solution.py
@@ -18,7 +18,7 @@
 
 
 def swap_rounds(sizes):
-    rounds = [(2,0),(2,1),(0,0),(0,1),(1,1),(1,0)]
+    rounds = [(2, 0), (2, 1), (0, 0), (0, 1), (1, 1), (1, 0)]
     return [(pos, phase) for pos, phase in rounds if sizes[pos] > 1 + phase]
 
 
@@ -157,7 +157,7 @@
 
 
 def tint(at_x, at_y):
-    return (at_x ^ (at_y >> 1)) & 1
+    return ((at_x >> 1) ^ (at_y >> 1)) & 1
 
 
 def half_starts(sizes, half, eb, columns):
@@ -344,8 +344,7 @@
     if halves:
         total = total + lax.ppermute(parts[1], AXES, mask_pairs(sizes, (0, 1, 0)))
     total = total.reshape(shape)
-    rest = [item for item in dims if item[0] != 0]
-    rest = sorted(rest, key=lambda item: (item[1], item[0])) + sorted(item for item in dims if item[0] == 0)
+    rest = sorted(item for item in dims if item[0] != 0) + sorted((item for item in dims if item[0] == 0), reverse=True)
     rounds = [rest[pos : pos + 2] for pos in range(0, len(rest), 2)]
     for order, group in enumerate(rounds):
         wide = order == len(rounds) - 1

time: 41.7 us -> 40.9 us (0.981)
  waiting for transfers between devices: 8.62 us -> 8.01 us
    ppermute x6, waiting for transfers between devices: 4.82 us -> 4.21 us  [scatter_sum(): got.append(lax.ppermute(piece, AXES, mask_pairs(sizes, flips)))]
  transfers between devices with their start and end apart: 17 -> 17, of which waited for: 8 -> 9; matrix products, arithmetic and copies ran while one was open for 0% -> 0% of each run, Pallas kernels for 9% -> 9%
where the time goes in v6:
time: 40.9 us; the launch traced here: 40.7 us
  starting transfers between devices  18.5 us (45%)
  Pallas kernels  13.4 us (33%)
  waiting for transfers between devices  8.01 us (20%)
  other arithmetic  0.67 us (2%)
    ppermute x10, starting transfers between devices, shards(): lax.ppermute(face, AXES, swap_pairs(sizes, pos, phase))  11.4 us
    ppermute x6, starting transfers between devices, scatter_sum(): got.append(lax.ppermute(piece, AXES, mask_pairs(sizes, flips)))  6.92 us
    pallas_call x1, Pallas kernels, first_sweep(): pl.pallas_call(functools.partial(first_kernel, sizes, rounds), out_shape=...  5.61 us
    ppermute x6, waiting for transfers between devices, scatter_sum(): got.append(lax.ppermute(piece, AXES, mask_pairs(sizes, flips)))  4.21 us
    pallas_call x1, Pallas kernels, later_sweep(): pl.pallas_call(functools.partial(sweep_kernel, count), out_shape=[jax.Sha...  3.18 us
    ppermute x10, waiting for transfers between devices, shards(): lax.ppermute(face, AXES, swap_pairs(sizes, pos, phase))  2.38 us
    pallas_call x1, Pallas kernels, placed_imag_and_incident(): pl.pallas_call(incident_kernel, out_shape=[OUT_VMEM((angles, source.shape...  2.19 us
    pallas_call x1, Pallas kernels, placed_real(): pl.pallas_call(functools.partial(columns_kernel, 0), out_shape=OUT_VMEM(s...  1.52 us
  transfers between devices with their start and end apart: 17, of which 9 were waited for; matrix products, arithmetic and copies ran while one was open for 0% of the time, Pallas kernels for 9%

profile of v6, /device:TPU:0, one launch (start us, length us, event | category | flops | bytes accessed | tf_op | source)
XLA Modules:
  0.0 40.7 jit_solution(3486047208519593221)
XLA Ops:
  0.0 5.6 %shard_map.55 = (bf16[192,256]{1,0:T(8,128)(2,1)S(1)}, bf16[192,256]{1,0:T(8,128)(2,1)S(1)}, bf16[192,256]{1,0:T(8,128)(2,1)S(1)}, bf16[192,256]{1,0:T(8,128)(2,...) custom-call(s32[6]{0:T(128)} %bitcast.15, ...), custom_call_target="tpu_custom_call" | custom-call | tf_op jit(solution)/shard_map/pallas_call | solution.py:233
  5.6 3.0 %collective-permute-start = (bf16[192,256]{1,0:T(8,128)(2,1)S(1)}, bf16[192,256]{1,0:T(8,128)(2,1)S(1)}, u32[]{:S(2)}, u32[]{:S(2)}) collective-permute-start(bf16[192,256]{1,0:T(8,128)(2,1)S(1)} %get-tuple-element.40), channel_id=1, source_target_pairs={{0,1},{1,0},{2,3},{3,2},{4,5},{5,4},{6,7},{7,6},{8,9},{9,8},{10,11... | collective-permute-start | bytes 294920 | tf_op jit(solution)/shard_map/ppermute | solution.py:389
  8.6 1.6 %collective-permute-start.1 = (bf16[192,256]{1,0:T(8,128)(2,1)S(1)}, bf16[192,256]{1,0:T(8,128)(2,1)S(1)}, u32[]{:S(2)}, u32[]{:S(2)}) collective-permute-start(bf16[192,256]{1,0:T(8,128)(2,1)S(1)} %get-tuple-element.41), channel_id=1, source_target_pairs={{0,8},{1,9},{2,10},{3,11},{4,12},{5,13},{6,14},{7,15},{8,0},{9,1},... | collective-permute-start | bytes 294920 | tf_op jit(solution)/shard_map/ppermute | solution.py:389
  10.2 3.1 %collective-permute-start.3 = (bf16[192,256]{1,0:T(8,128)(2,1)S(1)}, bf16[192,256]{1,0:T(8,128)(2,1)S(1)}, u32[]{:S(2)}, u32[]{:S(2)}) collective-permute-start(bf16[192,256]{1,0:T(8,128)(2,1)S(1)} %get-tuple-element.43), channel_id=1, source_target_pairs={{0,8},{1,9},{2,4},{3,5},{4,2},{5,3},{6,14},{7,15},{8,0},{9,1},{10,... | collective-permute-start | bytes 294920 | tf_op jit(solution)/shard_map/ppermute | solution.py:389
  13.4 1.5 %shard_map.56.placed = bf16[512,960]{1,0:T(8,128)(2,1)S(1)} custom-call(bf16[2,512,1280]{2,1,0:T(8,128)(2,1)S(1)} %bitcast.8, bf16[1280,960]{1,0:T(8,128)(2,1)S(1)} %get-tuple-element.56.puts), custom_call_target="tpu_custom_call" | custom-call | flops 1258291200 | bytes 4751360 | tf_op jit(solution)/shard_map/pallas_call | solution.py:273
  14.9 1.0 %collective-permute-done.3.refs_3_ = bf16[192,256]{1,0:T(8,128)(2,1)S(1)} collective-permute-done((bf16[192,256]{1,0:T(8,128)(2,1)S(1)}, bf16[192,256]{1,0:T(8,128)(2,1)S(1)}, u32[]{:S(2)}, u32[]{:S(2)}) %collective-permute-start.3) | collective-permute-done | bytes 98336 | tf_op jit(solution)/shard_map/ppermute | solution.py:389
  15.9 3.2 %shard_map.57 = (bf16[192,256]{1,0:T(8,128)(2,1)S(1)}, bf16[192,256]{1,0:T(8,128)(2,1)S(1)}, bf16[192,256]{1,0:T(8,128)(2,1)S(1)}, bf16[192,256]{1,0:T(8,128)(2,1)S(1)}, bf16[192,256]{1,0:T(8,128)(2,1)S(1)}) custom-call(bf16[2,1280,1280]{2,1,0:T(8,128)(2,1)S(1)} %get-tuple-element.38.response, bf16[1280,256]{1,0:T(8,128)(2,1)S(1)} %get-tuple-element.55.source, ...), custom_call_target="tpu_custom_call" | custom-call | tf_op jit(solution)/shard_map/pallas_call | solution.py:255
  19.1 0.6 %collective-permute-start.5 = (bf16[192,256]{1,0:T(8,128)(2,1)S(1)}, bf16[192,256]{1,0:T(8,128)(2,1)S(1)}, u32[]{:S(2)}, u32[]{:S(2)}) collective-permute-start(bf16[192,256]{1,0:T(8,128)(2,1)S(1)} %get-tuple-element.60), channel_id=1, source_target_pairs={{0,1},{1,0},{2,3},{3,2},{4,5},{5,4},{6,7},{7,6},{8,9},{9,8},{10,11... | collective-permute-start | bytes 294920 | tf_op jit(solution)/shard_map/ppermute | solution.py:389
  19.7 2.0 %collective-permute-start.6 = (bf16[192,256]{1,0:T(8,128)(2,1)S(1)}, bf16[192,256]{1,0:T(8,128)(2,1)S(1)}, u32[]{:S(2)}, u32[]{:S(2)}) collective-permute-start(bf16[192,256]{1,0:T(8,128)(2,1)S(1)} %get-tuple-element.61), channel_id=1, source_target_pairs={{0,8},{1,9},{2,10},{3,11},{4,12},{5,13},{6,14},{7,15},{8,0},{9,1},... | collective-permute-start | bytes 294920 | tf_op jit(solution)/shard_map/ppermute | solution.py:389
  21.8 1.1 %collective-permute-start.8 = (bf16[192,256]{1,0:T(8,128)(2,1)S(1)}, bf16[192,256]{1,0:T(8,128)(2,1)S(1)}, u32[]{:S(2)}, u32[]{:S(2)}) collective-permute-start(bf16[192,256]{1,0:T(8,128)(2,1)S(1)} %get-tuple-element.63), channel_id=1, source_target_pairs={{0,8},{1,9},{2,4},{3,5},{4,2},{5,3},{6,14},{7,15},{8,0},{9,1},{10,... | collective-permute-start | bytes 294920 | tf_op jit(solution)/shard_map/ppermute | solution.py:389
  22.8 2.2 %shard_map.58 = (f32[512,256]{1,0:T(8,128)S(1)}, bf16[512,960]{1,0:T(8,128)(2,1)S(1)}) custom-call(bf16[2,512,1280]{2,1,0:T(8,128)(2,1)S(1)} %bitcast.9, bf16[1280,256]{1,0:T(8,128)(2,1)S(1)} %get-tuple-element.55.source, bf16[1280,960]{1,0:T(8,128)(2,1)S(1)} %get-tuple-element.56.puts), custom_call_target="tpu_custom_call" | custom-call | flops 2516582400 | bytes 7045120 | tf_op jit(solution)/shard_map/pallas_call | solution.py:285
  25.1 1.3 %collective-permute-done.8.refs_3_ = bf16[192,256]{1,0:T(8,128)(2,1)S(1)} collective-permute-done((bf16[192,256]{1,0:T(8,128)(2,1)S(1)}, bf16[192,256]{1,0:T(8,128)(2,1)S(1)}, u32[]{:S(2)}, u32[]{:S(2)}) %collective-permute-start.8) | collective-permute-done | bytes 98336 | tf_op jit(solution)/shard_map/ppermute | solution.py:389
  26.4 0.9 %shard_map.59 = (f32[2,64,512]{2,1,0:T(8,128)S(1)}, f32[2,64,512]{2,1,0:T(8,128)S(1)}) custom-call(f32[512,256]{1,0:T(8,128)S(1)} %get-tuple-element.57.base, bf16[512,960]{1,0:T(8,128)(2,1)S(1)} %shard_map.56.placed, bf16[512,960]{1,0:T(8,128)(2,1)S(1)} %get-tuple-element.59.placed_imag, bf16[192,256]{1,0:T(8,128)(2,1)S(1)} %collective-permute-done.5.refs_0_, ...), custom_call_target="tpu_custom_call" | custom-call | tf_op jit(solution)/shard_map/pallas_call | solution.py:301
  27.4 1.4 %collective-permute-done.10 = f32[2,64,512]{2,1,0:T(8,128)S(1)} collective-permute-done((f32[2,64,512]{2,1,0:T(8,128)S(1)}, f32[2,64,512]{2,1,0:T(8,128)S(1)}, u32[]{:S(2)}, u32[]{:S(2)}) %collective-permute-start.10) | collective-permute-done | bytes 262176 | tf_op jit(solution)/shard_map/ppermute | solution.py:345
  28.9 1.1 %collective-permute-start.11 = (bf16[2,2,2,1,8,1,256]{6,4,0,5,3,2,1:T(8,128)(2,1)S(1)}, bf16[2,2,2,1,8,1,256]{6,4,0,5,3,2,1:T(8,128)(2,1)S(1)}, u32[]{:S(2)}, u32[]{:S(2)}) collective-permute-start(bf16[2,2,2,1,8,1,256]{6,4,0,5,3,2,1:T(8,128)(2,1)S(1)} %copy.24), channel_id=1, source_target_pairs={{0,7},{1,6},{2,5},{3,4},{4,3},{5,2},{6,1},{7,0},{8,15},{9,14},{10,... | collective-permute-start | bytes 98312 | tf_op jit(solution)/shard_map/ppermute | solution.py:367
  30.1 0.5 %collective-permute-start.12 = (bf16[2,2,2,1,8,1,256]{6,4,0,5,3,2,1:T(8,128)(2,1)S(1)}, bf16[2,2,2,1,8,1,256]{6,4,0,5,3,2,1:T(8,128)(2,1)S(1)}, u32[]{:S(2)}, u32[]{:S(2)}) collective-permute-start(bf16[2,2,2,1,8,1,256]{6,4,0,5,3,2,1:T(8,128)(2,1)S(1)} %copy.23), channel_id=1, source_target_pairs={{0,1},{1,0},{2,3},{3,2},{4,5},{5,4},{6,7},{7,6},{8,9},{9,8},{10,11... | collective-permute-start | bytes 98312 | tf_op jit(solution)/shard_map/ppermute | solution.py:367
  30.6 1.3 %collective-permute-start.13 = (bf16[2,2,2,1,8,1,256]{6,4,0,5,3,2,1:T(8,128)(2,1)S(1)}, bf16[2,2,2,1,8,1,256]{6,4,0,5,3,2,1:T(8,128)(2,1)S(1)}, u32[]{:S(2)}, u32[]{:S(2)}) collective-permute-start(bf16[2,2,2,1,8,1,256]{6,4,0,5,3,2,1:T(8,128)(2,1)S(1)} %copy.22), channel_id=1, source_target_pairs={{0,6},{1,7},{2,4},{3,5},{4,2},{5,3},{6,0},{7,1},{8,14},{9,15},{10,... | collective-permute-start | bytes 98312 | tf_op jit(solution)/shard_map/ppermute | solution.py:367
  31.9 1.3 %collective-permute-done.11 = bf16[2,2,2,1,8,1,256]{6,4,0,5,3,2,1:T(8,128)(2,1)S(1)} collective-permute-done((bf16[2,2,2,1,8,1,256]{6,4,0,5,3,2,1:T(8,128)(2,1)S(1)}, bf16[2,2,2,1,8,1,256]{6,4,0,5,3,2,1:T(8,128)(2,1)S(1)}, u32[]{:S(2)}, u32[]{:S(2)}) %collective-permute-start.11) | collective-permute-done | bytes 32800 | tf_op jit(solution)/shard_map/ppermute | solution.py:367
  33.3 0.7 %collective-permute-done.12 = bf16[2,2,2,1,8,1,256]{6,4,0,5,3,2,1:T(8,128)(2,1)S(1)} collective-permute-done((bf16[2,2,2,1,8,1,256]{6,4,0,5,3,2,1:T(8,128)(2,1)S(1)}, bf16[2,2,2,1,8,1,256]{6,4,0,5,3,2,1:T(8,128)(2,1)S(1)}, u32[]{:S(2)}, u32[]{:S(2)}) %collective-permute-start.12) | collective-permute-done | bytes 32800 | tf_op jit(solution)/shard_map/ppermute | solution.py:367
  34.1 1.7 %collective-permute-start.14 = (f32[2,1,1,1,8,1,256]{6,4,0,5,3,2,1:T(8,128)S(1)}, f32[2,1,1,1,8,1,256]{6,4,0,5,3,2,1:T(8,128)S(1)}, u32[]{:S(2)}, u32[]{:S(2)}) collective-permute-start(f32[2,1,1,1,8,1,256]{6,4,0,5,3,2,1:T(8,128)S(1)} %get-tuple-element.70), channel_id=1, source_target_pairs={{0,26},{1,27},{2,24},{3,25},{4,30},{5,31},{6,28},{7,29},{8,18},{9,... | collective-permute-start | bytes 49160 | tf_op jit(solution)/shard_map/ppermute | solution.py:367
  36.1 2.0 %collective-permute-start.16 = (f32[2,1,1,1,8,1,256]{6,4,0,5,3,2,1:T(8,128)S(1)}, f32[2,1,1,1,8,1,256]{6,4,0,5,3,2,1:T(8,128)S(1)}, u32[]{:S(2)}, u32[]{:S(2)}) collective-permute-start(f32[2,1,1,1,8,1,256]{6,4,0,5,3,2,1:T(8,128)S(1)} %get-tuple-element.71), channel_id=1, source_target_pairs={{0,18},{1,19},{2,16},{3,17},{4,22},{5,23},{6,20},{7,21},{8,26},{9,... | collective-permute-start | bytes 49160 | tf_op jit(solution)/shard_map/ppermute | solution.py:367
  38.0 1.1 %collective-permute-done.14 = f32[2,1,1,1,8,1,256]{6,4,0,5,3,2,1:T(8,128)S(1)} collective-permute-done((f32[2,1,1,1,8,1,256]{6,4,0,5,3,2,1:T(8,128)S(1)}, f32[2,1,1,1,8,1,256]{6,4,0,5,3,2,1:T(8,128)S(1)}, u32[]{:S(2)}, u32[]{:S(2)}) %collective-permute-start.14) | collective-permute-done | bytes 16416 | tf_op jit(solution)/shard_map/ppermute | solution.py:367
  39.6 0.5 %collective-permute-done.16 = f32[2,1,1,1,8,1,256]{6,4,0,5,3,2,1:T(8,128)S(1)} collective-permute-done((f32[2,1,1,1,8,1,256]{6,4,0,5,3,2,1:T(8,128)S(1)}, f32[2,1,1,1,8,1,256]{6,4,0,5,3,2,1:T(8,128)S(1)}, u32[]{:S(2)}, u32[]{:S(2)}) %collective-permute-start.16) | collective-permute-done | bytes 16416 | tf_op jit(solution)/shard_map/ppermute | solution.py:367
  40.1 0.6 %add_bitcast_fusion = f32[2,8,256]{2,1,0:T(8,128)} fusion(f32[2,1,1,1,8,1,256]{6,4,0,5,3,2,1:T(8,128)S(1)} %collective-permute-done.16, f32[2,1,1,1,8,1,256]{6,4,0,5,3,2,1:T(8,128)S(1)} %collective-permute-done.15, f32[2,1,1,1,8,1,256]{6,4,0,5,3,2,1:T(8,128)S(1)} %collective-permute-done.14, f32[2,2,2,1,8,1,256]{6,4,0,5,3,2,1:T(8,128)S(1)} %fusion.1, ...), kind=kLoop, calls=%fused_computation.6 | loop fusion | flops 12288 | bytes 81928 | tf_op jit(solution)/shard_map/reshape | solution.py:371
  (25 shorter events, 1.1 us)
Async XLA Ops:
  0.0 13.4 %copy-start = (bf16[1,1,1,2,512,1280]{5,4,3,2,1,0:T(8,128)(2,1)S(1)}, bf16[1,1,1,2,512,1280]{5,4,3,2,1,0:T(8,128)(2,1)}, u32[]{:S(2)}) copy-start(bf16[1,1,1,2,512,1280]{5,4,3,2,1,0:T(8,128)(2,1)} %param.7) | copy-start | bytes 7864324
  5.6 9.3 %collective-permute-start = (bf16[192,256]{1,0:T(8,128)(2,1)S(1)}, bf16[192,256]{1,0:T(8,128)(2,1)S(1)}, u32[]{:S(2)}, u32[]{:S(2)}) collective-permute-start(bf16[192,256]{1,0:T(8,128)(2,1)S(1)} %get-tuple-element.40), channel_id=1, source_target_pairs={{0,1},{1,0},{2,3},{3,2},{4,5},{5,4},{6,7},{7,6},{8,9},{9,8},{10,11... | collective-permute-start | bytes 294920 | tf_op jit(solution)/shard_map/ppermute | solution.py:389
  8.6 6.3 %collective-permute-start.1 = (bf16[192,256]{1,0:T(8,128)(2,1)S(1)}, bf16[192,256]{1,0:T(8,128)(2,1)S(1)}, u32[]{:S(2)}, u32[]{:S(2)}) collective-permute-start(bf16[192,256]{1,0:T(8,128)(2,1)S(1)} %get-tuple-element.41), channel_id=1, source_target_pairs={{0,8},{1,9},{2,10},{3,11},{4,12},{5,13},{6,14},{7,15},{8,0},{9,1},... | collective-permute-start | bytes 294920 | tf_op jit(solution)/shard_map/ppermute | solution.py:389
  10.2 4.7 %collective-permute-start.2 = (bf16[192,256]{1,0:T(8,128)(2,1)S(1)}, bf16[192,256]{1,0:T(8,128)(2,1)S(1)}, u32[]{:S(2)}, u32[]{:S(2)}) collective-permute-start(bf16[192,256]{1,0:T(8,128)(2,1)S(1)} %get-tuple-element.42), channel_id=1, source_target_pairs={{0,2},{1,3},{2,0},{3,1},{4,6},{5,7},{6,4},{7,5},{8,16},{9,17},{10,... | collective-permute-start | bytes 294920 | tf_op jit(solution)/shard_map/ppermute | solution.py:389
  10.2 5.7 %collective-permute-start.3 = (bf16[192,256]{1,0:T(8,128)(2,1)S(1)}, bf16[192,256]{1,0:T(8,128)(2,1)S(1)}, u32[]{:S(2)}, u32[]{:S(2)}) collective-permute-start(bf16[192,256]{1,0:T(8,128)(2,1)S(1)} %get-tuple-element.43), channel_id=1, source_target_pairs={{0,8},{1,9},{2,4},{3,5},{4,2},{5,3},{6,14},{7,15},{8,0},{9,1},{10,... | collective-permute-start | bytes 294920 | tf_op jit(solution)/shard_map/ppermute | solution.py:389
  13.4 2.6 %collective-permute-start.4 = (bf16[192,256]{1,0:T(8,128)(2,1)S(1)}, bf16[192,256]{1,0:T(8,128)(2,1)S(1)}, u32[]{:S(2)}, u32[]{:S(2)}) collective-permute-start(bf16[192,256]{1,0:T(8,128)(2,1)S(1)} %get-tuple-element.44), channel_id=1, source_target_pairs={{0,2},{1,3},{2,0},{3,1},{4,6},{5,7},{6,4},{7,5},{8,10},{9,11},{10,... | collective-permute-start | bytes 294920 | tf_op jit(solution)/shard_map/ppermute | solution.py:389
  19.1 5.9 %collective-permute-start.5 = (bf16[192,256]{1,0:T(8,128)(2,1)S(1)}, bf16[192,256]{1,0:T(8,128)(2,1)S(1)}, u32[]{:S(2)}, u32[]{:S(2)}) collective-permute-start(bf16[192,256]{1,0:T(8,128)(2,1)S(1)} %get-tuple-element.60), channel_id=1, source_target_pairs={{0,1},{1,0},{2,3},{3,2},{4,5},{5,4},{6,7},{7,6},{8,9},{9,8},{10,11... | collective-permute-start | bytes 294920 | tf_op jit(solution)/shard_map/ppermute | solution.py:389
  19.7 5.3 %collective-permute-start.6 = (bf16[192,256]{1,0:T(8,128)(2,1)S(1)}, bf16[192,256]{1,0:T(8,128)(2,1)S(1)}, u32[]{:S(2)}, u32[]{:S(2)}) collective-permute-start(bf16[192,256]{1,0:T(8,128)(2,1)S(1)} %get-tuple-element.61), channel_id=1, source_target_pairs={{0,8},{1,9},{2,10},{3,11},{4,12},{5,13},{6,14},{7,15},{8,0},{9,1},... | collective-permute-start | bytes 294920 | tf_op jit(solution)/shard_map/ppermute | solution.py:389
  21.8 3.3 %collective-permute-start.7 = (bf16[192,256]{1,0:T(8,128)(2,1)S(1)}, bf16[192,256]{1,0:T(8,128)(2,1)S(1)}, u32[]{:S(2)}, u32[]{:S(2)}) collective-permute-start(bf16[192,256]{1,0:T(8,128)(2,1)S(1)} %get-tuple-element.62), channel_id=1, source_target_pairs={{0,2},{1,3},{2,0},{3,1},{4,6},{5,7},{6,4},{7,5},{8,16},{9,17},{10,... | collective-permute-start | bytes 294920 | tf_op jit(solution)/shard_map/ppermute | solution.py:389
  21.8 4.6 %collective-permute-start.8 = (bf16[192,256]{1,0:T(8,128)(2,1)S(1)}, bf16[192,256]{1,0:T(8,128)(2,1)S(1)}, u32[]{:S(2)}, u32[]{:S(2)}) collective-permute-start(bf16[192,256]{1,0:T(8,128)(2,1)S(1)} %get-tuple-element.63), channel_id=1, source_target_pairs={{0,8},{1,9},{2,4},{3,5},{4,2},{5,3},{6,14},{7,15},{8,0},{9,1},{10,... | collective-permute-start | bytes 294920 | tf_op jit(solution)/shard_map/ppermute | solution.py:389
  22.8 3.6 %collective-permute-start.9 = (bf16[192,256]{1,0:T(8,128)(2,1)S(1)}, bf16[192,256]{1,0:T(8,128)(2,1)S(1)}, u32[]{:S(2)}, u32[]{:S(2)}) collective-permute-start(bf16[192,256]{1,0:T(8,128)(2,1)S(1)} %get-tuple-element.64), channel_id=1, source_target_pairs={{0,2},{1,3},{2,0},{3,1},{4,6},{5,7},{6,4},{7,5},{8,10},{9,11},{10,... | collective-permute-start | bytes 294920 | tf_op jit(solution)/shard_map/ppermute | solution.py:389
  27.3 1.6 %collective-permute-start.10 = (f32[2,64,512]{2,1,0:T(8,128)S(1)}, f32[2,64,512]{2,1,0:T(8,128)S(1)}, u32[]{:S(2)}, u32[]{:S(2)}) collective-permute-start(f32[2,64,512]{2,1,0:T(8,128)S(1)} %get-tuple-element.66), channel_id=1, source_target_pairs={{0,2},{1,3},{2,0},{3,1},{4,6},{5,7},{6,4},{7,5},{8,10},{9,11},{10,... | collective-permute-start | bytes 786440 | tf_op jit(solution)/shard_map/ppermute | solution.py:345
  28.9 4.3 %collective-permute-start.11 = (bf16[2,2,2,1,8,1,256]{6,4,0,5,3,2,1:T(8,128)(2,1)S(1)}, bf16[2,2,2,1,8,1,256]{6,4,0,5,3,2,1:T(8,128)(2,1)S(1)}, u32[]{:S(2)}, u32[]{:S(2)}) collective-permute-start(bf16[2,2,2,1,8,1,256]{6,4,0,5,3,2,1:T(8,128)(2,1)S(1)} %copy.24), channel_id=1, source_target_pairs={{0,7},{1,6},{2,5},{3,4},{4,3},{5,2},{6,1},{7,0},{8,15},{9,14},{10,... | collective-permute-start | bytes 98312 | tf_op jit(solution)/shard_map/ppermute | solution.py:367
  30.1 3.9 %collective-permute-start.12 = (bf16[2,2,2,1,8,1,256]{6,4,0,5,3,2,1:T(8,128)(2,1)S(1)}, bf16[2,2,2,1,8,1,256]{6,4,0,5,3,2,1:T(8,128)(2,1)S(1)}, u32[]{:S(2)}, u32[]{:S(2)}) collective-permute-start(bf16[2,2,2,1,8,1,256]{6,4,0,5,3,2,1:T(8,128)(2,1)S(1)} %copy.23), channel_id=1, source_target_pairs={{0,1},{1,0},{2,3},{3,2},{4,5},{5,4},{6,7},{7,6},{8,9},{9,8},{10,11... | collective-permute-start | bytes 98312 | tf_op jit(solution)/shard_map/ppermute | solution.py:367
  30.6 3.4 %collective-permute-start.13 = (bf16[2,2,2,1,8,1,256]{6,4,0,5,3,2,1:T(8,128)(2,1)S(1)}, bf16[2,2,2,1,8,1,256]{6,4,0,5,3,2,1:T(8,128)(2,1)S(1)}, u32[]{:S(2)}, u32[]{:S(2)}) collective-permute-start(bf16[2,2,2,1,8,1,256]{6,4,0,5,3,2,1:T(8,128)(2,1)S(1)} %copy.22), channel_id=1, source_target_pairs={{0,6},{1,7},{2,4},{3,5},{4,2},{5,3},{6,0},{7,1},{8,14},{9,15},{10,... | collective-permute-start | bytes 98312 | tf_op jit(solution)/shard_map/ppermute | solution.py:367
  34.1 5.0 %collective-permute-start.14 = (f32[2,1,1,1,8,1,256]{6,4,0,5,3,2,1:T(8,128)S(1)}, f32[2,1,1,1,8,1,256]{6,4,0,5,3,2,1:T(8,128)S(1)}, u32[]{:S(2)}, u32[]{:S(2)}) collective-permute-start(f32[2,1,1,1,8,1,256]{6,4,0,5,3,2,1:T(8,128)S(1)} %get-tuple-element.70), channel_id=1, source_target_pairs={{0,26},{1,27},{2,24},{3,25},{4,30},{5,31},{6,28},{7,29},{8,18},{9,... | collective-permute-start | bytes 49160 | tf_op jit(solution)/shard_map/ppermute | solution.py:367
  35.8 3.8 %collective-permute-start.15 = (f32[2,1,1,1,8,1,256]{6,4,0,5,3,2,1:T(8,128)S(1)}, f32[2,1,1,1,8,1,256]{6,4,0,5,3,2,1:T(8,128)S(1)}, u32[]{:S(2)}, u32[]{:S(2)}) collective-permute-start(f32[2,1,1,1,8,1,256]{6,4,0,5,3,2,1:T(8,128)S(1)} %get-tuple-element.72), channel_id=1, source_target_pairs={{0,8},{1,9},{2,10},{3,11},{4,12},{5,13},{6,14},{7,15},{8,0},{9,1},... | collective-permute-start | bytes 49160 | tf_op jit(solution)/shard_map/ppermute | solution.py:367
  36.1 4.1 %collective-permute-start.16 = (f32[2,1,1,1,8,1,256]{6,4,0,5,3,2,1:T(8,128)S(1)}, f32[2,1,1,1,8,1,256]{6,4,0,5,3,2,1:T(8,128)S(1)}, u32[]{:S(2)}, u32[]{:S(2)}) collective-permute-start(f32[2,1,1,1,8,1,256]{6,4,0,5,3,2,1:T(8,128)S(1)} %get-tuple-element.71), channel_id=1, source_target_pairs={{0,18},{1,19},{2,16},{3,17},{4,22},{5,23},{6,20},{7,21},{8,26},{9,... | collective-permute-start | bytes 49160 | tf_op jit(solution)/shard_map/ppermute | solution.py:367

commit v7 on v6

--- a/solution.py
+++ b/solution.py
@@ -11,8 +11,8 @@
 AXES = ("gx", "gy", "gz")
 F32 = jnp.float32
 BF16 = jnp.bfloat16
-CHUNKS = 8
-STAGES = (4, 6, 8)
+CHUNKS = 10
+STAGES = (6, 10)
 VMEM_LIMIT = 40 * 1024 * 1024
 OUT_VMEM = pltpu.VMEM
 

time: 40.9 us -> 40.7 us (level)
  no operation moved by 1% of the time
where the time goes in v7:
time: 40.7 us; the launch traced here: 40.6 us
  starting transfers between devices  18.5 us (45%)
  Pallas kernels  13.2 us (32%)
  waiting for transfers between devices  8 us (20%)
  other arithmetic  0.67 us (2%)
    ppermute x10, starting transfers between devices, shards(): lax.ppermute(face, AXES, swap_pairs(sizes, pos, phase))  11.4 us
    ppermute x6, starting transfers between devices, scatter_sum(): got.append(lax.ppermute(piece, AXES, mask_pairs(sizes, flips)))  6.92 us
    pallas_call x1, Pallas kernels, first_sweep(): pl.pallas_call(functools.partial(first_kernel, sizes, rounds), out_shape=...  5.45 us
    ppermute x6, waiting for transfers between devices, scatter_sum(): got.append(lax.ppermute(piece, AXES, mask_pairs(sizes, flips)))  4.2 us
    pallas_call x1, Pallas kernels, later_sweep(): pl.pallas_call(functools.partial(sweep_kernel, count), out_shape=[jax.Sha...  3.19 us
    ppermute x10, waiting for transfers between devices, shards(): lax.ppermute(face, AXES, swap_pairs(sizes, pos, phase))  2.38 us
    pallas_call x1, Pallas kernels, placed_imag_and_incident(): pl.pallas_call(incident_kernel, out_shape=[OUT_VMEM((angles, source.shape...  2.19 us
    pallas_call x1, Pallas kernels, placed_real(): pl.pallas_call(functools.partial(columns_kernel, 0), out_shape=OUT_VMEM(s...  1.52 us
  transfers between devices with their start and end apart: 17, of which 9 were waited for; matrix products, arithmetic and copies ran while one was open for 0% of the time, Pallas kernels for 9%

profile of v7, /device:TPU:0, one launch (start us, length us, event | category | flops | bytes accessed | tf_op | source)
XLA Modules:
  0.0 40.6 jit_solution(2389092411183765872)
XLA Ops:
  0.0 5.4 %shard_map.55 = (bf16[192,256]{1,0:T(8,128)(2,1)S(1)}, bf16[192,256]{1,0:T(8,128)(2,1)S(1)}, bf16[192,256]{1,0:T(8,128)(2,1)S(1)}, bf16[192,256]{1,0:T(8,128)(2,...) custom-call(s32[6]{0:T(128)} %bitcast.15, ...), custom_call_target="tpu_custom_call" | custom-call | tf_op jit(solution)/shard_map/pallas_call | solution.py:233
  5.5 3.0 %collective-permute-start = (bf16[192,256]{1,0:T(8,128)(2,1)S(1)}, bf16[192,256]{1,0:T(8,128)(2,1)S(1)}, u32[]{:S(2)}, u32[]{:S(2)}) collective-permute-start(bf16[192,256]{1,0:T(8,128)(2,1)S(1)} %get-tuple-element.40), channel_id=1, source_target_pairs={{0,1},{1,0},{2,3},{3,2},{4,5},{5,4},{6,7},{7,6},{8,9},{9,8},{10,11... | collective-permute-start | bytes 294920 | tf_op jit(solution)/shard_map/ppermute | solution.py:389
  8.5 1.6 %collective-permute-start.1 = (bf16[192,256]{1,0:T(8,128)(2,1)S(1)}, bf16[192,256]{1,0:T(8,128)(2,1)S(1)}, u32[]{:S(2)}, u32[]{:S(2)}) collective-permute-start(bf16[192,256]{1,0:T(8,128)(2,1)S(1)} %get-tuple-element.41), channel_id=1, source_target_pairs={{0,8},{1,9},{2,10},{3,11},{4,12},{5,13},{6,14},{7,15},{8,0},{9,1},... | collective-permute-start | bytes 294920 | tf_op jit(solution)/shard_map/ppermute | solution.py:389
  10.0 3.2 %collective-permute-start.3 = (bf16[192,256]{1,0:T(8,128)(2,1)S(1)}, bf16[192,256]{1,0:T(8,128)(2,1)S(1)}, u32[]{:S(2)}, u32[]{:S(2)}) collective-permute-start(bf16[192,256]{1,0:T(8,128)(2,1)S(1)} %get-tuple-element.43), channel_id=1, source_target_pairs={{0,8},{1,9},{2,4},{3,5},{4,2},{5,3},{6,14},{7,15},{8,0},{9,1},{10,... | collective-permute-start | bytes 294920 | tf_op jit(solution)/shard_map/ppermute | solution.py:389
  13.2 1.5 %shard_map.56.placed = bf16[512,960]{1,0:T(8,128)(2,1)S(1)} custom-call(bf16[2,512,1280]{2,1,0:T(8,128)(2,1)S(1)} %bitcast.8, bf16[1280,960]{1,0:T(8,128)(2,1)S(1)} %get-tuple-element.56.puts), custom_call_target="tpu_custom_call" | custom-call | flops 1258291200 | bytes 4751360 | tf_op jit(solution)/shard_map/pallas_call | solution.py:273
  14.8 1.0 %collective-permute-done.3.refs_3_ = bf16[192,256]{1,0:T(8,128)(2,1)S(1)} collective-permute-done((bf16[192,256]{1,0:T(8,128)(2,1)S(1)}, bf16[192,256]{1,0:T(8,128)(2,1)S(1)}, u32[]{:S(2)}, u32[]{:S(2)}) %collective-permute-start.3) | collective-permute-done | bytes 98336 | tf_op jit(solution)/shard_map/ppermute | solution.py:389
  15.8 3.2 %shard_map.57 = (bf16[192,256]{1,0:T(8,128)(2,1)S(1)}, bf16[192,256]{1,0:T(8,128)(2,1)S(1)}, bf16[192,256]{1,0:T(8,128)(2,1)S(1)}, bf16[192,256]{1,0:T(8,128)(2,1)S(1)}, bf16[192,256]{1,0:T(8,128)(2,1)S(1)}) custom-call(bf16[2,1280,1280]{2,1,0:T(8,128)(2,1)S(1)} %get-tuple-element.38.response, bf16[1280,256]{1,0:T(8,128)(2,1)S(1)} %get-tuple-element.55.source, ...), custom_call_target="tpu_custom_call" | custom-call | tf_op jit(solution)/shard_map/pallas_call | solution.py:255
  19.0 0.6 %collective-permute-start.5 = (bf16[192,256]{1,0:T(8,128)(2,1)S(1)}, bf16[192,256]{1,0:T(8,128)(2,1)S(1)}, u32[]{:S(2)}, u32[]{:S(2)}) collective-permute-start(bf16[192,256]{1,0:T(8,128)(2,1)S(1)} %get-tuple-element.60), channel_id=1, source_target_pairs={{0,1},{1,0},{2,3},{3,2},{4,5},{5,4},{6,7},{7,6},{8,9},{9,8},{10,11... | collective-permute-start | bytes 294920 | tf_op jit(solution)/shard_map/ppermute | solution.py:389
  19.6 2.0 %collective-permute-start.6 = (bf16[192,256]{1,0:T(8,128)(2,1)S(1)}, bf16[192,256]{1,0:T(8,128)(2,1)S(1)}, u32[]{:S(2)}, u32[]{:S(2)}) collective-permute-start(bf16[192,256]{1,0:T(8,128)(2,1)S(1)} %get-tuple-element.61), channel_id=1, source_target_pairs={{0,8},{1,9},{2,10},{3,11},{4,12},{5,13},{6,14},{7,15},{8,0},{9,1},... | collective-permute-start | bytes 294920 | tf_op jit(solution)/shard_map/ppermute | solution.py:389
  21.6 1.1 %collective-permute-start.8 = (bf16[192,256]{1,0:T(8,128)(2,1)S(1)}, bf16[192,256]{1,0:T(8,128)(2,1)S(1)}, u32[]{:S(2)}, u32[]{:S(2)}) collective-permute-start(bf16[192,256]{1,0:T(8,128)(2,1)S(1)} %get-tuple-element.63), channel_id=1, source_target_pairs={{0,8},{1,9},{2,4},{3,5},{4,2},{5,3},{6,14},{7,15},{8,0},{9,1},{10,... | collective-permute-start | bytes 294920 | tf_op jit(solution)/shard_map/ppermute | solution.py:389
  22.7 2.2 %shard_map.58 = (f32[512,256]{1,0:T(8,128)S(1)}, bf16[512,960]{1,0:T(8,128)(2,1)S(1)}) custom-call(bf16[2,512,1280]{2,1,0:T(8,128)(2,1)S(1)} %bitcast.9, bf16[1280,256]{1,0:T(8,128)(2,1)S(1)} %get-tuple-element.55.source, bf16[1280,960]{1,0:T(8,128)(2,1)S(1)} %get-tuple-element.56.puts), custom_call_target="tpu_custom_call" | custom-call | flops 2516582400 | bytes 7045120 | tf_op jit(solution)/shard_map/pallas_call | solution.py:285
  24.9 1.3 %collective-permute-done.8.refs_3_ = bf16[192,256]{1,0:T(8,128)(2,1)S(1)} collective-permute-done((bf16[192,256]{1,0:T(8,128)(2,1)S(1)}, bf16[192,256]{1,0:T(8,128)(2,1)S(1)}, u32[]{:S(2)}, u32[]{:S(2)}) %collective-permute-start.8) | collective-permute-done | bytes 98336 | tf_op jit(solution)/shard_map/ppermute | solution.py:389
  26.3 0.9 %shard_map.59 = (f32[2,64,512]{2,1,0:T(8,128)S(1)}, f32[2,64,512]{2,1,0:T(8,128)S(1)}) custom-call(f32[512,256]{1,0:T(8,128)S(1)} %get-tuple-element.57.base, bf16[512,960]{1,0:T(8,128)(2,1)S(1)} %shard_map.56.placed, bf16[512,960]{1,0:T(8,128)(2,1)S(1)} %get-tuple-element.59.placed_imag, bf16[192,256]{1,0:T(8,128)(2,1)S(1)} %collective-permute-done.5.refs_0_, ...), custom_call_target="tpu_custom_call" | custom-call | tf_op jit(solution)/shard_map/pallas_call | solution.py:301
  27.3 1.4 %collective-permute-done.10 = f32[2,64,512]{2,1,0:T(8,128)S(1)} collective-permute-done((f32[2,64,512]{2,1,0:T(8,128)S(1)}, f32[2,64,512]{2,1,0:T(8,128)S(1)}, u32[]{:S(2)}, u32[]{:S(2)}) %collective-permute-start.10) | collective-permute-done | bytes 262176 | tf_op jit(solution)/shard_map/ppermute | solution.py:345
  28.8 1.1 %collective-permute-start.11 = (bf16[2,2,2,1,8,1,256]{6,4,0,5,3,2,1:T(8,128)(2,1)S(1)}, bf16[2,2,2,1,8,1,256]{6,4,0,5,3,2,1:T(8,128)(2,1)S(1)}, u32[]{:S(2)}, u32[]{:S(2)}) collective-permute-start(bf16[2,2,2,1,8,1,256]{6,4,0,5,3,2,1:T(8,128)(2,1)S(1)} %copy.24), channel_id=1, source_target_pairs={{0,7},{1,6},{2,5},{3,4},{4,3},{5,2},{6,1},{7,0},{8,15},{9,14},{10,... | collective-permute-start | bytes 98312 | tf_op jit(solution)/shard_map/ppermute | solution.py:367
  29.9 0.6 %collective-permute-start.12 = (bf16[2,2,2,1,8,1,256]{6,4,0,5,3,2,1:T(8,128)(2,1)S(1)}, bf16[2,2,2,1,8,1,256]{6,4,0,5,3,2,1:T(8,128)(2,1)S(1)}, u32[]{:S(2)}, u32[]{:S(2)}) collective-permute-start(bf16[2,2,2,1,8,1,256]{6,4,0,5,3,2,1:T(8,128)(2,1)S(1)} %copy.23), channel_id=1, source_target_pairs={{0,1},{1,0},{2,3},{3,2},{4,5},{5,4},{6,7},{7,6},{8,9},{9,8},{10,11... | collective-permute-start | bytes 98312 | tf_op jit(solution)/shard_map/ppermute | solution.py:367
  30.5 1.3 %collective-permute-start.13 = (bf16[2,2,2,1,8,1,256]{6,4,0,5,3,2,1:T(8,128)(2,1)S(1)}, bf16[2,2,2,1,8,1,256]{6,4,0,5,3,2,1:T(8,128)(2,1)S(1)}, u32[]{:S(2)}, u32[]{:S(2)}) collective-permute-start(bf16[2,2,2,1,8,1,256]{6,4,0,5,3,2,1:T(8,128)(2,1)S(1)} %copy.22), channel_id=1, source_target_pairs={{0,6},{1,7},{2,4},{3,5},{4,2},{5,3},{6,0},{7,1},{8,14},{9,15},{10,... | collective-permute-start | bytes 98312 | tf_op jit(solution)/shard_map/ppermute | solution.py:367
  31.8 1.3 %collective-permute-done.11 = bf16[2,2,2,1,8,1,256]{6,4,0,5,3,2,1:T(8,128)(2,1)S(1)} collective-permute-done((bf16[2,2,2,1,8,1,256]{6,4,0,5,3,2,1:T(8,128)(2,1)S(1)}, bf16[2,2,2,1,8,1,256]{6,4,0,5,3,2,1:T(8,128)(2,1)S(1)}, u32[]{:S(2)}, u32[]{:S(2)}) %collective-permute-start.11) | collective-permute-done | bytes 32800 | tf_op jit(solution)/shard_map/ppermute | solution.py:367
  33.1 0.7 %collective-permute-done.12 = bf16[2,2,2,1,8,1,256]{6,4,0,5,3,2,1:T(8,128)(2,1)S(1)} collective-permute-done((bf16[2,2,2,1,8,1,256]{6,4,0,5,3,2,1:T(8,128)(2,1)S(1)}, bf16[2,2,2,1,8,1,256]{6,4,0,5,3,2,1:T(8,128)(2,1)S(1)}, u32[]{:S(2)}, u32[]{:S(2)}) %collective-permute-start.12) | collective-permute-done | bytes 32800 | tf_op jit(solution)/shard_map/ppermute | solution.py:367
  34.0 1.6 %collective-permute-start.14 = (f32[2,1,1,1,8,1,256]{6,4,0,5,3,2,1:T(8,128)S(1)}, f32[2,1,1,1,8,1,256]{6,4,0,5,3,2,1:T(8,128)S(1)}, u32[]{:S(2)}, u32[]{:S(2)}) collective-permute-start(f32[2,1,1,1,8,1,256]{6,4,0,5,3,2,1:T(8,128)S(1)} %get-tuple-element.70), channel_id=1, source_target_pairs={{0,26},{1,27},{2,24},{3,25},{4,30},{5,31},{6,28},{7,29},{8,18},{9,... | collective-permute-start | bytes 49160 | tf_op jit(solution)/shard_map/ppermute | solution.py:367
  35.9 2.0 %collective-permute-start.16 = (f32[2,1,1,1,8,1,256]{6,4,0,5,3,2,1:T(8,128)S(1)}, f32[2,1,1,1,8,1,256]{6,4,0,5,3,2,1:T(8,128)S(1)}, u32[]{:S(2)}, u32[]{:S(2)}) collective-permute-start(f32[2,1,1,1,8,1,256]{6,4,0,5,3,2,1:T(8,128)S(1)} %get-tuple-element.71), channel_id=1, source_target_pairs={{0,18},{1,19},{2,16},{3,17},{4,22},{5,23},{6,20},{7,21},{8,26},{9,... | collective-permute-start | bytes 49160 | tf_op jit(solution)/shard_map/ppermute | solution.py:367
  37.9 1.1 %collective-permute-done.14 = f32[2,1,1,1,8,1,256]{6,4,0,5,3,2,1:T(8,128)S(1)} collective-permute-done((f32[2,1,1,1,8,1,256]{6,4,0,5,3,2,1:T(8,128)S(1)}, f32[2,1,1,1,8,1,256]{6,4,0,5,3,2,1:T(8,128)S(1)}, u32[]{:S(2)}, u32[]{:S(2)}) %collective-permute-start.14) | collective-permute-done | bytes 16416 | tf_op jit(solution)/shard_map/ppermute | solution.py:367
  39.5 0.5 %collective-permute-done.16 = f32[2,1,1,1,8,1,256]{6,4,0,5,3,2,1:T(8,128)S(1)} collective-permute-done((f32[2,1,1,1,8,1,256]{6,4,0,5,3,2,1:T(8,128)S(1)}, f32[2,1,1,1,8,1,256]{6,4,0,5,3,2,1:T(8,128)S(1)}, u32[]{:S(2)}, u32[]{:S(2)}) %collective-permute-start.16) | collective-permute-done | bytes 16416 | tf_op jit(solution)/shard_map/ppermute | solution.py:367
  40.0 0.6 %add_bitcast_fusion = f32[2,8,256]{2,1,0:T(8,128)} fusion(f32[2,1,1,1,8,1,256]{6,4,0,5,3,2,1:T(8,128)S(1)} %collective-permute-done.16, f32[2,1,1,1,8,1,256]{6,4,0,5,3,2,1:T(8,128)S(1)} %collective-permute-done.15, f32[2,1,1,1,8,1,256]{6,4,0,5,3,2,1:T(8,128)S(1)} %collective-permute-done.14, f32[2,2,2,1,8,1,256]{6,4,0,5,3,2,1:T(8,128)S(1)} %fusion.1, ...), kind=kLoop, calls=%fused_computation.6 | loop fusion | flops 12288 | bytes 81928 | tf_op jit(solution)/shard_map/reshape | solution.py:371
  (25 shorter events, 1.2 us)
Async XLA Ops:
  0.0 13.2 %copy-start = (bf16[1,1,1,2,512,1280]{5,4,3,2,1,0:T(8,128)(2,1)S(1)}, bf16[1,1,1,2,512,1280]{5,4,3,2,1,0:T(8,128)(2,1)}, u32[]{:S(2)}) copy-start(bf16[1,1,1,2,512,1280]{5,4,3,2,1,0:T(8,128)(2,1)} %param.7) | copy-start | bytes 7864324
  5.5 9.3 %collective-permute-start = (bf16[192,256]{1,0:T(8,128)(2,1)S(1)}, bf16[192,256]{1,0:T(8,128)(2,1)S(1)}, u32[]{:S(2)}, u32[]{:S(2)}) collective-permute-start(bf16[192,256]{1,0:T(8,128)(2,1)S(1)} %get-tuple-element.40), channel_id=1, source_target_pairs={{0,1},{1,0},{2,3},{3,2},{4,5},{5,4},{6,7},{7,6},{8,9},{9,8},{10,11... | collective-permute-start | bytes 294920 | tf_op jit(solution)/shard_map/ppermute | solution.py:389
  8.5 6.3 %collective-permute-start.1 = (bf16[192,256]{1,0:T(8,128)(2,1)S(1)}, bf16[192,256]{1,0:T(8,128)(2,1)S(1)}, u32[]{:S(2)}, u32[]{:S(2)}) collective-permute-start(bf16[192,256]{1,0:T(8,128)(2,1)S(1)} %get-tuple-element.41), channel_id=1, source_target_pairs={{0,8},{1,9},{2,10},{3,11},{4,12},{5,13},{6,14},{7,15},{8,0},{9,1},... | collective-permute-start | bytes 294920 | tf_op jit(solution)/shard_map/ppermute | solution.py:389
  10.0 4.7 %collective-permute-start.2 = (bf16[192,256]{1,0:T(8,128)(2,1)S(1)}, bf16[192,256]{1,0:T(8,128)(2,1)S(1)}, u32[]{:S(2)}, u32[]{:S(2)}) collective-permute-start(bf16[192,256]{1,0:T(8,128)(2,1)S(1)} %get-tuple-element.42), channel_id=1, source_target_pairs={{0,2},{1,3},{2,0},{3,1},{4,6},{5,7},{6,4},{7,5},{8,16},{9,17},{10,... | collective-permute-start | bytes 294920 | tf_op jit(solution)/shard_map/ppermute | solution.py:389
  10.0 5.8 %collective-permute-start.3 = (bf16[192,256]{1,0:T(8,128)(2,1)S(1)}, bf16[192,256]{1,0:T(8,128)(2,1)S(1)}, u32[]{:S(2)}, u32[]{:S(2)}) collective-permute-start(bf16[192,256]{1,0:T(8,128)(2,1)S(1)} %get-tuple-element.43), channel_id=1, source_target_pairs={{0,8},{1,9},{2,4},{3,5},{4,2},{5,3},{6,14},{7,15},{8,0},{9,1},{10,... | collective-permute-start | bytes 294920 | tf_op jit(solution)/shard_map/ppermute | solution.py:389
  13.2 2.6 %collective-permute-start.4 = (bf16[192,256]{1,0:T(8,128)(2,1)S(1)}, bf16[192,256]{1,0:T(8,128)(2,1)S(1)}, u32[]{:S(2)}, u32[]{:S(2)}) collective-permute-start(bf16[192,256]{1,0:T(8,128)(2,1)S(1)} %get-tuple-element.44), channel_id=1, source_target_pairs={{0,2},{1,3},{2,0},{3,1},{4,6},{5,7},{6,4},{7,5},{8,10},{9,11},{10,... | collective-permute-start | bytes 294920 | tf_op jit(solution)/shard_map/ppermute | solution.py:389
  19.0 5.9 %collective-permute-start.5 = (bf16[192,256]{1,0:T(8,128)(2,1)S(1)}, bf16[192,256]{1,0:T(8,128)(2,1)S(1)}, u32[]{:S(2)}, u32[]{:S(2)}) collective-permute-start(bf16[192,256]{1,0:T(8,128)(2,1)S(1)} %get-tuple-element.60), channel_id=1, source_target_pairs={{0,1},{1,0},{2,3},{3,2},{4,5},{5,4},{6,7},{7,6},{8,9},{9,8},{10,11... | collective-permute-start | bytes 294920 | tf_op jit(solution)/shard_map/ppermute | solution.py:389
  19.6 5.3 %collective-permute-start.6 = (bf16[192,256]{1,0:T(8,128)(2,1)S(1)}, bf16[192,256]{1,0:T(8,128)(2,1)S(1)}, u32[]{:S(2)}, u32[]{:S(2)}) collective-permute-start(bf16[192,256]{1,0:T(8,128)(2,1)S(1)} %get-tuple-element.61), channel_id=1, source_target_pairs={{0,8},{1,9},{2,10},{3,11},{4,12},{5,13},{6,14},{7,15},{8,0},{9,1},... | collective-permute-start | bytes 294920 | tf_op jit(solution)/shard_map/ppermute | solution.py:389
  21.6 3.3 %collective-permute-start.7 = (bf16[192,256]{1,0:T(8,128)(2,1)S(1)}, bf16[192,256]{1,0:T(8,128)(2,1)S(1)}, u32[]{:S(2)}, u32[]{:S(2)}) collective-permute-start(bf16[192,256]{1,0:T(8,128)(2,1)S(1)} %get-tuple-element.62), channel_id=1, source_target_pairs={{0,2},{1,3},{2,0},{3,1},{4,6},{5,7},{6,4},{7,5},{8,16},{9,17},{10,... | collective-permute-start | bytes 294920 | tf_op jit(solution)/shard_map/ppermute | solution.py:389
  21.6 4.6 %collective-permute-start.8 = (bf16[192,256]{1,0:T(8,128)(2,1)S(1)}, bf16[192,256]{1,0:T(8,128)(2,1)S(1)}, u32[]{:S(2)}, u32[]{:S(2)}) collective-permute-start(bf16[192,256]{1,0:T(8,128)(2,1)S(1)} %get-tuple-element.63), channel_id=1, source_target_pairs={{0,8},{1,9},{2,4},{3,5},{4,2},{5,3},{6,14},{7,15},{8,0},{9,1},{10,... | collective-permute-start | bytes 294920 | tf_op jit(solution)/shard_map/ppermute | solution.py:389
  22.7 3.6 %collective-permute-start.9 = (bf16[192,256]{1,0:T(8,128)(2,1)S(1)}, bf16[192,256]{1,0:T(8,128)(2,1)S(1)}, u32[]{:S(2)}, u32[]{:S(2)}) collective-permute-start(bf16[192,256]{1,0:T(8,128)(2,1)S(1)} %get-tuple-element.64), channel_id=1, source_target_pairs={{0,2},{1,3},{2,0},{3,1},{4,6},{5,7},{6,4},{7,5},{8,10},{9,11},{10,... | collective-permute-start | bytes 294920 | tf_op jit(solution)/shard_map/ppermute | solution.py:389
  27.1 1.6 %collective-permute-start.10 = (f32[2,64,512]{2,1,0:T(8,128)S(1)}, f32[2,64,512]{2,1,0:T(8,128)S(1)}, u32[]{:S(2)}, u32[]{:S(2)}) collective-permute-start(f32[2,64,512]{2,1,0:T(8,128)S(1)} %get-tuple-element.66), channel_id=1, source_target_pairs={{0,2},{1,3},{2,0},{3,1},{4,6},{5,7},{6,4},{7,5},{8,10},{9,11},{10,... | collective-permute-start | bytes 786440 | tf_op jit(solution)/shard_map/ppermute | solution.py:345
  28.8 4.3 %collective-permute-start.11 = (bf16[2,2,2,1,8,1,256]{6,4,0,5,3,2,1:T(8,128)(2,1)S(1)}, bf16[2,2,2,1,8,1,256]{6,4,0,5,3,2,1:T(8,128)(2,1)S(1)}, u32[]{:S(2)}, u32[]{:S(2)}) collective-permute-start(bf16[2,2,2,1,8,1,256]{6,4,0,5,3,2,1:T(8,128)(2,1)S(1)} %copy.24), channel_id=1, source_target_pairs={{0,7},{1,6},{2,5},{3,4},{4,3},{5,2},{6,1},{7,0},{8,15},{9,14},{10,... | collective-permute-start | bytes 98312 | tf_op jit(solution)/shard_map/ppermute | solution.py:367
  29.9 3.9 %collective-permute-start.12 = (bf16[2,2,2,1,8,1,256]{6,4,0,5,3,2,1:T(8,128)(2,1)S(1)}, bf16[2,2,2,1,8,1,256]{6,4,0,5,3,2,1:T(8,128)(2,1)S(1)}, u32[]{:S(2)}, u32[]{:S(2)}) collective-permute-start(bf16[2,2,2,1,8,1,256]{6,4,0,5,3,2,1:T(8,128)(2,1)S(1)} %copy.23), channel_id=1, source_target_pairs={{0,1},{1,0},{2,3},{3,2},{4,5},{5,4},{6,7},{7,6},{8,9},{9,8},{10,11... | collective-permute-start | bytes 98312 | tf_op jit(solution)/shard_map/ppermute | solution.py:367
  30.5 3.5 %collective-permute-start.13 = (bf16[2,2,2,1,8,1,256]{6,4,0,5,3,2,1:T(8,128)(2,1)S(1)}, bf16[2,2,2,1,8,1,256]{6,4,0,5,3,2,1:T(8,128)(2,1)S(1)}, u32[]{:S(2)}, u32[]{:S(2)}) collective-permute-start(bf16[2,2,2,1,8,1,256]{6,4,0,5,3,2,1:T(8,128)(2,1)S(1)} %copy.22), channel_id=1, source_target_pairs={{0,6},{1,7},{2,4},{3,5},{4,2},{5,3},{6,0},{7,1},{8,14},{9,15},{10,... | collective-permute-start | bytes 98312 | tf_op jit(solution)/shard_map/ppermute | solution.py:367
  34.0 5.0 %collective-permute-start.14 = (f32[2,1,1,1,8,1,256]{6,4,0,5,3,2,1:T(8,128)S(1)}, f32[2,1,1,1,8,1,256]{6,4,0,5,3,2,1:T(8,128)S(1)}, u32[]{:S(2)}, u32[]{:S(2)}) collective-permute-start(f32[2,1,1,1,8,1,256]{6,4,0,5,3,2,1:T(8,128)S(1)} %get-tuple-element.70), channel_id=1, source_target_pairs={{0,26},{1,27},{2,24},{3,25},{4,30},{5,31},{6,28},{7,29},{8,18},{9,... | collective-permute-start | bytes 49160 | tf_op jit(solution)/shard_map/ppermute | solution.py:367
  35.6 3.9 %collective-permute-start.15 = (f32[2,1,1,1,8,1,256]{6,4,0,5,3,2,1:T(8,128)S(1)}, f32[2,1,1,1,8,1,256]{6,4,0,5,3,2,1:T(8,128)S(1)}, u32[]{:S(2)}, u32[]{:S(2)}) collective-permute-start(f32[2,1,1,1,8,1,256]{6,4,0,5,3,2,1:T(8,128)S(1)} %get-tuple-element.72), channel_id=1, source_target_pairs={{0,8},{1,9},{2,10},{3,11},{4,12},{5,13},{6,14},{7,15},{8,0},{9,1},... | collective-permute-start | bytes 49160 | tf_op jit(solution)/shard_map/ppermute | solution.py:367
  35.9 4.1 %collective-permute-start.16 = (f32[2,1,1,1,8,1,256]{6,4,0,5,3,2,1:T(8,128)S(1)}, f32[2,1,1,1,8,1,256]{6,4,0,5,3,2,1:T(8,128)S(1)}, u32[]{:S(2)}, u32[]{:S(2)}) collective-permute-start(f32[2,1,1,1,8,1,256]{6,4,0,5,3,2,1:T(8,128)S(1)} %get-tuple-element.71), channel_id=1, source_target_pairs={{0,18},{1,19},{2,16},{3,17},{4,22},{5,23},{6,20},{7,21},{8,26},{9,... | collective-permute-start | bytes 49160 | tf_op jit(solution)/shard_map/ppermute | solution.py:367
